TPU v7x, 32 devices: a whole 2x2x4 slice. The times are simulated.
32 devices in a mesh: dp: 8 (over z, x), seq: 4 (over y, core).
Axes of the slice: x: 2, y: 2, z: 4, core: 2. Of those that a mesh axis runs over, the one named last changes fastest.
Arguments:
- images: bfloat16 [32, 16, 16, 256], P('dp', 'seq'), may hold values from -6 to 6
- timesteps: int32 [32], P('dp'), may hold values from 0 to 999
- step_table: bfloat16 [1000, 512], replicated, may hold values from -6 to 6
- norm1_gain: float32 [256], replicated, may hold values from 0.1 to 1.9
- norm1_bias: float32 [256], replicated, may hold values from -3 to 3
- conv1_weight: bfloat16 [3, 3, 256, 256], replicated, may hold values from -0.125 to 0.125
- embed_weight: bfloat16 [512, 256], replicated, may hold values from -0.25 to 0.25
- embed_bias: float32 [256], replicated, may hold values from -3 to 3
- norm2_gain: float32 [256], replicated, may hold values from 0.1 to 1.9
- norm2_bias: float32 [256], replicated, may hold values from -3 to 3
- conv2_weight: bfloat16 [3, 3, 256, 256], replicated, may hold values from -0.125 to 0.125
- conv2_bias: float32 [256], replicated, may hold values from -3 to 3
- norm3_gain: float32 [256], replicated, may hold values from 0.1 to 1.9
- norm3_bias: float32 [256], replicated, may hold values from -3 to 3
- qkv_weight: bfloat16 [256, 768], replicated, may hold values from -0.5 to 0.5
- query_bias: float32 [256], replicated, may hold values from -3 to 3
- out_weight: bfloat16 [256, 256], replicated, may hold values from -1.5 to 1.5
- out_bias: float32 [256], replicated, may hold values from -3 to 3
- cotangent: bfloat16 [32, 16, 16, 256], P('dp', 'seq'), may hold values from -6 to 6
Outputs:
- output: bfloat16 [32, 16, 16, 256], P('dp', 'seq')
- grad_images: bfloat16 [32, 16, 16, 256], P('dp', 'seq')
- grad_step_table: float32 [1000, 512], replicated
- grad_norm1_gain: float32 [256], replicated
- grad_norm1_bias: float32 [256], replicated
- grad_conv1_weight: float32 [3, 3, 256, 256], replicated
- grad_embed_weight: float32 [512, 256], replicated
- grad_embed_bias: float32 [256], replicated
- grad_norm2_gain: float32 [256], replicated
- grad_norm2_bias: float32 [256], replicated
- grad_conv2_weight: float32 [3, 3, 256, 256], replicated
- grad_conv2_bias: float32 [256], replicated
- grad_norm3_gain: float32 [256], replicated
- grad_norm3_bias: float32 [256], replicated
- grad_qkv_weight: float32 [256, 768], replicated
- grad_query_bias: float32 [256], replicated
- grad_out_weight: float32 [256, 256], replicated
- grad_out_bias: float32 [256], replicated
All inputs are finite; a program needn't handle non-finite values.
Results may differ from a plain program's by a relative error of at most 0.019.
The roundings to bfloat16 on the way count: a program that leaves them out, or rounds other values in their place, can miss the bound.
Values may be sent and summed in bfloat16 or wider, within the bound.
No kernel may reach another device: no remote copies, remote signals or barrier semaphores. Data moves between devices by JAX's collectives and lax.ppermute only.
A program may use at most 64 MiB of HBM per device.

v0:
```python
import jax
import jax.numpy as jnp
from jax import lax
from jax.sharding import PartitionSpec as P

GROUPS = 32


norm_eps = 1e-05
highest_precision = lax.Precision.HIGHEST


def with_halo(array, sides, width):
    for axis, dim in sides:
        size, length = (lax.axis_size(axis), array.shape[dim])
        up = [(i, (i + 1) % size) for i in range(size - 1)]
        down = [(j, i) for i, j in up]
        last = lax.slice_in_dim(array, length - width, length, axis=dim)
        initial = lax.slice_in_dim(array, 0, width, axis=dim)
        before = lax.ppermute(last, axis, up)
        after = lax.ppermute(initial, axis, down)
        array = jnp.concatenate([before, array, after], axis=dim)
    return array


def silu_slope(argument):
    logistic = jax.nn.sigmoid(argument)
    return logistic * (1.0 + argument * (1.0 - logistic))


def widened_rows(field, backward):
    if backward:
        padded = with_halo(field, (("seq", 1),), 1)
    else:
        padded = with_halo(field, (("seq", 1),), 1)
    return jnp.pad(padded, ((0, 0), (0, 0), (1, 1), (0, 0)))


def patches(padded, row_count, col_count, flipped):
    pieces = []
    for row_step in range(3):
        for col_step in range(3):
            top_row = 2 - row_step if flipped else row_step
            left_col = 2 - col_step if flipped else col_step
            pieces.append(
                padded[:, top_row : top_row + row_count, left_col : left_col + col_count, :]
            )
    joined = jnp.concatenate(pieces, axis=-1)
    return joined.reshape(-1, joined.shape[-1])


def conv_forward(padded, kernel, row_count, col_count):
    channels = kernel.shape[-1]
    result = jnp.dot(
        patches(padded, row_count, col_count, False),
        kernel.reshape(-1, channels),
        preferred_element_type=jnp.float32,
    )
    return result.reshape(padded.shape[0], row_count, col_count, channels)


def conv_back(grad_branch, kernel):
    row_count = grad_branch.shape[1]
    col_count = grad_branch.shape[2]
    channels = grad_branch.shape[3]
    padded = widened_rows(grad_branch, True)
    turned = jnp.transpose(kernel, (0, 1, 3, 2)).reshape(-1, channels)
    result = jnp.dot(
        patches(padded, row_count, col_count, True), turned, preferred_element_type=jnp.float32
    )
    return result.reshape(grad_branch.shape)


def kernel_grad(padded, grad_branch):
    row_count = grad_branch.shape[1]
    col_count = grad_branch.shape[2]
    channels = grad_branch.shape[3]
    columns = patches(padded, row_count, col_count, False)
    result = lax.dot_general(
        columns,
        grad_branch.reshape(-1, channels),
        (((0,), (0,)), ((), ())),
        preferred_element_type=jnp.float32,
    )
    return result.reshape(3, 3, channels, channels)


def group_forward(field, norm_gain, norm_bias):
    grouped_shape = (
        field.shape[0],
        field.shape[1],
        field.shape[2],
        GROUPS,
        field.shape[3] // GROUPS,
    )
    grouped = field.reshape(grouped_shape)
    first_sums = jnp.sum(grouped, axis=(1, 2, 4))
    second_sums = jnp.sum(grouped * grouped, axis=(1, 2, 4))
    entries = field.shape[1] * field.shape[2] * (field.shape[3] // GROUPS)
    first_sums, second_sums = lax.psum((first_sums, second_sums), "seq")
    entries = entries * lax.axis_size("seq")
    group_mean = first_sums / entries
    inverse = lax.rsqrt(second_sums / entries - group_mean * group_mean + norm_eps)
    scaled = (grouped - group_mean[:, None, None, :, None]) * inverse[:, None, None, :, None]
    scaled = scaled.reshape(field.shape)
    return (scaled * norm_gain + norm_bias, scaled, inverse)


def group_backward(grad_out, scaled, inverse, norm_gain):
    grouped_shape = (
        grad_out.shape[0],
        grad_out.shape[1],
        grad_out.shape[2],
        GROUPS,
        grad_out.shape[3] // GROUPS,
    )
    scaled_grad = (grad_out * norm_gain).reshape(grouped_shape)
    hat_grouped = scaled.reshape(grouped_shape)
    first_sums = jnp.sum(scaled_grad, axis=(1, 2, 4))
    second_sums = jnp.sum(scaled_grad * hat_grouped, axis=(1, 2, 4))
    entries = grad_out.shape[1] * grad_out.shape[2] * (grad_out.shape[3] // GROUPS)
    first_sums, second_sums = lax.psum((first_sums, second_sums), "seq")
    entries = entries * lax.axis_size("seq")
    result = inverse[:, None, None, :, None] * (
        scaled_grad
        - first_sums[:, None, None, :, None] / entries
        - hat_grouped * second_sums[:, None, None, :, None] / entries
    )
    gain_grad = jnp.sum(grad_out * scaled, axis=(0, 1, 2))
    bias_grad = jnp.sum(grad_out, axis=(0, 1, 2))
    return (result.reshape(grad_out.shape), gain_grad, bias_grad)


def shards(
    images,
    timesteps,
    step_table,
    norm1_gain,
    norm1_bias,
    conv1_weight,
    embed_weight,
    embed_bias,
    norm2_gain,
    norm2_bias,
    conv2_weight,
    conv2_bias,
    norm3_gain,
    norm3_bias,
    qkv_weight,
    query_bias,
    out_weight,
    out_bias,
    cotangent,
):
    map_count, row_count, col_count, channels = images.shape
    pixels = row_count * col_count
    step_count = step_table.shape[0]
    onehot = (timesteps[:, None] == jnp.arange(step_count, dtype=jnp.int32)[None, :]).astype(
        jnp.float32
    )
    embedded = jnp.dot(onehot, step_table.astype(jnp.float32), precision=highest_precision)
    lifted = jax.nn.silu(embedded)
    embed_float = embed_weight.astype(jnp.float32)
    projected = jnp.dot(lifted, embed_float, precision=highest_precision) + embed_bias
    source = images.astype(jnp.float32)
    pre1, hat1, inverse1 = group_forward(source, norm1_gain, norm1_bias)
    act1 = jax.nn.silu(pre1).astype(jnp.bfloat16)
    padded1 = widened_rows(act1, False)
    hidden1 = (
        conv_forward(padded1, conv1_weight, row_count, col_count) + projected[:, None, None, :]
    )
    pre2, hat2, inverse2 = group_forward(hidden1, norm2_gain, norm2_bias)
    act2 = jax.nn.silu(pre2).astype(jnp.bfloat16)
    padded2 = widened_rows(act2, False)
    hidden2 = source + conv_forward(padded2, conv2_weight, row_count, col_count) + conv2_bias
    pre3, hat3, inverse3 = group_forward(hidden2, norm3_gain, norm3_bias)
    normed3 = pre3.astype(jnp.bfloat16).reshape(map_count * pixels, channels)
    bias_row = jnp.concatenate([query_bias, jnp.zeros((2 * channels,), jnp.float32)])
    projections = (
        jnp.dot(normed3, qkv_weight, preferred_element_type=jnp.float32) + bias_row
    ).astype(jnp.bfloat16)
    projections = projections.reshape(map_count, pixels, 3 * channels)
    query_rows = projections[..., :channels]
    own_keys = projections[..., channels : 2 * channels]
    own_values = projections[..., 2 * channels :]
    gathered_keys, gathered_values = (
        lax.all_gather(own_keys, "seq", axis=1, tiled=True),
        lax.all_gather(own_values, "seq", axis=1, tiled=True),
    )
    score_scale = channels ** (-0.5)
    attention_scores = (
        jnp.einsum("ume,upe->ump", query_rows, gathered_keys, preferred_element_type=jnp.float32)
        * score_scale
    )
    row_peak = jnp.max(attention_scores, axis=-1, keepdims=True)
    log_total = row_peak + jnp.log(
        jnp.sum(jnp.exp(attention_scores - row_peak), axis=-1, keepdims=True)
    )
    probabilities_low_precision = jnp.exp(attention_scores - log_total).astype(jnp.bfloat16)
    attended_values = jnp.einsum(
        "whn,wnx->whx",
        probabilities_low_precision,
        gathered_values,
        preferred_element_type=jnp.float32,
    ).astype(jnp.bfloat16)
    mixed_flat = attended_values.reshape(map_count * pixels, channels)
    attended = jnp.dot(mixed_flat, out_weight, preferred_element_type=jnp.float32) + out_bias
    output = (hidden2 + attended.reshape(images.shape)).astype(jnp.bfloat16)
    cot_flat = cotangent.reshape(map_count * pixels, channels)
    grad_out_weight = lax.dot_general(
        mixed_flat, cot_flat, (((0,), (0,)), ((), ())), preferred_element_type=jnp.float32
    )
    grad_out_bias = jnp.sum(cot_flat.astype(jnp.float32), axis=0)
    mixed_gradient = lax.dot_general(
        cot_flat, out_weight, (((1,), (1,)), ((), ())), preferred_element_type=jnp.float32
    )
    mixed_gradient = mixed_gradient.astype(jnp.bfloat16).reshape(map_count, pixels, channels)
    again = (
        jnp.einsum("ume,upe->ump", query_rows, gathered_keys, preferred_element_type=jnp.float32)
        * score_scale
    )
    attention_probabilities = jnp.exp(again - log_total)
    recomputed_probabilities = attention_probabilities.astype(jnp.bfloat16)
    probability_gradient = jnp.einsum(
        "ume,upe->ump", mixed_gradient, gathered_values, preferred_element_type=jnp.float32
    )
    grad_values = jnp.einsum(
        "ntf,ntl->nfl", recomputed_probabilities, mixed_gradient, preferred_element_type=jnp.float32
    )
    inner_sum = jnp.sum(attention_probabilities * probability_gradient, axis=-1, keepdims=True)
    score_gradient = (attention_probabilities * (probability_gradient - inner_sum)).astype(
        jnp.bfloat16
    )
    d_queries = (
        jnp.einsum(
            "whn,wnx->whx", score_gradient, gathered_keys, preferred_element_type=jnp.float32
        )
        * score_scale
    ).astype(jnp.bfloat16)
    grad_keys = (
        jnp.einsum("ntf,ntl->nfl", score_gradient, query_rows, preferred_element_type=jnp.float32)
        * score_scale
    )
    grad_keys, grad_values = (
        lax.psum_scatter(
            grad_keys.astype(jnp.bfloat16), "seq", scatter_dimension=1, tiled=True
        ).astype(jnp.float32),
        lax.psum_scatter(
            grad_values.astype(jnp.bfloat16), "seq", scatter_dimension=1, tiled=True
        ).astype(jnp.float32),
    )
    d_projections = jnp.concatenate(
        [d_queries, grad_keys.astype(jnp.bfloat16), grad_values.astype(jnp.bfloat16)], axis=-1
    )
    d_projections = d_projections.reshape(map_count * pixels, 3 * channels)
    grad_qkv_weight = lax.dot_general(
        normed3, d_projections, (((0,), (0,)), ((), ())), preferred_element_type=jnp.float32
    )
    grad_query_bias = jnp.sum(d_queries.astype(jnp.float32), axis=(0, 1))
    d_normed3 = lax.dot_general(
        d_projections, qkv_weight, (((1,), (1,)), ((), ())), preferred_element_type=jnp.float32
    )
    d_source3, grad_norm3_gain, grad_norm3_bias = group_backward(
        d_normed3.reshape(images.shape), hat3, inverse3, norm3_gain
    )
    d_hidden2 = cotangent.astype(jnp.float32) + d_source3
    grad_conv2_bias = jnp.sum(d_hidden2, axis=(0, 1, 2))
    d_branch2 = d_hidden2.astype(jnp.bfloat16)
    grad_conv2_weight = kernel_grad(padded2, d_branch2)
    d_act2 = conv_back(d_branch2, conv2_weight)
    d_hidden1, grad_norm2_gain, grad_norm2_bias = group_backward(
        d_act2 * silu_slope(pre2), hat2, inverse2, norm2_gain
    )
    d_projected = jnp.sum(d_hidden1, axis=(1, 2))
    grad_embed_bias = jnp.sum(d_projected, axis=0)
    grad_embed_weight = lax.dot_general(
        lifted, d_projected, (((0,), (0,)), ((), ())), precision=highest_precision
    )
    d_embedded = lax.dot_general(
        d_projected, embed_float, (((1,), (1,)), ((), ())), precision=highest_precision
    ) * silu_slope(embedded)
    grad_step_table = lax.dot_general(
        onehot, d_embedded, (((0,), (0,)), ((), ())), precision=highest_precision
    )
    d_branch1 = d_hidden1.astype(jnp.bfloat16)
    grad_conv1_weight = kernel_grad(padded1, d_branch1)
    d_act1 = conv_back(d_branch1, conv1_weight)
    d_source1, grad_norm1_gain, grad_norm1_bias = group_backward(
        d_act1 * silu_slope(pre1), hat1, inverse1, norm1_gain
    )
    grad_images = (d_hidden2 + d_source1).astype(jnp.bfloat16)
    summed = lax.psum(
        (
            grad_step_table,
            grad_norm1_gain,
            grad_norm1_bias,
            grad_conv1_weight,
            grad_embed_weight,
            grad_embed_bias,
            grad_norm2_gain,
            grad_norm2_bias,
            grad_conv2_weight,
            grad_conv2_bias,
            grad_norm3_gain,
            grad_norm3_bias,
            grad_qkv_weight,
            grad_query_bias,
            grad_out_weight,
            grad_out_bias,
        ),
        ("dp", "seq"),
    )
    return (
        output,
        grad_images,
        summed[0],
        summed[1],
        summed[2],
        summed[3],
        summed[4],
        summed[5],
        summed[6],
        summed[7],
        summed[8],
        summed[9],
        summed[10],
        summed[11],
        summed[12],
        summed[13],
        summed[14],
        summed[15],
    )


def solution(mesh):
    placed = (
        P("dp", "seq", None, None),
        P("dp"),
        P(),
        P(),
        P(),
        P(),
        P(),
        P(),
        P(),
        P(),
        P(),
        P(),
        P(),
        P(),
        P(),
        P(),
        P(),
        P(),
        P("dp", "seq", None, None),
    )
    return jax.shard_map(
        shards,
        mesh=mesh,
        in_specs=placed,
        out_specs=(
            P("dp", "seq", None, None),
            P("dp", "seq", None, None),
            P(),
            P(),
            P(),
            P(),
            P(),
            P(),
            P(),
            P(),
            P(),
            P(),
            P(),
            P(),
            P(),
            P(),
            P(),
            P(),
        ),
        check_vma=False,
    )
```

profile of v0, /device:TPU:0, one launch (start us, length us, event | category | flops | bytes accessed | tf_op | source)
XLA Modules:
  0.0 363.2 jit_solution(10802159510393724635)
XLA Ops:
  7.3 1.0 convert_reduce_fusion
  8.7 8.4 %all-reduce.12 = (f32[4,32]{1,0:T(4,128)S(1)}, f32[4,32]{1,0:T(4,128)S(1)}) all-reduce(f32[4,32]{1,0:T(4,128)S(1)} %reduce_sum.259, f32[4,32]{1,0:T(4,128)S(1)} %reduce_sum.256), channel_id=1, replica_groups=mesh['dp'=8,'seq'=4] {'seq'}, use_global_device_ids=true, to_apply=%region_5.6 | all-reduce | flops 256 | bytes 2048 | tf_op jit(solution)/shard_map/psum | solution.py:100
  17.5 1.0 fusion.24
  18.5 1.3 collective-permute-start
  19.8 1.3 collective-permute-start.1
  21.1 0.9 fusion.49
  22.3 1.2 collective-permute-done.1
  24.0 0.9 copy-done.19
  25.8 8.3 %all-reduce.11 = (f32[4,32]{1,0:T(4,128)S(1)}, f32[4,32]{1,0:T(4,128)S(1)}) all-reduce(f32[4,32]{1,0:T(4,128)S(1)} %reduce_sum.320, f32[4,32]{1,0:T(4,128)S(1)} %reduce_sum.265), channel_id=1, replica_groups=mesh['dp'=8,'seq'=4] {'seq'}, use_global_device_ids=true, to_apply=%region_11.12 | all-reduce | flops 256 | bytes 2048 | tf_op jit(solution)/shard_map/psum | solution.py:100
  34.7 1.4 collective-permute-start.2
  36.0 1.3 collective-permute-start.3
  37.6 3.3 collective-permute-done.3
  41.4 0.9 copy-done.18
  43.3 8.3 %all-reduce.10 = (f32[4,32]{1,0:T(4,128)S(1)}, f32[4,32]{1,0:T(4,128)S(1)}) all-reduce(f32[4,32]{1,0:T(4,128)S(1)} %reduce_sum.326, f32[4,32]{1,0:T(4,128)S(1)} %reduce_sum.323), channel_id=1, replica_groups=mesh['dp'=8,'seq'=4] {'seq'}, use_global_device_ids=true, to_apply=%region_17.18 | all-reduce | flops 256 | bytes 2048 | tf_op jit(solution)/shard_map/psum | solution.py:100
  52.6 7.3 %all_gather.6 = bf16[4,256,256]{2,1,0:T(8,128)(2,1)S(1)} all-gather(bf16[4,64,256]{2,1,0:T(8,128)(2,1)S(1)} %get-tuple-element.69), channel_id=1, replica_groups=mesh['dp'=8,'seq'=4] {'seq'}, dimensions={1}, use_global_device_ids=true | all-gather | bytes 655360 | tf_op jit(solution)/shard_map/all_gather | solution.py:187
  60.5 7.3 %all_gather.7 = bf16[4,256,256]{2,1,0:T(8,128)(2,1)S(1)} all-gather(bf16[4,64,256]{2,1,0:T(8,128)(2,1)S(1)} %get-tuple-element.70), channel_id=1, replica_groups=mesh['dp'=8,'seq'=4] {'seq'}, dimensions={1}, use_global_device_ids=true | all-gather | bytes 655360 | tf_op jit(solution)/shard_map/all_gather | solution.py:188
  69.4 1.1 fusion
  70.6 1.3 convolution_convert_fusion
  72.0 2.4 copy.39
  75.0 1.6 copy.42
  76.6 1.4 convolution_convert_fusion.1
  78.0 1.9 fusion.69
  79.9 0.9 convolution_add_fusion.1
  80.8 1.4 convert_reduce_fusion.2
  82.2 10.8 %reduce-scatter.3.cloned.1.call-done = bf16[4,64,256]{2,1,0:T(8,128)(2,1)} async-done(((bf16[4,256,256]{2,1,0:T(8,128)(2,1)}), bf16[4,64,256]{2,1,0:T(8,128)(2,1)}) %reduce-scatter.3.cloned.1.call-update) | async-done | bytes 131088 | tf_op jit(solution)/shard_map/reduce_scatter | solution.py:245
  93.1 24.9 %reduce-scatter.5.cloned.1.call-done = bf16[4,64,256]{2,1,0:T(8,128)(2,1)} async-done(((bf16[4,256,256]{2,1,0:T(8,128)(2,1)}), bf16[4,64,256]{2,1,0:T(8,128)(2,1)}) %reduce-scatter.5.cloned.1.call-update) | async-done | bytes 131088 | tf_op jit(solution)/shard_map/reduce_scatter | solution.py:248
  118.0 1.1 pad_maximum_fusion
  119.1 0.7 copy-done.12
  119.8 2.7 multiply_reduce_fusion
  122.5 0.7 reduce_sum.333
  123.2 0.9 reduce_sum.334
  124.2 1.4 reduce_sum.330
  125.6 0.9 reduce_sum.331
  126.5 6.3 %all-reduce.9 = (f32[4,32]{1,0:T(4,128)}, f32[4,32]{1,0:T(4,128)}) all-reduce(f32[4,32]{1,0:T(4,128)S(1)} %reduce_sum.334, f32[4,32]{1,0:T(4,128)S(1)} %reduce_sum.331), channel_id=1, replica_groups=mesh['dp'=8,'seq'=4] {'seq'}, use_global_device_ids=true, to_apply=%region_28.29 | all-reduce | flops 256 | bytes 2048 | tf_op jit(solution)/shard_map/psum | solution.py:122
  132.8 0.7 broadcast_multiply_fusion.2
  133.5 0.7 sub.163
  134.2 0.9 sub.164
  135.2 1.4 mul.281
  136.6 0.9 mul.282
  137.5 2.5 fusion.59
  140.1 1.7 collective-permute-start.4
  141.8 1.3 collective-permute-start.5
  143.1 1.9 fusion.67
  145.0 1.2 fusion.68
  148.9 8.5 %all-reduce.8 = (f32[4,32]{1,0:T(4,128)S(1)}, f32[4,32]{1,0:T(4,128)S(1)}) all-reduce(f32[4,32]{1,0:T(4,128)S(1)} %reduce_sum.340, f32[4,32]{1,0:T(4,128)S(1)} %reduce_sum.337), channel_id=1, replica_groups=mesh['dp'=8,'seq'=4] {'seq'}, use_global_device_ids=true, to_apply=%region_34.35 | all-reduce | flops 256 | bytes 2048 | tf_op jit(solution)/shard_map/psum | solution.py:122
  158.2 1.5 fusion.53
  159.6 2.4 fusion.48
  162.0 1.9 fusion.66
  163.9 1.7 collective-permute-start.6
  165.6 1.3 collective-permute-start.7
  166.9 1.6 copy.40
  168.5 1.8 collective-permute-done.7
  170.8 1.3 copy-done.22
  173.1 9.5 %all-reduce.7 = (f32[4,32]{1,0:T(4,128)S(1)}, f32[4,32]{1,0:T(4,128)S(1)}) all-reduce(f32[4,32]{1,0:T(4,128)S(1)} %reduce_sum.346, f32[4,32]{1,0:T(4,128)S(1)} %reduce_sum.343), channel_id=1, replica_groups=mesh['dp'=8,'seq'=4] {'seq'}, use_global_device_ids=true, to_apply=%region_40.41 | all-reduce | flops 256 | bytes 2048 | tf_op jit(solution)/shard_map/psum | solution.py:122
  183.0 41.8 %all-reduce.5 = (f32[256]{0:T(256)}, f32[256]{0:T(256)}, f32[256]{0:T(256)}, f32[256]{0:T(256)}, f32[256]{0:T(256)}, /*index=5*/f32[256]{0:T(256)}, f32[256]{0:T(256)}, f32[256]{0:T(256)}, f32[256]{0:T(256)}, f32[256]{0:T(256)}) all-reduce(f32[256]{0:T(256)S(1)} %get-tuple-element.22, ...), channel_id=1, replica_groups=mesh['dp'=8,'seq'=4] {'dp','seq'}, use_global_device_ids=true, to_apply=%region_44.45 | all-reduce | flops 2560 | bytes 20480 | tf_op jit(solution)/shard_map/psum | solution.py:292
  224.9 0.8 fusion.32
  225.6 121.4 %all-reduce.15.cloned.1.call-done = (f32[1000,512]{1,0:T(8,128)}, f32[3,3,256,256]{3,2,1,0:T(8,128)}, f32[512,256]{1,0:T(8,128)}, f32[3,3,256,256]{3,2,1,0:T(8,1...) async-done(((f32[1000,512]{1,0:T(8,128)}, f32[3,3,256,256]{3,2,1,0:T(8,128)}, f32[512,256]{1,0:T(8,128)}, f32[3,3,256,256]{3,2,1,0:T(8,128)}, f32[256,768]{1,0:T(8,128)}, ...) | async-done | bytes 8339472 | tf_op jit(solution)/shard_map/psum | solution.py:292
  347.1 3.2 copy.88
  350.3 1.4 copy.89
  351.7 0.8 copy.90
  352.5 0.7 copy-done.7
  353.2 1.4 copy.91
  354.8 0.9 copy.92
  355.9 0.7 copy.93
  (223 shorter events, 13.9 us)
Async XLA Ops:
  7.2 13.9 %copy-start = (bf16[1000,512]{1,0:T(8,128)(2,1)S(1)}, bf16[1000,512]{1,0:T(8,128)(2,1)}, u32[]{:S(2)}) copy-start(bf16[1000,512]{1,0:T(8,128)(2,1)} %param.21) | copy-start | bytes 3072004
  7.2 14.8 %copy-start.25 = (bf16[512,256]{1,0:T(8,128)(2,1)S(1)}, bf16[512,256]{1,0:T(8,128)(2,1)}, u32[]{:S(2)}) copy-start(bf16[512,256]{1,0:T(8,128)(2,1)} %param.25) | copy-start | bytes 786436
  7.2 14.8 %copy-start.47 = (f32[256]{0:T(256)S(1)}, f32[256]{0:T(256)}, u32[]{:S(2)}) copy-start(f32[256]{0:T(256)} %param.26) | copy-start | bytes 3076
  7.2 85.8 %reduce-scatter.3.cloned.1.call-start = ((), (), s32[]{:S(2)}) async-start(), calls=%async_computation.2 | async-start | bytes 655360 | tf_op jit(solution)/shard_map/reduce_scatter | solution.py:245
  18.5 3.8 %collective-permute-start = (bf16[4,1,16,256]{3,2,1,0:T(8,128)(2,1)S(1)}, bf16[4,1,16,256]{3,2,1,0:T(8,128)(2,1)S(1)}, u32[]{:S(2)}, u32[]{:S(2)}) collective-permute-start(bf16[4,1,16,256]{3,2,1,0:T(8,128)(2,1)S(1)} %get-tuple-element.79), channel_id=1, source_target_pairs={{0,1},{1,2},{2,3},{4,5},{5,6},{6,7},{8,9},{9,10},{10,11},{12,13},{... | collective-permute-start | bytes 98312 | tf_op jit(solution)/shard_map/ppermute | solution.py:20
  19.8 3.7 %collective-permute-start.1 = (bf16[4,1,16,256]{3,2,1,0:T(8,128)(2,1)S(1)}, bf16[4,1,16,256]{3,2,1,0:T(8,128)(2,1)S(1)}, u32[]{:S(2)}, u32[]{:S(2)}) collective-permute-start(bf16[4,1,16,256]{3,2,1,0:T(8,128)(2,1)S(1)} %get-tuple-element.80), channel_id=1, source_target_pairs={{1,0},{2,1},{3,2},{5,4},{6,5},{7,6},{9,8},{10,9},{11,10},{13,12},{... | collective-permute-start | bytes 98312 | tf_op jit(solution)/shard_map/ppermute | solution.py:21
  22.1 1.7 copy-start.11
  22.1 1.7 copy-start.36
  22.1 1.7 copy-start.41
  23.6 1.3 copy-start.19
  24.9 9.6 %copy-start.34 = (f32[256]{0:T(256)S(1)}, f32[256]{0:T(256)}, u32[]{:S(2)}) copy-start(f32[256]{0:T(256)} %param.27) | copy-start | bytes 3076
  24.9 9.6 %copy-start.39 = (f32[256]{0:T(256)S(1)}, f32[256]{0:T(256)}, u32[]{:S(2)}) copy-start(f32[256]{0:T(256)} %param.28) | copy-start | bytes 3076
  25.4 15.8 %copy-start.9 = (f32[4,4,16,256]{3,2,1,0:T(8,128)}, f32[4,4,16,256]{3,2,1,0:T(8,128)S(1)}, u32[]{:S(2)}) copy-start(f32[4,4,16,256]{3,2,1,0:T(8,128)S(1)} %get-tuple-element.87) | copy-start | bytes 786436
  25.4 11.9 %copy-start.17 = (bf16[4,4,16,256]{3,2,1,0:T(8,128)(2,1)S(1)}, bf16[4,4,16,256]{3,2,1,0:T(8,128)(2,1)}, u32[]{:S(2)}) copy-start(bf16[4,4,16,256]{3,2,1,0:T(8,128)(2,1)} %param.37) | copy-start | bytes 393220
  25.4 11.9 %copy-start.30 = (bf16[256,256]{1,0:T(8,128)(2,1)S(1)}, bf16[256,256]{1,0:T(8,128)(2,1)}, u32[]{:S(2)}) copy-start(bf16[256,256]{1,0:T(8,128)(2,1)} %param.35) | copy-start | bytes 393220
  25.4 12.1 %copy-start.52 = (f32[256]{0:T(256)S(1)}, f32[256]{0:T(256)}, u32[]{:S(2)}) copy-start(f32[256]{0:T(256)} %param.34) | copy-start | bytes 3076
  34.7 2.9 collective-permute-start.2
  36.0 4.9 %collective-permute-start.3 = (bf16[4,1,16,256]{3,2,1,0:T(8,128)(2,1)S(1)}, bf16[4,1,16,256]{3,2,1,0:T(8,128)(2,1)S(1)}, u32[]{:S(2)}, u32[]{:S(2)}) collective-permute-start(bf16[4,1,16,256]{3,2,1,0:T(8,128)(2,1)S(1)} %get-tuple-element.78), channel_id=1, source_target_pairs={{1,0},{2,1},{3,2},{5,4},{6,5},{7,6},{9,8},{10,9},{11,10},{13,12},{... | collective-permute-start | bytes 98312 | tf_op jit(solution)/shard_map/ppermute | solution.py:21
  41.1 1.3 copy-start.18
  41.1 1.3 copy-start.53
  41.4 1.4 copy-start.14
  42.3 9.6 %copy-start.38 = (f32[256]{0:T(256)S(1)}, f32[256]{0:T(256)}, u32[]{:S(2)}) copy-start(f32[256]{0:T(256)} %param.31) | copy-start | bytes 3076
  42.3 9.6 %copy-start.48 = (f32[256]{0:T(256)S(1)}, f32[256]{0:T(256)}, u32[]{:S(2)}) copy-start(f32[256]{0:T(256)} %param.32) | copy-start | bytes 3076
  42.3 9.7 %copy-start.32 = (bf16[256,768]{1,0:T(8,128)(2,1)S(1)}, bf16[256,768]{1,0:T(8,128)(2,1)}, u32[]{:S(2)}) copy-start(bf16[256,768]{1,0:T(8,128)(2,1)} %param.33) | copy-start | bytes 1179652
  42.9 9.5 %copy-start.27 = (f32[4,4,16,256]{3,2,1,0:T(8,128)}, f32[4,4,16,256]{3,2,1,0:T(8,128)S(1)}, u32[]{:S(2)}) copy-start(f32[4,4,16,256]{3,2,1,0:T(8,128)S(1)} %get-tuple-element.88) | copy-start | bytes 786436
  59.9 8.2 %copy-start.2 = (bf16[4,256,256]{2,1,0:T(8,128)(2,1)}, bf16[4,256,256]{2,1,0:T(8,128)(2,1)S(1)}, u32[]{:S(2)}) copy-start(bf16[4,256,256]{2,1,0:T(8,128)(2,1)S(1)} %all_gather.6) | copy-start | bytes 1572868
  60.3 10.3 %copy-start.1 = (f32[4,64,256]{2,1,0:T(8,128)}, f32[4,64,256]{2,1,0:T(8,128)S(1)}, u32[]{:S(2)}) copy-start(f32[4,64,256]{2,1,0:T(8,128)S(1)} %get-tuple-element.90) | copy-start | bytes 786436
  67.8 0.8 copy-start.4
  68.7 0.7 copy-start.23
  70.6 47.4 %reduce-scatter.5.cloned.1.call-start = ((), (), s32[]{:S(2)}) async-start(), calls=%async_computation.3 | async-start | bytes 655360 | tf_op jit(solution)/shard_map/reduce_scatter | solution.py:248
  71.9 275.1 %all-reduce.15.cloned.1.call-start = ((), (), s32[]{:S(2)}) async-start(), calls=%async_computation.4 | async-start | bytes 16678912 | tf_op jit(solution)/shard_map/psum | solution.py:292
  76.6 3.4 copy-start.31
  76.6 3.3 copy-start.49
  76.6 4.2 %copy-start.3 = (bf16[4,256,256]{2,1,0:T(8,128)(2,1)S(1)}, bf16[4,256,256]{2,1,0:T(8,128)(2,1)}, u32[]{:S(2)}) copy-start(bf16[4,256,256]{2,1,0:T(8,128)(2,1)} %copy-done.2) | copy-start | bytes 1572868
  76.6 4.2 %copy-start.24 = (bf16[4,64,256]{2,1,0:T(8,128)(2,1)S(1)}, bf16[4,64,256]{2,1,0:T(8,128)(2,1)}, u32[]{:S(2)}) copy-start(bf16[4,64,256]{2,1,0:T(8,128)(2,1)} %copy-done.23) | copy-start | bytes 393220
  119.0 0.7 copy-start.12
  140.0 6.7 %copy-start.5 = (f32[4,4,16,256]{3,2,1,0:T(8,128)}, f32[4,4,16,256]{3,2,1,0:T(8,128)S(1)}, u32[]{:S(2)}) copy-start(f32[4,4,16,256]{3,2,1,0:T(8,128)S(1)} %get-tuple-element.67) | copy-start | bytes 786436
  140.1 6.1 %collective-permute-start.4 = (bf16[4,1,16,256]{3,2,1,0:T(8,128)(2,1)S(1)}, bf16[4,1,16,256]{3,2,1,0:T(8,128)(2,1)S(1)}, u32[]{:S(2)}, u32[]{:S(2)}) collective-permute-start(bf16[4,1,16,256]{3,2,1,0:T(8,128)(2,1)S(1)} %get-tuple-element.75), channel_id=1, source_target_pairs={{0,1},{1,2},{2,3},{4,5},{5,6},{6,7},{8,9},{9,10},{10,11},{12,13},{... | collective-permute-start | bytes 98312 | tf_op jit(solution)/shard_map/ppermute | solution.py:20
  141.8 4.6 %collective-permute-start.5 = (bf16[4,1,16,256]{3,2,1,0:T(8,128)(2,1)S(1)}, bf16[4,1,16,256]{3,2,1,0:T(8,128)(2,1)S(1)}, u32[]{:S(2)}, u32[]{:S(2)}) collective-permute-start(bf16[4,1,16,256]{3,2,1,0:T(8,128)(2,1)S(1)} %get-tuple-element.76), channel_id=1, source_target_pairs={{1,0},{2,1},{3,2},{5,4},{6,5},{7,6},{9,8},{10,9},{11,10},{13,12},{... | collective-permute-start | bytes 98312 | tf_op jit(solution)/shard_map/ppermute | solution.py:21
  143.1 1.9 copy-start.13
  143.1 1.9 copy-start.16
  146.6 1.0 copy-start.10
  146.6 1.4 copy-start.21
  146.6 1.3 copy-start.35
  146.6 1.3 copy-start.40
  148.5 9.4 %copy-start.26 = (bf16[512,256]{1,0:T(8,128)(2,1)S(1)}, bf16[512,256]{1,0:T(8,128)(2,1)}, u32[]{:S(2)}) copy-start(bf16[512,256]{1,0:T(8,128)(2,1)} %param.25) | copy-start | bytes 786436
  148.5 11.1 %copy-start.46 = (s32[4]{0:T(128)S(1)}, s32[4]{0:T(128)}, u32[]{:S(2)}) copy-start(s32[4]{0:T(128)} %param.20) | copy-start | bytes 52
  163.9 3.0 copy-start.20
  163.9 4.6 %collective-permute-start.6 = (bf16[4,1,16,256]{3,2,1,0:T(8,128)(2,1)S(1)}, bf16[4,1,16,256]{3,2,1,0:T(8,128)(2,1)S(1)}, u32[]{:S(2)}, u32[]{:S(2)}) collective-permute-start(bf16[4,1,16,256]{3,2,1,0:T(8,128)(2,1)S(1)} %get-tuple-element.73), channel_id=1, source_target_pairs={{0,1},{1,2},{2,3},{4,5},{5,6},{6,7},{8,9},{9,10},{10,11},{12,13},{... | collective-permute-start | bytes 98312 | tf_op jit(solution)/shard_map/ppermute | solution.py:20
  165.6 4.7 %collective-permute-start.7 = (bf16[4,1,16,256]{3,2,1,0:T(8,128)(2,1)S(1)}, bf16[4,1,16,256]{3,2,1,0:T(8,128)(2,1)S(1)}, u32[]{:S(2)}, u32[]{:S(2)}) collective-permute-start(bf16[4,1,16,256]{3,2,1,0:T(8,128)(2,1)S(1)} %get-tuple-element.74), channel_id=1, source_target_pairs={{1,0},{2,1},{3,2},{5,4},{6,5},{7,6},{9,8},{10,9},{11,10},{13,12},{... | collective-permute-start | bytes 98312 | tf_op jit(solution)/shard_map/ppermute | solution.py:21
  170.5 1.6 copy-start.22
  170.5 1.6 copy-start.37
  170.5 1.6 copy-start.42
  172.1 10.9 %copy-start.43 = (f32[256]{0:T(256)S(1)}, f32[256]{0:T(256)}, u32[]{:S(2)}) copy-start(f32[256]{0:T(256)} %get-tuple-element.96) | copy-start | bytes 3076
  172.1 10.9 %copy-start.44 = (f32[256]{0:T(256)S(1)}, f32[256]{0:T(256)}, u32[]{:S(2)}) copy-start(f32[256]{0:T(256)} %get-tuple-element.66) | copy-start | bytes 3076
  172.1 10.9 %copy-start.45 = (f32[256]{0:T(256)S(1)}, f32[256]{0:T(256)}, u32[]{:S(2)}) copy-start(f32[256]{0:T(256)} %get-tuple-element.72) | copy-start | bytes 3076
  172.1 10.9 %copy-start.50 = (f32[256]{0:T(256)S(1)}, f32[256]{0:T(256)}, u32[]{:S(2)}) copy-start(f32[256]{0:T(256)} %get-tuple-element.18) | copy-start | bytes 3076
  172.1 10.9 %copy-start.51 = (f32[256]{0:T(256)S(1)}, f32[256]{0:T(256)}, u32[]{:S(2)}) copy-start(f32[256]{0:T(256)} %get-tuple-element.27) | copy-start | bytes 3076
  172.1 52.8 %copy-start.6 = (f32[4,4,16,256]{3,2,1,0:T(8,128)S(1)}, f32[4,4,16,256]{3,2,1,0:T(8,128)}, u32[]{:S(2)}) copy-start(f32[4,4,16,256]{3,2,1,0:T(8,128)} %copy-done.5) | copy-start | bytes 786436
  347.1 3.2 copy-start.8
  350.3 1.4 copy-start.29
  350.3 2.9 copy-start.7
  353.1 1.7 copy-start.28
  354.8 1.1 copy-start.33
  (1 other events, 0.6 us)
Sparse Core Ops, SparseCore 0:
  70.7 22.3 reduce-scatter.2
  96.3 21.6 reduce-scatter.4
  164.0 182.9 all-reduce.14
where the time goes:
time: 364 us; the launch traced here: 363 us
  waiting for transfers between devices  164 us (45%)
  blocking collectives  106 us (29%)
  local copies, waits for them, and re-layouts  31.8 us (9%)
  matrix products  24.2 us (7%)
  between operations  15 us (4%)
  starting transfers between devices  11.4 us (3%)
  other arithmetic  11.3 us (3%)
    psum x1, waiting for transfers between devices, shards(): lax.psum((grad_step_table, grad_norm1_gain, grad_norm1_bias, grad_conv1_w...  121 us
    psum x1, blocking collectives, shards(): lax.psum((grad_step_table, grad_norm1_gain, grad_norm1_bias, grad_conv1_w...  41.8 us
    psum x3, blocking collectives, group_forward(): first_sums, second_sums = lax.psum((first_sums, second_sums), 'seq')  24.9 us
    reduce_scatter x1, waiting for transfers between devices, shards(): lax.psum_scatter(grad_values.astype(jnp.bfloat16), 'seq', scatter_dimensi...  24.9 us
    psum x3, blocking collectives, group_backward(): first_sums, second_sums = lax.psum((first_sums, second_sums), 'seq')  24.3 us
    unnamed x137, local copies, waits for them, and re-layouts  20.6 us
    reduce_scatter x1, waiting for transfers between devices, shards(): lax.psum_scatter(grad_keys.astype(jnp.bfloat16), 'seq', scatter_dimension...  10.8 us
    all_gather x1, blocking collectives, shards(): lax.all_gather(own_values, 'seq', axis=1, tiled=True)  7.3 us
  transfers between devices with their start and end apart: 11, of which 7 were waited for; matrix products, arithmetic and copies ran while one was open for 5% of the time, Pallas kernels for 0%

commit v1 on v0

v1 whole, which is shorter than its diff:
```python
import functools

import jax
import jax.numpy as jnp
from jax import lax
from jax.experimental import pallas as pl
from jax.experimental.pallas import tpu as pltpu
from jax.sharding import PartitionSpec as P

GROUPS = 32
EPS = 1e-5
F32 = jnp.float32
BF16 = jnp.bfloat16
HIGHEST = lax.Precision.HIGHEST
EARLY_COST = 20 * 10**9
LONG_COST = 40 * 10**9
SUM_COST = 10**9
SMALL_COST = 10**9
UNPACK_COST = 3 * 10**8
AXES = ("dp", "seq")
VMEM = pl.BlockSpec(memory_space=pltpu.VMEM)
SMEM = pl.BlockSpec(memory_space=pltpu.SMEM)
HBM = pl.BlockSpec(memory_space=pltpu.HBM)
ANY = pl.BlockSpec(memory_space=pl.ANY)
N1_GAIN, N1_BIAS, N2_GAIN, N2_BIAS, C2_BIAS, N3_GAIN, N3_BIAS, Q_BIAS, O_BIAS, PROJECTED = range(10)
N3G, N3B, QB, OB, C2B, N2G, N2B, EB = range(8)
HIGH, LOW = 7, 8
VEC_ROWS = 16
EARLY_TAPS = 5
DIGIT = 32


def mm(a, b):
    return lax.dot_general(a, b, (((1,), (0,)), ((), ())), preferred_element_type=F32)


def mt(a, b):
    return lax.dot_general(a, b, (((1,), (1,)), ((), ())), preferred_element_type=F32)


def tm(a, b):
    return lax.dot_general(a, b, (((0,), (0,)), ((), ())), preferred_element_type=F32)


def three(v):
    hi = v.astype(BF16).astype(F32)
    mid = (v - hi).astype(BF16).astype(F32)
    return hi, mid, (v - hi) - mid


def rows_of(pieces, count, width):
    at = lax.broadcasted_iota(jnp.int32, (count, width), 0)
    out = jnp.zeros((count, width), F32)
    for i, piece in enumerate(pieces):
        out = jnp.where(at == i, piece, out)
    return out


def exact_rows(rows, matrix):
    pieces = [p for row in rows for p in three(row)]
    out = mm(rows_of(pieces, 16, rows[0].shape[1]).astype(BF16), matrix)
    return [out[3 * i : 3 * i + 1] + out[3 * i + 1 : 3 * i + 2] + out[3 * i + 2 : 3 * i + 3] for i in range(len(rows))]


def spread_matrix(c):
    per = c // GROUPS
    a = lax.broadcasted_iota(jnp.int32, (c, c), 0) // per
    b = lax.broadcasted_iota(jnp.int32, (c, c), 1) // per
    return jnp.where(a == b, 1.0, 0.0).astype(BF16)


def col_sum(v):
    return jnp.sum(v, axis=0, keepdims=True)


def norm_stats(v, spread, count):
    m, s = exact_rows([col_sum(v), col_sum(v * v)], spread)
    m = m / count
    s = s / count
    return m, lax.rsqrt(s - m * m + EPS)


def norm_back(d, hat, inv, gain, spread, count):
    bias_sum = col_sum(d)
    gain_sum = col_sum(d * hat)
    m1, m2 = exact_rows([bias_sum * gain, gain_sum * gain], spread)
    return inv * (d * gain - m1 / count - hat * (m2 / count)), gain_sum, bias_sum


def silu(v):
    return v / (1.0 + jnp.exp(-v))


def silu_slope(v):
    s = 1.0 / (1.0 + jnp.exp(-v))
    return s * (1.0 + v * (1.0 - s))


def put_shifted(ref, v, w):
    px, c = v.shape
    col = lax.broadcasted_iota(jnp.int32, (px, c), 0) % w
    edge = jnp.zeros((w, 3 * c), BF16)
    ref[0:w, :] = edge
    ref[w + px : 2 * w + px, :] = edge
    ref[w : w + px, 0:c] = jnp.where(col == 0, 0.0, pltpu.roll(v, 1, 0)).astype(BF16)
    ref[w : w + px, c : 2 * c] = v.astype(BF16)
    ref[w : w + px, 2 * c : 3 * c] = jnp.where(col == w - 1, 0.0, pltpu.roll(v, px - 1, 0)).astype(BF16)


def conv(ref, weight_ref, px, w):
    k = ref.shape[1]
    return sum(mm(ref[a * w : a * w + px, :], weight_ref[a * k : (a + 1) * k, :]) for a in range(3))


def device():
    return lax.axis_index("dp") * lax.axis_size("seq") + lax.axis_index("seq")


def digit(step):
    low, radix = step
    index = device()
    if low(0) == low(1):
        return (index >> low(0)) & (radix - 1)
    return jnp.where(index & 1 == 0, index >> low(0), index >> low(1)) & (radix - 1)


def put_halves(keep_ref, send_ref, at, v):
    n, c = v.shape
    half = c // 2
    lo = v[:, :half].astype(BF16)
    hi = v[:, half:].astype(BF16)
    first = device() & 1 == 0
    keep_ref[at : at + n, :] = jnp.where(first, lo, hi)
    send_ref[at : at + n, :] = jnp.where(first, hi, lo)


def padded(n, unit):
    return -(-n // unit) * unit


def sums_rows(total):
    return 2 * (VEC_ROWS + total)


def own_rows(total):
    return padded(32, 2 * total)


def put_both(keep_ref, send_ref, at, v):
    n, c = v.shape
    half = c // 2
    for i in range(2):
        part = v[:, i * half : (i + 1) * half].astype(BF16)
        keep_ref[at + i * n : at + (i + 1) * n, :] = part
        send_ref[at + i * n : at + (i + 1) * n, :] = part


def tap_grad(act_t, ref, tap, px, w):
    c = act_t.shape[0]
    a, b = tap // 3, tap % 3
    return mm(act_t, ref[(2 - a) * w : (2 - a) * w + px, (2 - b) * c : (3 - b) * c])


def at_rows(place, size):
    return pl.ds(pl.multiple_of(place * size, 16), size)


def pack_kernel(first_hbm, second_hbm, *refs):
    outs, sems = refs[:-1], refs[-1]
    copies = []
    for o, out in enumerate(outs):
        to = lax.axis_index("seq") ^ o
        for i, source in enumerate((first_hbm, second_hbm)):
            copies.append(pltpu.make_async_copy(source.at[to], out.at[i], sems.at[2 * o + i]))
    for copy in copies:
        copy.start()
    for copy in copies:
        copy.wait()


def unpack_kernel(*refs):
    parts, (first_ref, second_ref, token_ref) = refs[:-4], refs[-3:]
    token_ref[...] = jnp.zeros_like(token_ref)
    for o, part in enumerate(parts):
        at = lax.axis_index("seq") ^ o
        first_ref[at] = part[0]
        second_ref[at] = part[1]


def setup_kernel(steps_ref, table_ref, embed_ref, conv1_ref, conv2_ref, qkv_ref, out_ref, *refs):
    vec_refs = refs[:10]
    vec_ref, turned1_ref, turned2_ref, qkv_turned_ref, out_turned_ref = refs[10:]
    c = out_ref.shape[0]
    steps = table_ref.shape[0]
    step = steps_ref[lax.axis_index("seq")]
    pick = jnp.where(lax.broadcasted_iota(jnp.int32, (16, steps), 1) == step, 1.0, 0.0).astype(BF16)
    lifted = silu(mm(pick, table_ref[...])[0:1, :])
    (projected,) = exact_rows([lifted], embed_ref[...])
    rows = [r[...] for r in vec_refs]
    rows[PROJECTED] = rows[PROJECTED] + projected
    vec_ref[...] = rows_of(rows, 16, c)
    for source, turned in ((conv1_ref, turned1_ref), (conv2_ref, turned2_ref)):
        for tap in range(9):
            turned[(8 - tap) * c : (9 - tap) * c, :] = source[tap * c : (tap + 1) * c, :].T
    for i in range(3):
        qkv_turned_ref[i * c : (i + 1) * c, :] = qkv_ref[:, i * c : (i + 1) * c].T
    out_turned_ref[...] = out_ref[...].T


def main_kernel(w, vec_ref, conv1_ref, conv2_ref, qkv_ref, out_ref, qkv_turned_ref, out_turned_ref, *refs):
    parts, refs = refs[:-12], refs[-12:]
    (
        keep_ref, send_ref, small_ref, output_ref, image_ref, act1_ref, hat2_ref, dh2_ref, q2_ref, stat_ref,
        cot_ref, p_ref,
    ) = refs
    px, c = act1_ref.shape
    count = float(px * (c // GROUPS))
    scale = c ** (-0.5)
    spread = spread_matrix(c)
    vec = lambda i: vec_ref[i : i + 1, :]
    for o, part in enumerate(parts):
        rows = at_rows(lax.axis_index("seq") ^ o, part.shape[1])
        image_ref[rows, :] = part[0]
        cot_ref[rows, :] = part[1]

    source = image_ref[...].astype(F32)
    m1, inv1 = norm_stats(source, spread, count)
    act1 = silu((source - m1) * inv1 * vec(N1_GAIN) + vec(N1_BIAS))
    act1_ref[...] = act1.astype(BF16)
    put_shifted(p_ref, act1, w)
    hidden1 = conv(p_ref, conv1_ref, px, w) + vec(PROJECTED)
    m2, inv2 = norm_stats(hidden1, spread, count)
    hat2 = (hidden1 - m2) * inv2
    hat2_ref[...] = hat2
    stat_ref[...] = rows_of([m1, inv1, inv2], 8, c)
    act2 = silu(hat2 * vec(N2_GAIN) + vec(N2_BIAS))
    put_shifted(p_ref, act2, w)
    hidden2 = image_ref[...].astype(F32) + conv(p_ref, conv2_ref, px, w) + vec(C2_BIAS)
    act2_t = p_ref[w : w + px, c : 2 * c].T

    m3, inv3 = norm_stats(hidden2, spread, count)
    hat3 = (hidden2 - m3) * inv3
    normed3 = (hat3 * vec(N3_GAIN) + vec(N3_BIAS)).astype(BF16)
    qkv = mm(normed3, qkv_ref[...])
    q = (qkv[:, :c] + vec(Q_BIAS)).astype(BF16)
    k = qkv[:, c : 2 * c].astype(BF16)
    v = qkv[:, 2 * c :].astype(BF16)
    scores = mt(q, k) * scale
    e = jnp.exp(scores - jnp.max(scores, axis=1, keepdims=True))
    probs = e / jnp.sum(e, axis=1, keepdims=True)
    low = probs.astype(BF16)
    mixed = mm(low, v).astype(BF16)
    output_ref[...] = (hidden2 + mm(mixed, out_ref[...]) + vec(O_BIAS)).astype(BF16)

    cot = cot_ref[...]
    put_halves(keep_ref, send_ref, 12 * c, tm(mixed, cot))
    cot_wide = cot.astype(F32)
    d_mixed = mm(cot, out_turned_ref[...]).astype(BF16)
    d_probs = mt(d_mixed, v)
    inner = jnp.sum(probs * d_probs, axis=1, keepdims=True)
    d_scores = (probs * (d_probs - inner)).astype(BF16)
    d_q = (mm(d_scores, k) * scale).astype(BF16)
    d_k = (tm(d_scores, q) * scale).astype(BF16)
    d_v = tm(low, d_mixed).astype(BF16)
    normed3_t = normed3.T
    for i, d in enumerate((d_q, d_k, d_v)):
        put_halves(keep_ref, send_ref, (9 + i) * c, mm(normed3_t, d))
    d_normed3 = mm(jnp.concatenate([d_q, d_k, d_v], axis=1), qkv_turned_ref[...])
    d_src3, g_n3g, g_n3b = norm_back(d_normed3, hat3, inv3, vec(N3_GAIN), spread, count)
    d_hidden2 = cot_wide + d_src3
    dh2_ref[...] = d_hidden2
    put_shifted(q2_ref, d_hidden2, w)
    for tap in range(9):
        put_halves(keep_ref, send_ref, tap * c, tap_grad(act2_t, q2_ref, tap, px, w))
    sums = [g_n3g, g_n3b, col_sum(d_q.astype(F32)), col_sum(cot_wide), col_sum(d_hidden2)]
    small_ref[...] = rows_of(sums, 8, c)


def back_kernel(
    w, total, steps_ref, vec_ref, turned2_ref, act1_ref, hat2_ref, q2_ref, stat_ref, small_ref, keep_ref, send_ref, q1_ref,
):
    px, c = act1_ref.shape
    count = float(px * (c // GROUPS))
    spread = spread_matrix(c)
    vec = lambda i: vec_ref[i : i + 1, :]
    hat2 = hat2_ref[...]
    d = conv(q2_ref, turned2_ref, px, w) * silu_slope(hat2 * vec(N2_GAIN) + vec(N2_BIAS))
    d_hidden1, g_n2g, g_n2b = norm_back(d, hat2, stat_ref[2:3, :], vec(N2_GAIN), spread, count)
    put_shifted(q1_ref, d_hidden1, w)
    act1_t = act1_ref[...].T
    for tap in range(9):
        put_halves(keep_ref, send_ref, tap * c, tap_grad(act1_t, q1_ref, tap, px, w))

    step = steps_ref[lax.axis_index("seq")]
    lane = lax.broadcasted_iota(jnp.int32, (1, c), 1) == device()
    digits = [jnp.where(lane, d, 0).astype(F32) for d in (step // DIGIT, step % DIGIT)]
    rows = [small_ref[i : i + 1, :] for i in range(5)] + [g_n2g, g_n2b] + digits
    own = lax.broadcasted_iota(jnp.int32, (total, c), 0) == device()
    sums = [rows_of(rows, VEC_ROWS, c), jnp.where(own, col_sum(d_hidden1), 0.0)]
    put_both(keep_ref, send_ref, keep_ref.shape[0] - sums_rows(total), jnp.concatenate(sums, axis=0))


def source_kernel(
    w, vec_ref, turned1_ref, image_ref, dh2_ref, q1_ref, stat_ref, output_ref, token_ref, own_ref, *refs
):
    parts, grad_ref = refs[:-1], refs[-1]
    px, c = image_ref.shape
    count = float(px * (c // GROUPS))
    spread = spread_matrix(c)
    vec = lambda i: vec_ref[i : i + 1, :]
    inv1 = stat_ref[1:2, :]
    hat1 = (image_ref[...].astype(F32) - stat_ref[0:1, :]) * inv1
    d = conv(q1_ref, turned1_ref, px, w) * silu_slope(hat1 * vec(N1_GAIN) + vec(N1_BIAS))
    d_src1, g_n1g, g_n1b = norm_back(d, hat1, inv1, vec(N1_GAIN), spread, count)
    grad_ref[...] = (dh2_ref[...] + d_src1).astype(BF16)
    for o, part in enumerate(parts):
        rows = at_rows(lax.axis_index("seq") ^ o, part.shape[1])
        part[0] = output_ref[rows, :]
        part[1] = grad_ref[rows, :]

    half = c // 2
    own_ref[...] = jnp.zeros(own_ref.shape, BF16)
    for i in range(2):
        rows = rows_of([g_n1g[:, i * half : (i + 1) * half], g_n1b[:, i * half : (i + 1) * half]], 16, half)
        own_ref[16 * i : 16 * i + 16, :] = rows.astype(BF16)


def add_kernel(step, groups, outputs, *refs):
    count = sum(g[0] for g in groups)
    outs = refs[count + 1 :]
    radix = step[1] if step else 1
    starts = [0] * len(outs)
    used = 0
    for i, (n, first, rows, whole) in enumerate(groups):
        ins = refs[used : used + n]
        used += n
        size = rows if whole else rows // radix
        targets = range(radix) if step else [0 if i < outputs[0] else 1]
        for o in targets:
            if step and not whole:
                where = pl.ds(pl.multiple_of(first + (digit(step) ^ o) * size, 16), size)
            else:
                where = slice(first, first + size)
            total = sum(r[where, :].astype(F32) for r in ins).astype(BF16)
            outs[o][starts[o] : starts[o] + size, :] = total
            starts[o] += size


def join_kernel(step, sizes, *refs):
    ins, outs = refs[: step[1]], refs[step[1] + 1 :]
    at = 0
    for out, parts in zip(outs, sizes):
        base = 0
        for rows in parts:
            size = rows // step[1]
            for o, part in enumerate(ins):
                where = base + (digit(step) ^ o) * size
                out[pl.ds(pl.multiple_of(where, 16), size), :] = part[at : at + size, :]
            base += rows
            at += size


class Writer:
    def __init__(self, sems):
        self.sems = sems
        self.copies = []

    def send(self, source, target):
        copy = pltpu.make_async_copy(source, target, self.sems.at[len(self.copies)])
        copy.start()
        self.copies.append(copy)

    def half(self, source, at, buffer, where, target, row, col):
        n = 2 * source.shape[1]
        buffer[where : where + n, :] = source[at : at + n, :].astype(F32)
        cols = pl.ds(pl.multiple_of(col, 128), source.shape[1])
        self.send(buffer.at[pl.ds(where, n)], target.at[pl.ds(row, n), cols])

    def more(self, source, core, buffer, conv2_hbm, qkv_hbm, out_hbm):
        c = out_hbm.shape[0]
        plan = [(conv2_hbm, tap * c, 0) for tap in range(EARLY_TAPS, 9)]
        plan += [(qkv_hbm, 0, i * c) for i in range(3)] + [(out_hbm, 0, 0)]
        for i, (target, row, col) in enumerate(plan):
            self.half(source, i * c, buffer, i * c, target, row, col + core * (c // 2))

    def first(self, source, core, buffer, at, conv1_hbm):
        c = conv1_hbm.shape[1]
        for tap in range(9):
            self.half(source, tap * c, buffer, at + tap * c, conv1_hbm, tap * c, core * (c // 2))

    def wait(self):
        for copy in self.copies:
            copy.wait()


def exact_tm(a, b):
    return tm(jnp.concatenate(a, axis=0).astype(BF16), jnp.concatenate(b, axis=0).astype(BF16))


def table_kernel(total, sums_ref, table_ref, embed_ref, token_in, grad_table_hbm, grad_embed_hbm, *refs):
    vec_refs, token_ref = refs[:8], refs[8]
    grad_table_ref, grad_embed_ref, sems = refs[9:]
    token_ref[...] = jnp.zeros_like(token_ref)
    steps = table_ref.shape[0]
    writer = Writer(sems)
    n = VEC_ROWS + total

    def take(row, rows):
        return sums_ref[row : row + rows, :].astype(F32), sums_ref[n + row : n + row + rows, :].astype(F32)

    d_proj = jnp.concatenate(take(VEC_ROWS, total), axis=1)
    rows = jnp.concatenate(take(0, VEC_ROWS), axis=1)
    both = rows[HIGH : HIGH + 1, :] * DIGIT + rows[LOW : LOW + 1, :]
    c = both.shape[1]
    own = lax.broadcasted_iota(jnp.int32, (total, c), 0) == lax.broadcasted_iota(jnp.int32, (total, c), 1)
    step = jnp.sum(jnp.where(own, both, 0.0), axis=1, keepdims=True).astype(jnp.int32)
    pick = jnp.where(lax.broadcasted_iota(jnp.int32, (total, steps), 1) == step, 1.0, 0.0)
    embedded = mm(pick.astype(BF16), table_ref[...])
    d_lifted = mt(d_proj.astype(BF16), embed_ref[...])
    d_embedded = d_lifted * silu_slope(embedded)
    pieces = three(d_embedded)
    for at in range(0, steps, 256):
        part = slice(at, min(at + 256, steps))
        grad_table_ref[part, :] = exact_tm([pick[:, part]] * 3, pieces)
        writer.send(grad_table_ref.at[part], grad_table_hbm.at[part])
    grad_embed_ref[...] = exact_tm(three(silu(embedded)), [d_proj] * 3)
    writer.send(grad_embed_ref, grad_embed_hbm)
    for i, ref in enumerate(vec_refs):
        ref[...] = col_sum(d_proj) if i == EB else rows[i : i + 1, :]
    writer.wait()


def early_kernel(own, mine_ref, got_ref, token_ref, conv2_hbm, gain_ref, bias_ref, out_token_ref, conv_ref, sems):
    c = conv2_hbm.shape[1]
    half = c // 2
    out_token_ref[...] = jnp.zeros_like(out_token_ref)
    at = mine_ref.shape[0] - own
    for i in range(2):
        rows = slice(at + 16 * i, at + 16 * i + 16)
        both = mine_ref[rows, :].astype(F32) + got_ref[rows, :].astype(F32)
        gain_ref[:, i * half : (i + 1) * half] = both[0:1, :]
        bias_ref[:, i * half : (i + 1) * half] = both[1:2, :]
    first = device() & 1 == 0
    writer = Writer(sems)
    for tap in range(EARLY_TAPS):
        rows = slice(tap * c, (tap + 1) * c)
        a, b = mine_ref[rows, :].astype(F32), got_ref[rows, :].astype(F32)
        conv_ref[rows, :half] = jnp.where(first, a, b)
        conv_ref[rows, half:] = jnp.where(first, b, a)
        writer.send(conv_ref.at[rows], conv2_hbm.at[rows])
    writer.wait()


def middle_kernel(more_ref, first_ref, conv2_in, conv1_hbm, conv2_hbm, qkv_hbm, out_hbm, buffer, sems):
    writer = Writer(sems)
    core = device() & 1
    writer.more(more_ref, core, buffer, conv2_hbm, qkv_hbm, out_hbm)
    writer.first(first_ref, core, buffer, (13 - EARLY_TAPS) * out_hbm.shape[0], conv1_hbm)
    writer.wait()


def more_kernel(more_ref, conv2_in, qkv_in, out_in, token_ref, conv2_hbm, qkv_hbm, out_hbm, buffer, sems):
    writer = Writer(sems)
    writer.more(more_ref, 1 - (device() & 1), buffer, conv2_hbm, qkv_hbm, out_hbm)
    writer.wait()


def first_kernel(first_ref, conv1_in, conv1_hbm, token_ref, buffer, sems):
    token_ref[...] = jnp.zeros_like(token_ref)
    writer = Writer(sems)
    writer.first(first_ref, 1 - (device() & 1), buffer, 0, conv1_hbm)
    writer.wait()


def call(kernel, outs, specs, out_specs=None, scratch=(), limit=40, cost=1, aliases={}):
    return pl.pallas_call(
        kernel,
        out_shape=outs,
        in_specs=specs,
        out_specs=out_specs or [VMEM] * len(outs),
        scratch_shapes=scratch,
        input_output_aliases=aliases,
        compiler_params=pltpu.CompilerParams(vmem_limit_bytes=limit * 2**20),
        cost_estimate=pl.CostEstimate(flops=cost, bytes_accessed=1, transcendentals=0),
    )


def permute(array, partner, total):
    return lax.ppermute(array, AXES, [(i, partner(i)) for i in range(total)])


class Chain:
    def __init__(self, total, groups):
        self.total = total
        self.groups = groups

    def swap(self, array, low, offset):
        return permute(array, lambda i: i ^ (offset << low(i)), self.total)

    def add(self, step, token, cost=1, outputs=None):
        low, radix = step or (None, 1)
        flat = [p for g in self.groups for p in g[0]]
        sizes = [g[2] if g[3] else g[2] // radix for g in self.groups]
        outputs = outputs or [len(sizes)]
        cuts = [sum(sizes[: outputs[0]]), sum(sizes[outputs[0] :])][: len(outputs)]
        outs = [jax.ShapeDtypeStruct((n, flat[0].shape[1]), BF16) for n in (cuts if radix == 1 else cuts * radix)]
        groups = [(len(g[0]), g[1], g[2], g[3]) for g in self.groups]
        kernel = functools.partial(add_kernel, step, groups, outputs)
        outs = call(kernel, outs, [VMEM] * len(flat) + [ANY], cost=cost)(*flat, token)
        if len(outputs) > 1:
            self.parts = outs[:1]
            return outs
        self.parts = [outs[0]] + [self.swap(a, low, o + 1) for o, a in enumerate(outs[1:])]
        self.groups = [(self.parts, sum(sizes[:i]), n, g[3]) for i, (n, g) in enumerate(zip(sizes, self.groups))]
        return outs[0]

    def spread(self, step):
        low, radix = step
        self.parts = [self.parts[0]] + [self.swap(self.parts[0], low, o) for o in range(1, radix)]
        self.groups = [(self.parts,) + g[1:] for g in self.groups]

    def join(self, step, token, cost=1, sizes=None, every=False):
        rows, cols = self.parts[0].shape
        sizes = sizes or [[rows * step[1]]]
        outs = [jax.ShapeDtypeStruct((sum(n), cols), BF16) for n in sizes]
        kernel = functools.partial(join_kernel, step, sizes)
        self.parts = call(kernel, outs, [VMEM] * step[1] + [ANY], cost=cost)(*self.parts, token)
        return self.parts if every else self.parts[0]


def plan(total):
    bits = total.bit_length() - 1
    assert bits > 3 and 2**bits == total
    near = [(lambda i: 1 if i & 1 == 0 else 2, 2), (lambda i: 2 if i & 1 == 0 else 1, 2)]
    far = []
    low = 3
    while low < bits:
        take = min(2, bits - low)
        far.append((lambda i, low=low: low, 2**take))
        low += take
    return (lambda i: 0, 2), near, far


def shards(
    images, timesteps, step_table, norm1_gain, norm1_bias, conv1_weight, embed_weight, embed_bias,
    norm2_gain, norm2_bias, conv2_weight, conv2_bias, norm3_gain, norm3_bias, qkv_weight, query_bias,
    out_weight, out_bias, cotangent,
):
    maps, rows_here, w, c = images.shape
    seq = lax.axis_size("seq")
    total = lax.axis_size("dp") * seq
    assert maps == seq and total <= c
    px = rows_here * seq * w
    core, near, far = plan(total)
    shape = jax.ShapeDtypeStruct
    block = (maps, rows_here * w, c)
    pair = shape((2,) + block[1:], BF16)
    tiny = shape((8, c // 2), F32)
    field = lambda dtype: shape((px, c), dtype)
    shifted = (px + 2 * w, 3 * c)
    rows_a, rows_o, rows_v = padded(EARLY_TAPS * c, 2 * total), own_rows(total), sums_rows(total)
    rows_m, rows_1 = padded((13 - EARLY_TAPS) * c, 8 * total), padded(9 * c, 8 * total)
    conv1 = conv1_weight.reshape(9 * c, c)
    conv2 = conv2_weight.reshape(9 * c, c)

    def trade(parts):
        return [parts[0]] + [permute(p, lambda i, o=o + 1: i ^ o, total) for o, p in enumerate(parts[1:])]

    pieces = trade(
        call(pack_kernel, [pair] * seq, [HBM] * 2, None, [pltpu.SemaphoreType.DMA((2 * seq,))], 54, EARLY_COST)(
            images.reshape(block), cotangent.reshape(block)
        )
    )
    vectors = [norm1_gain, norm1_bias, norm2_gain, norm2_bias, conv2_bias, norm3_gain, norm3_bias, query_bias, out_bias, embed_bias]
    vec, turned1, turned2, qkv_turned, out_turned = call(
        setup_kernel,
        [shape((16, c), F32)] + [shape((n, c), BF16) for n in (9 * c, 9 * c, 3 * c, c)],
        [SMEM] + [VMEM] * 16,
        cost=EARLY_COST,
    )(timesteps, step_table, embed_weight, conv1, conv2, qkv_weight, out_weight, *[v.reshape(1, c) for v in vectors])
    half = lambda n: shape((n, c // 2), BF16)
    keep_e, send_e, small, output, image, act1, hat2, d_hidden2, q2, stats = call(
        functools.partial(main_kernel, w),
        [half(rows_a + rows_m)] * 2
        + [shape((8, c), F32), field(BF16), field(BF16), field(BF16), field(F32), field(F32), shape(shifted, BF16), shape((8, c), F32)],
        [VMEM] * (7 + seq),
        None,
        [pltpu.VMEM((px, c), BF16), pltpu.VMEM(shifted, BF16)],
    )(vec, conv1, conv2, qkv_weight, out_weight, qkv_turned, out_turned, *pieces)
    swap = lambda array: permute(array, lambda i: i ^ 1, total)
    got_e = swap(send_e)
    keep_1, send_1, q1 = call(
        functools.partial(back_kernel, w, total), [half(rows_1 + rows_v)] * 2 + [shape(shifted, BF16)], [SMEM] + [VMEM] * 7
    )(timesteps, vec, turned2, act1, hat2, q2, stats, small)
    got_1 = swap(send_1)
    m = Chain(total, [([keep_e, got_e], rows_a, rows_m, False)])
    token = m.add(near[0], q1)
    own, *results = call(
        functools.partial(source_kernel, w), [half(rows_o)] + [pair] * seq, [VMEM] * 7 + [ANY], None, [pltpu.VMEM((px, c), BF16)]
    )(vec, turned1, image, d_hidden2, q1, stats, output, token)
    results = trade(results)
    f = Chain(total, [([keep_1, got_1], 0, rows_1, False)])
    a = Chain(total, [([keep_e, got_e], 0, rows_a, False), ([own], 0, rows_o, False), ([keep_1, got_1], rows_1, rows_v, True)])

    far_cuts = [1]
    for _, radix in far:
        far_cuts.append(far_cuts[-1] * radix)
    sizes_a = lambda cuts: [[rows_a // cuts, rows_o // cuts]]
    sizes_b = lambda cuts: [[rows_m // cuts, rows_1 // cuts]]
    token = f.add(near[0], results[0])
    token = a.add(far[0], token)
    token = m.add(None, token, SMALL_COST)
    b = Chain(total, m.groups + f.groups)
    token = b.add(near[1], token)
    for step in far[1:] + [None]:
        token = a.add(step, token, LONG_COST)
    token = b.add(far[0], token)
    token = a.add(None, token)
    a.spread(near[0])
    for step in far[1:] + [None]:
        token = b.add(step, token, SUM_COST)
    b.spread(far[-1])
    token = a.add(None, token)
    a.spread(near[1])
    output, grad_images, token = call(unpack_kernel, [shape(block, BF16)] * 2 + [tiny], [VMEM] * seq + [ANY], cost=UNPACK_COST)(*results, token)
    for i in range(len(far))[::-1]:
        token = b.join(far[i], token, LONG_COST, sizes_b(4 * far_cuts[i]))
        b.spread(far[i - 1] if i else near[1])
    token, sums = a.add(None, token, LONG_COST, [2, 1])
    a.spread(far[-1])
    token = b.join(near[1], token, 1, sizes_b(2))
    b.spread(near[0])
    outs = [shape(step_table.shape, F32), shape(embed_weight.shape, F32)]
    grad_table, grad_embed, *vecs, token = call(
        functools.partial(table_kernel, total),
        outs + [shape((1, c), F32)] * 8 + [tiny],
        [VMEM] * 3 + [ANY],
        [HBM] * 2 + [VMEM] * 9,
        [pltpu.VMEM(o.shape, F32) for o in outs] + [pltpu.SemaphoreType.DMA((1 + -(-step_table.shape[0] // 256),))],
    )(sums, step_table, embed_weight, token)
    for i in range(len(far))[::-1]:
        token = a.join(far[i], token, LONG_COST, sizes_a(far_cuts[i]))
        a.spread(far[i - 1] if i else core)
    grads = [shape((9 * c, c), F32), shape((9 * c, c), F32), shape(qkv_weight.shape, F32), shape(out_weight.shape, F32)]
    grad_conv2, grad_norm1_gain, grad_norm1_bias, token = call(
        functools.partial(early_kernel, rows_o),
        grads[:1] + [shape((1, c), F32)] * 2 + [tiny],
        [VMEM] * 2 + [ANY],
        [HBM] + [VMEM] * 3,
        [pltpu.VMEM((EARLY_TAPS * c, c), F32), pltpu.SemaphoreType.DMA((EARLY_TAPS,))],
    )(*a.parts, token)
    more, first = b.join(near[0], token, 1, [[rows_m], [rows_1]], True)
    got_more, got_first = swap(more), swap(first)
    scratch = lambda blocks: [pltpu.VMEM((blocks * c, c // 2), F32), pltpu.SemaphoreType.DMA((blocks,))]
    count = 13 - EARLY_TAPS
    grad_conv1, *others = call(middle_kernel, grads, [VMEM] * 2 + [HBM], [HBM] * 4, scratch(count + 9), aliases={2: 1})(more, first, grad_conv2)
    grad_conv1, token = call(first_kernel, grads[:1] + [tiny], [VMEM, HBM], [HBM, VMEM], scratch(9), aliases={1: 0})(got_first, grad_conv1)
    grad_conv2, grad_qkv, grad_out = call(
        more_kernel, grads[1:], [VMEM] + [HBM] * 3 + [ANY], [HBM] * 3, scratch(count), aliases={1: 0, 2: 1, 3: 2}
    )(got_more, *others, token)
    one = lambda r: vecs[r].reshape(c)
    return (
        output.reshape(images.shape), grad_images.reshape(images.shape), grad_table, grad_norm1_gain.reshape(c), grad_norm1_bias.reshape(c),
        grad_conv1.reshape(conv1_weight.shape), grad_embed, one(EB), one(N2G), one(N2B), grad_conv2.reshape(conv2_weight.shape),
        one(C2B), one(N3G), one(N3B), grad_qkv, one(QB), grad_out, one(OB),
    )


def solution(mesh):
    field = P("dp", "seq", None, None)
    return jax.shard_map(
        shards,
        mesh=mesh,
        in_specs=(field, P("dp")) + (P(),) * 16 + (field,),
        out_specs=(field, field) + (P(),) * 16,
        check_vma=False,
    )
```

time: 364 us -> 74.4 us (0.20)
  waiting for transfers between devices: 164 us -> 19.8 us
  blocking collectives: 106 us -> 0 us
  local copies, waits for them, and re-layouts: 31.8 us -> 0.08 us
  matrix products: 24.2 us -> 0 us
  Pallas kernels: 0 us -> 20.9 us
  starting transfers between devices: 11.4 us -> 32.3 us
  between operations: 15 us -> 1.17 us
  other arithmetic: 11.3 us -> 0 us
    psum x1 -> x0, waiting for transfers between devices: 121 us -> none  [shards(): lax.psum((grad_step_table, grad_norm1_gain, grad_norm1_bias, grad_conv1_w...]
    psum x7 -> x0, blocking collectives: 91.1 us -> none  [the longest x1 41.8 us: shards(): lax.psum((grad_step_table, grad_norm1_gain, grad_norm1_bias, grad_conv1_w...]
    reduce_scatter x2 -> x0, waiting for transfers between devices: 35.8 us -> none  [the longest x1 24.9 us: shards(): lax.psum_scatter(grad_values.astype(jnp.bfloat16), 'seq', scatter_dimensi...]
    dot_general x23 -> x0, matrix products: 24.2 us -> none  [the longest x2 3.75 us: kernel_grad(): lax.dot_general(columns, grad_branch.reshape(-1, channels), (((0,), (0,))...]
    ppermute x8 -> x30, starting transfers between devices: 11.2 us -> 32.3 us  [permute(): return lax.ppermute(array, AXES, [(i, partner(i)) for i in range(total)])]
    pallas_call x0 -> x26, Pallas kernels: none -> 20.9 us  [the longest x1 4.76 us: shards(): call(functools.partial(main_kernel, w), [half(rows_a + rows_m)] * 2 + [sh...]
    unnamed x137 -> x36, local copies, waits for them, and re-layouts: 20.6 us -> 0.08 us
    all_gather x2 -> x0, blocking collectives: 14.6 us -> none  [the longest x1 7.3 us: shards(): lax.all_gather(own_values, 'seq', axis=1, tiled=True)]
  transfers between devices with their start and end apart: 11 -> 30, of which waited for: 7 -> 12; matrix products, arithmetic and copies ran while one was open for 5% -> 0% of each run, Pallas kernels for 0% -> 18%
where the time goes in v1:
time: 74.4 us; the launch traced here: 74.2 us
  starting transfers between devices  32.3 us (43%)
  Pallas kernels  20.9 us (28%)
  waiting for transfers between devices  19.8 us (27%)
  between operations  1.17 us (2%)
    ppermute x30, starting transfers between devices, permute(): return lax.ppermute(array, AXES, [(i, partner(i)) for i in range(total)])  32.3 us
    ppermute x30, waiting for transfers between devices, permute(): return lax.ppermute(array, AXES, [(i, partner(i)) for i in range(total)])  19.8 us
    pallas_call x1, Pallas kernels, shards(): call(functools.partial(main_kernel, w), [half(rows_a + rows_m)] * 2 + [sh...  4.76 us
    pallas_call x1, Pallas kernels, shards(): call(functools.partial(table_kernel, total), outs + [shape((1, c), F32)]...  2.79 us
    pallas_call x1, Pallas kernels, shards(): call(functools.partial(back_kernel, w, total), [half(rows_1 + rows_v)] *...  2.38 us
    pallas_call x1, Pallas kernels, shards(): call(pack_kernel, [pair] * seq, [HBM] * 2, None, [pltpu.SemaphoreType.DMA...  1.79 us
    pallas_call x1, Pallas kernels, shards(): call(functools.partial(early_kernel, rows_o), grads[:1] + [shape((1, c),...  1.69 us
    pallas_call x1, Pallas kernels, shards(): call(middle_kernel, grads, [VMEM] * 2 + [HBM], [HBM] * 4, scratch(count +...  1.5 us
  transfers between devices with their start and end apart: 30, of which 12 were waited for; matrix products, arithmetic and copies ran while one was open for 0% of the time, Pallas kernels for 18%

profile of v1, /device:TPU:0, one launch (start us, length us, event | category | flops | bytes accessed | tf_op | source)
XLA Modules:
  0.0 74.2 jit_solution(10601380123564511156)
XLA Ops:
  0.8 1.8 %shard_map.323 = (bf16[2,64,256]{2,1,0:T(8,128)(2,1)}, bf16[2,64,256]{2,1,0:T(8,128)(2,1)}, bf16[2,64,256]{2,1,0:T(8,128)(2,1)}, bf16[2,64,256]{2,1,0:T(8,128)(2,1)}) custom-call(bf16[4,64,256]{2,1,0:T(8,128)(2,1)} %bitcast.44, bf16[4,64,256]{2,1,0:T(8,128)(2,1)} %bitcast.45), custom_call_target="tpu_custom_call" | custom-call | flops 20000000000 | bytes 1 | tf_op jit(solution)/shard_map/pallas_call | solution.py:570
  2.6 0.5 collective-permute-start
  3.1 2.6 %collective-permute-start.1 = (bf16[2,64,256]{2,1,0:T(8,128)(2,1)}, bf16[2,64,256]{2,1,0:T(8,128)(2,1)S(1)}, u32[]{:S(2)}, u32[]{:S(2)}) collective-permute-start(bf16[2,64,256]{2,1,0:T(8,128)(2,1)} %get-tuple-element.96), channel_id=1, source_target_pairs={{0,2},{1,3},{2,0},{3,1},{4,6},{5,7},{6,4},{7,5},{8,10},{9,11},{10,... | collective-permute-start | bytes 196616 | tf_op jit(solution)/shard_map/ppermute | solution.py:489
  5.7 0.1 collective-permute-start.2
  6.0 0.0 copy-start.6
  6.0 1.4 %shard_map.322 = (f32[16,256]{1,0:T(8,128)S(1)}, bf16[2304,256]{1,0:T(8,128)(2,1)S(1)}, bf16[2304,256]{1,0:T(8,128)(2,1)S(1)}, bf16[768,256]{1,0:T(8,128)(2,1)S(1)}, bf16[256,256]{1,0:T(8,128)(2,1)S(1)}) custom-call(s32[4]{0:T(128)S(1)} %copy-done.7, bf16[1000,512]{1,0:T(8,128)(2,1)S(1)} %copy-done.2, bf16[512,256]{1,0:T(8,128)(2,1)S(1)} %copy-done.4, ...), custom_call_target="tpu_custom_call" | custom-call | flops 20000000000 | bytes 1 | tf_op jit(solution)/shard_map/pallas_call | solution.py:575
  7.3 1.3 %collective-permute-done.1.refs_2_ = bf16[2,64,256]{2,1,0:T(8,128)(2,1)S(1)} collective-permute-done((bf16[2,64,256]{2,1,0:T(8,128)(2,1)}, bf16[2,64,256]{2,1,0:T(8,128)(2,1)S(1)}, u32[]{:S(2)}, u32[]{:S(2)}) %collective-permute-start.1) | collective-permute-done | bytes 65568 | tf_op jit(solution)/shard_map/ppermute | solution.py:489
  8.6 1.4 %collective-permute-done.2.refs_3_ = bf16[2,64,256]{2,1,0:T(8,128)(2,1)S(1)} collective-permute-done((bf16[2,64,256]{2,1,0:T(8,128)(2,1)}, bf16[2,64,256]{2,1,0:T(8,128)(2,1)S(1)}, u32[]{:S(2)}, u32[]{:S(2)}) %collective-permute-start.2) | collective-permute-done | bytes 65568 | tf_op jit(solution)/shard_map/ppermute | solution.py:489
  10.1 4.8 %shard_map.324 = (bf16[3328,128]{1,0:T(8,128)(2,1)S(1)}, bf16[3328,128]{1,0:T(8,128)(2,1)S(1)}, f32[8,256]{1,0:T(8,128)S(1)}, bf16[256,256]{1,0:T(8,128)(2,1)S(1...) custom-call(f32[16,256]{1,0:T(8,128)S(1)} %get-tuple-element.90.vec_, ...), custom_call_target="tpu_custom_call" | custom-call | flops 1 | bytes 1 | tf_op jit(solution)/shard_map/pallas_call | solution.py:582
  14.9 0.2 collective-permute-start.3
  15.0 2.4 %shard_map.325 = (bf16[2400,128]{1,0:T(8,128)(2,1)S(1)}, bf16[2400,128]{1,0:T(8,128)(2,1)S(1)}, bf16[288,768]{1,0:T(8,128)(2,1)S(1)}) custom-call(s32[4]{0:T(128)S(1)} %copy-done.7, f32[16,256]{1,0:T(8,128)S(1)} %get-tuple-element.90.vec_ref, bf16[2304,256]{1,0:T(8,128)(2,1)S(1)} %get-tuple-element.100.turned2_ref, ...), custom_call_target="tpu_custom_call" | custom-call | flops 1 | bytes 1 | tf_op jit(solution)/shard_map/pallas_call | solution.py:592
  17.4 0.5 collective-permute-start.7
  17.9 0.1 shard_map.326
  18.0 1.3 %collective-permute-start.11 = (bf16[1024,128]{1,0:T(8,128)(2,1)S(1)}, bf16[1024,128]{1,0:T(8,128)(2,1)S(1)}, u32[]{:S(2)}, u32[]{:S(2)}) collective-permute-start(bf16[1024,128]{1,0:T(8,128)(2,1)S(1)} %get-tuple-element.123), channel_id=1, source_target_pairs={{0,2},{1,5},{2,0},{3,7},{4,6},{5,1},{6,4},{7,3},{8,10},{9,13},{10,... | collective-permute-start | bytes 786440 | tf_op jit(solution)/shard_map/ppermute | solution.py:489
  19.3 0.7 shard_map.327
  20.1 0.2 shard_map.328
  20.2 0.9 %collective-permute-start.12 = (bf16[1152,128]{1,0:T(8,128)(2,1)S(1)}, bf16[1152,128]{1,0:T(8,128)(2,1)S(1)}, u32[]{:S(2)}, u32[]{:S(2)}) collective-permute-start(bf16[1152,128]{1,0:T(8,128)(2,1)S(1)} %get-tuple-element.124), channel_id=1, source_target_pairs={{0,2},{1,5},{2,0},{3,7},{4,6},{5,1},{6,4},{7,3},{8,10},{9,13},{10,... | collective-permute-start | bytes 884744 | tf_op jit(solution)/shard_map/ppermute | solution.py:489
  21.1 0.1 shard_map.329
  21.2 3.7 %collective-permute-start.10 = (bf16[432,128]{1,0:T(8,128)(2,1)S(1)}, bf16[432,128]{1,0:T(8,128)(2,1)S(1)}, u32[]{:S(2)}, u32[]{:S(2)}) collective-permute-start(bf16[432,128]{1,0:T(8,128)(2,1)S(1)} %get-tuple-element.122), channel_id=1, source_target_pairs={{0,24},{1,25},{2,26},{3,27},{4,28},{5,29},{6,30},{7,31},{8,16},{9,... | collective-permute-start | bytes 331784 | tf_op jit(solution)/shard_map/ppermute | solution.py:489
  24.9 0.8 %collective-permute-start.9 = (bf16[432,128]{1,0:T(8,128)(2,1)S(1)}, bf16[432,128]{1,0:T(8,128)(2,1)S(1)}, u32[]{:S(2)}, u32[]{:S(2)}) collective-permute-start(bf16[432,128]{1,0:T(8,128)(2,1)S(1)} %get-tuple-element.121), channel_id=1, source_target_pairs={{0,16},{1,17},{2,18},{3,19},{4,20},{5,21},{6,22},{7,23},{8,24},{9,... | collective-permute-start | bytes 331784 | tf_op jit(solution)/shard_map/ppermute | solution.py:489
  25.7 0.1 shard_map.330.refs_0_.refs_3_
  25.8 1.9 %collective-permute-done.12.refs_2_ = bf16[1152,128]{1,0:T(8,128)(2,1)S(1)} collective-permute-done((bf16[1152,128]{1,0:T(8,128)(2,1)S(1)}, bf16[1152,128]{1,0:T(8,128)(2,1)S(1)}, u32[]{:S(2)}, u32[]{:S(2)}) %collective-permute-start.12) | collective-permute-done | bytes 294944 | tf_op jit(solution)/shard_map/ppermute | solution.py:489
  27.6 0.1 shard_map.331
  27.7 1.6 %collective-permute-start.13 = (bf16[1088,128]{1,0:T(8,128)(2,1)S(1)}, bf16[1088,128]{1,0:T(8,128)(2,1)S(1)}, u32[]{:S(2)}, u32[]{:S(2)}) collective-permute-start(bf16[1088,128]{1,0:T(8,128)(2,1)S(1)} %get-tuple-element.126), channel_id=1, source_target_pairs={{0,4},{1,3},{2,6},{3,1},{4,0},{5,7},{6,2},{7,5},{8,12},{9,11},{10,... | collective-permute-start | bytes 835592 | tf_op jit(solution)/shard_map/ppermute | solution.py:489
  29.3 2.5 %collective-permute-done.8.refs_1_.refs_5_.refs_9_ = bf16[432,128]{1,0:T(8,128)(2,1)S(1)} collective-permute-done((bf16[432,128]{1,0:T(8,128)(2,1)S(1)}, bf16[432,128]{1,0:T(8,128)(2,1)S(1)}, u32[]{:S(2)}, u32[]{:S(2)}) %collective-permute-start.8) | collective-permute-done | bytes 110624 | tf_op jit(solution)/shard_map/ppermute | solution.py:489
  31.8 2.8 %collective-permute-done.9.refs_2_.refs_6_.refs_10_ = bf16[432,128]{1,0:T(8,128)(2,1)S(1)} collective-permute-done((bf16[432,128]{1,0:T(8,128)(2,1)S(1)}, bf16[432,128]{1,0:T(8,128)(2,1)S(1)}, u32[]{:S(2)}, u32[]{:S(2)}) %collective-permute-start.9) | collective-permute-done | bytes 110624 | tf_op jit(solution)/shard_map/ppermute | solution.py:489
  34.6 0.1 shard_map.332.refs_4_.refs_0_.refs_1_.refs_2_
  34.7 0.1 shard_map.333
  34.7 1.3 %collective-permute-start.15 = (bf16[272,128]{1,0:T(8,128)(2,1)S(1)}, bf16[272,128]{1,0:T(8,128)(2,1)S(1)}, u32[]{:S(2)}, u32[]{:S(2)}) collective-permute-start(bf16[272,128]{1,0:T(8,128)(2,1)S(1)} %get-tuple-element.128), channel_id=1, source_target_pairs={{0,8},{1,9},{2,10},{3,11},{4,12},{5,13},{6,14},{7,15},{8,0},{9,1},... | collective-permute-start | bytes 208904 | tf_op jit(solution)/shard_map/ppermute | solution.py:489
  36.1 2.6 %collective-permute-start.16 = (bf16[272,128]{1,0:T(8,128)(2,1)S(1)}, bf16[272,128]{1,0:T(8,128)(2,1)S(1)}, u32[]{:S(2)}, u32[]{:S(2)}) collective-permute-start(bf16[272,128]{1,0:T(8,128)(2,1)S(1)} %get-tuple-element.129), channel_id=1, source_target_pairs={{0,16},{1,17},{2,18},{3,19},{4,20},{5,21},{6,22},{7,23},{8,24},{9,... | collective-permute-start | bytes 208904 | tf_op jit(solution)/shard_map/ppermute | solution.py:489
  38.7 0.5 collective-permute-start.17
  39.2 1.3 %collective-permute-start.14 = (bf16[432,128]{1,0:T(8,128)(2,1)S(1)}, bf16[432,128]{1,0:T(8,128)(2,1)S(1)}, u32[]{:S(2)}, u32[]{:S(2)}) collective-permute-start(bf16[432,128]{1,0:T(8,128)(2,1)S(1)} %shard_map.334.refs_8_.refs_0_.refs_2_.refs_4_), channel_id=1, source_target_pairs={{0,2},{1,5},{2,0},{3,7},{4,6},{5,1},{6,4},{7,3},{8,10},{9,13},{10,... | collective-permute-start | bytes 331784 | tf_op jit(solution)/shard_map/ppermute | solution.py:489
  40.6 0.8 %collective-permute-start.5 = (bf16[2,64,256]{2,1,0:T(8,128)(2,1)S(1)}, bf16[2,64,256]{2,1,0:T(8,128)(2,1)S(1)}, u32[]{:S(2)}, u32[]{:S(2)}) collective-permute-start(bf16[2,64,256]{2,1,0:T(8,128)(2,1)S(1)} %get-tuple-element.113), channel_id=1, source_target_pairs={{0,2},{1,3},{2,0},{3,1},{4,6},{5,7},{6,4},{7,5},{8,10},{9,11},{10,... | collective-permute-start | bytes 196616 | tf_op jit(solution)/shard_map/ppermute | solution.py:489
  41.3 1.4 %collective-permute-done.16.refs_2_.refs_6_ = bf16[272,128]{1,0:T(8,128)(2,1)S(1)} collective-permute-done((bf16[272,128]{1,0:T(8,128)(2,1)S(1)}, bf16[272,128]{1,0:T(8,128)(2,1)S(1)}, u32[]{:S(2)}, u32[]{:S(2)}) %collective-permute-start.16) | collective-permute-done | bytes 69664 | tf_op jit(solution)/shard_map/ppermute | solution.py:489
  42.8 0.0 collective-permute-start.6
  42.8 2.0 %collective-permute-done.17.refs_3_.refs_7_ = bf16[272,128]{1,0:T(8,128)(2,1)S(1)} collective-permute-done((bf16[272,128]{1,0:T(8,128)(2,1)S(1)}, bf16[272,128]{1,0:T(8,128)(2,1)S(1)}, u32[]{:S(2)}, u32[]{:S(2)}) %collective-permute-start.17) | collective-permute-done | bytes 69664 | tf_op jit(solution)/shard_map/ppermute | solution.py:489
  44.8 0.1 collective-permute-start.19
  44.9 0.0 collective-permute-done.4.refs_1_
  44.9 1.7 %collective-permute-start.20 = (bf16[272,128]{1,0:T(8,128)(2,1)S(1)}, bf16[272,128]{1,0:T(8,128)(2,1)S(1)}, u32[]{:S(2)}, u32[]{:S(2)}) collective-permute-start(bf16[272,128]{1,0:T(8,128)(2,1)S(1)} %shard_map.335.refs_6_.refs_0_), channel_id=1, source_target_pairs={{0,16},{1,17},{2,18},{3,19},{4,20},{5,21},{6,22},{7,23},{8,24},{9,... | collective-permute-start | bytes 208904 | tf_op jit(solution)/shard_map/ppermute | solution.py:489
  46.6 0.0 collective-permute-done.14.refs_1_.refs_3_.refs_5_
  46.6 2.7 %collective-permute-start.21 = (bf16[272,128]{1,0:T(8,128)(2,1)S(1)}, bf16[272,128]{1,0:T(8,128)(2,1)S(1)}, u32[]{:S(2)}, u32[]{:S(2)}) collective-permute-start(bf16[272,128]{1,0:T(8,128)(2,1)S(1)} %shard_map.335.refs_6_.refs_0_), channel_id=1, source_target_pairs={{0,24},{1,25},{2,26},{3,27},{4,28},{5,29},{6,30},{7,31},{8,16},{9,... | collective-permute-start | bytes 208904 | tf_op jit(solution)/shard_map/ppermute | solution.py:489
  49.3 0.0 collective-permute-done.5.refs_2_
  49.3 1.6 %collective-permute-start.18 = (bf16[432,128]{1,0:T(8,128)(2,1)S(1)}, bf16[432,128]{1,0:T(8,128)(2,1)S(1)}, u32[]{:S(2)}, u32[]{:S(2)}) collective-permute-start(bf16[432,128]{1,0:T(8,128)(2,1)S(1)} %shard_map.336.refs_4_.refs_0_.refs_2_), channel_id=1, source_target_pairs={{0,4},{1,3},{2,6},{3,1},{4,0},{5,7},{6,2},{7,5},{8,12},{9,11},{10,... | collective-permute-start | bytes 331784 | tf_op jit(solution)/shard_map/ppermute | solution.py:489
  50.9 0.7 shard_map.337
  51.6 2.0 %collective-permute-done.20.refs_2_ = bf16[272,128]{1,0:T(8,128)(2,1)S(1)} collective-permute-done((bf16[272,128]{1,0:T(8,128)(2,1)S(1)}, bf16[272,128]{1,0:T(8,128)(2,1)S(1)}, u32[]{:S(2)}, u32[]{:S(2)}) %collective-permute-start.20) | collective-permute-done | bytes 69664 | tf_op jit(solution)/shard_map/ppermute | solution.py:489
  53.6 0.0 collective-permute-done.21.refs_3_
  53.6 1.7 %collective-permute-start.22 = (bf16[1088,128]{1,0:T(8,128)(2,1)S(1)}, bf16[1088,128]{1,0:T(8,128)(2,1)S(1)}, u32[]{:S(2)}, u32[]{:S(2)}) collective-permute-start(bf16[1088,128]{1,0:T(8,128)(2,1)S(1)} %shard_map.338.refs_6_.refs_0_), channel_id=1, source_target_pairs={{0,4},{1,3},{2,6},{3,1},{4,0},{5,7},{6,2},{7,5},{8,12},{9,11},{10,... | collective-permute-start | bytes 835592 | tf_op jit(solution)/shard_map/ppermute | solution.py:489
  55.3 1.5 %collective-permute-start.23 = (bf16[336,128]{1,0:T(8,128)(2,1)S(1)}, bf16[336,128]{1,0:T(8,128)(2,1)S(1)}, u32[]{:S(2)}, u32[]{:S(2)}) collective-permute-start(bf16[336,128]{1,0:T(8,128)(2,1)S(1)} %get-tuple-element.135.refs_2_.refs_0_), channel_id=1, source_target_pairs={{0,8},{1,9},{2,10},{3,11},{4,12},{5,13},{6,14},{7,15},{8,0},{9,1},... | collective-permute-start | bytes 258056 | tf_op jit(solution)/shard_map/ppermute | solution.py:489
  56.8 1.4 %collective-permute-start.24 = (bf16[336,128]{1,0:T(8,128)(2,1)S(1)}, bf16[336,128]{1,0:T(8,128)(2,1)S(1)}, u32[]{:S(2)}, u32[]{:S(2)}) collective-permute-start(bf16[336,128]{1,0:T(8,128)(2,1)S(1)} %get-tuple-element.135.refs_2_.refs_0_), channel_id=1, source_target_pairs={{0,16},{1,17},{2,18},{3,19},{4,20},{5,21},{6,22},{7,23},{8,24},{9,... | collective-permute-start | bytes 258056 | tf_op jit(solution)/shard_map/ppermute | solution.py:489
  58.2 1.5 %collective-permute-start.25 = (bf16[336,128]{1,0:T(8,128)(2,1)S(1)}, bf16[336,128]{1,0:T(8,128)(2,1)S(1)}, u32[]{:S(2)}, u32[]{:S(2)}) collective-permute-start(bf16[336,128]{1,0:T(8,128)(2,1)S(1)} %get-tuple-element.135.refs_2_.refs_0_), channel_id=1, source_target_pairs={{0,24},{1,25},{2,26},{3,27},{4,28},{5,29},{6,30},{7,31},{8,16},{9,... | collective-permute-start | bytes 258056 | tf_op jit(solution)/shard_map/ppermute | solution.py:489
  59.8 0.5 collective-permute-done.22.refs_1_
  60.3 1.0 %collective-permute-start.27 = (bf16[2176,128]{1,0:T(8,128)(2,1)S(1)}, bf16[2176,128]{1,0:T(8,128)(2,1)S(1)}, u32[]{:S(2)}, u32[]{:S(2)}) collective-permute-start(bf16[2176,128]{1,0:T(8,128)(2,1)S(1)} %shard_map.340.token_in.refs_0_), channel_id=1, source_target_pairs={{0,2},{1,5},{2,0},{3,7},{4,6},{5,1},{6,4},{7,3},{8,10},{9,13},{10,... | collective-permute-start | bytes 1671176 | tf_op jit(solution)/shard_map/ppermute | solution.py:489
  61.3 2.8 %shard_map.341 = (f32[1000,512]{1,0:T(8,128)}, f32[512,256]{1,0:T(8,128)}, f32[1,256]{1,0:T(1,128)}, f32[1,256]{1,0:T(1,128)}, f32[1,256]{1,0:T(1,128)}, /*index...) custom-call(bf16[96,128]{1,0:T(8,128)(2,1)S(1)} %get-tuple-element.1, ...), custom_call_target="tpu_custom_call" | custom-call | flops 1 | bytes 1 | tf_op jit(solution)/shard_map/pallas_call | solution.py:634
  64.1 0.5 collective-permute-done.25.refs_3_
  64.7 0.1 collective-permute-start.26
  64.7 1.6 %collective-permute-done.26.got_ref = bf16[1344,128]{1,0:T(8,128)(2,1)S(1)} collective-permute-done((bf16[1344,128]{1,0:T(8,128)(2,1)S(1)}, bf16[1344,128]{1,0:T(8,128)(2,1)S(1)}, u32[]{:S(2)}, u32[]{:S(2)}) %collective-permute-start.26) | collective-permute-done | bytes 344096 | tf_op jit(solution)/shard_map/ppermute | solution.py:489
  66.4 1.7 %shard_map.343 = (f32[2304,256]{1,0:T(8,128)}, f32[1,256]{1,0:T(1,128)}, f32[1,256]{1,0:T(1,128)}, f32[8,128]{1,0:T(8,128)S(1)}) custom-call(bf16[1344,128]{1,0:T(8,128)(2,1)S(1)} %shard_map.342.mine_ref.token_ref, bf16[1344,128]{1,0:T(8,128)(2,1)S(1)} %collective-permute-done.26.got_ref, bf16[1344,128]{1,0:T(8,128)(2,1)S(1)} %shard_map.342.mine_ref.token_ref), custom_call_target="tpu_custom_call" | custom-call | flops 1 | bytes 1 | tf_op jit(solution)/shard_map/pallas_call | solution.py:645
  68.1 1.8 %collective-permute-done.27.refs_1_ = bf16[2176,128]{1,0:T(8,128)(2,1)S(1)} collective-permute-done((bf16[2176,128]{1,0:T(8,128)(2,1)S(1)}, bf16[2176,128]{1,0:T(8,128)(2,1)S(1)}, u32[]{:S(2)}, u32[]{:S(2)}) %collective-permute-start.27) | collective-permute-done | bytes 557088 | tf_op jit(solution)/shard_map/ppermute | solution.py:489
  69.9 0.1 shard_map.344
  70.0 0.1 collective-permute-start.28
  70.1 0.5 collective-permute-start.29
  70.6 1.5 %shard_map.345 = (f32[2304,256]{1,0:T(8,128)}, f32[2304,256]{1,0:T(8,128)}, f32[256,768]{1,0:T(8,128)}, f32[256,256]{1,0:T(8,128)}) custom-call(bf16[2048,128]{1,0:T(8,128)(2,1)S(1)} %get-tuple-element.142.more_ref, bf16[2304,128]{1,0:T(8,128)(2,1)S(1)} %get-tuple-element.141.first_ref, ...), custom_call_target="tpu_custom_call", output_to_operand_aliasing={{1}: (2, {})} | custom-call | flops 1 | bytes 1 | tf_op jit(solution)/shard_map/pallas_call | solution.py:656
  72.1 1.1 %shard_map.346 = (f32[2304,256]{1,0:T(8,128)}, f32[8,128]{1,0:T(8,128)S(1)}) custom-call(bf16[2304,128]{1,0:T(8,128)(2,1)S(1)} %collective-permute-done.28.first_ref, f32[2304,256]{1,0:T(8,128)} %get-tuple-element.144.conv1_in), custom_call_target="tpu_custom_call", output_to_operand_aliasing={{0}: (1, {})} | custom-call | flops 1 | bytes 1 | tf_op jit(solution)/shard_map/pallas_call | solution.py:657
  73.2 1.0 %shard_map.347 = (f32[2304,256]{1,0:T(8,128)}, f32[256,768]{1,0:T(8,128)}, f32[256,256]{1,0:T(8,128)}) custom-call(bf16[2048,128]{1,0:T(8,128)(2,1)S(1)} %collective-permute-done.29.more_ref, f32[2304,256]{1,0:T(8,128)} %get-tuple-element.150.conv2_in, ...), custom_call_target="tpu_custom_call", output_to_operand_aliasing={{0}: (1, {}), {1}: (2, {}), {2}: (3, {})} | custom-call | flops 1 | bytes 1 | tf_op jit(solution)/shard_map/pallas_call | solution.py:658
  (58 shorter events, 0.3 us)
Async XLA Ops:
  0.7 5.1 %copy-start = (bf16[3,3,256,256]{3,2,1,0:T(8,128)(2,1)S(1)}, bf16[3,3,256,256]{3,2,1,0:T(8,128)(2,1)}, u32[]{:S(2)}) copy-start(bf16[3,3,256,256]{3,2,1,0:T(8,128)(2,1)} %param.24) | copy-start | bytes 3538948
  0.7 5.1 %copy-start.1 = (bf16[3,3,256,256]{3,2,1,0:T(8,128)(2,1)S(1)}, bf16[3,3,256,256]{3,2,1,0:T(8,128)(2,1)}, u32[]{:S(2)}) copy-start(bf16[3,3,256,256]{3,2,1,0:T(8,128)(2,1)} %param.29) | copy-start | bytes 3538948
  0.7 5.1 %copy-start.2 = (bf16[1000,512]{1,0:T(8,128)(2,1)S(1)}, bf16[1000,512]{1,0:T(8,128)(2,1)}, u32[]{:S(2)}) copy-start(bf16[1000,512]{1,0:T(8,128)(2,1)} %table_ref.3) | copy-start | bytes 3072004
  0.7 5.1 %copy-start.3 = (bf16[256,768]{1,0:T(8,128)(2,1)S(1)}, bf16[256,768]{1,0:T(8,128)(2,1)}, u32[]{:S(2)}) copy-start(bf16[256,768]{1,0:T(8,128)(2,1)} %qkv_ref.3) | copy-start | bytes 1179652
  0.7 5.1 %copy-start.4 = (bf16[512,256]{1,0:T(8,128)(2,1)S(1)}, bf16[512,256]{1,0:T(8,128)(2,1)}, u32[]{:S(2)}) copy-start(bf16[512,256]{1,0:T(8,128)(2,1)} %embed_ref.3) | copy-start | bytes 786436
  0.7 5.1 %copy-start.5 = (bf16[256,256]{1,0:T(8,128)(2,1)S(1)}, bf16[256,256]{1,0:T(8,128)(2,1)}, u32[]{:S(2)}) copy-start(bf16[256,256]{1,0:T(8,128)(2,1)} %out_ref.3) | copy-start | bytes 393220
  0.7 5.1 %copy-start.7 = (s32[4]{0:T(128)S(1)}, s32[4]{0:T(128)}, u32[]{:S(2)}) copy-start(s32[4]{0:T(128)} %steps_ref.3) | copy-start | bytes 52
  0.7 5.1 %copy-start.8 = (f32[256]{0:T(256)S(1)}, f32[256]{0:T(256)}, u32[]{:S(2)}) copy-start(f32[256]{0:T(256)} %param.22) | copy-start | bytes 3076
  0.7 5.1 %copy-start.9 = (f32[256]{0:T(256)S(1)}, f32[256]{0:T(256)}, u32[]{:S(2)}) copy-start(f32[256]{0:T(256)} %param.23) | copy-start | bytes 3076
  0.8 5.1 %copy-start.10 = (f32[256]{0:T(256)S(1)}, f32[256]{0:T(256)}, u32[]{:S(2)}) copy-start(f32[256]{0:T(256)} %param.27) | copy-start | bytes 3076
  0.8 5.1 %copy-start.11 = (f32[256]{0:T(256)S(1)}, f32[256]{0:T(256)}, u32[]{:S(2)}) copy-start(f32[256]{0:T(256)} %param.28) | copy-start | bytes 3076
  0.8 5.1 %copy-start.12 = (f32[256]{0:T(256)S(1)}, f32[256]{0:T(256)}, u32[]{:S(2)}) copy-start(f32[256]{0:T(256)} %param.30) | copy-start | bytes 3076
  0.8 5.1 %copy-start.13 = (f32[256]{0:T(256)S(1)}, f32[256]{0:T(256)}, u32[]{:S(2)}) copy-start(f32[256]{0:T(256)} %param.31) | copy-start | bytes 3076
  0.8 5.1 %copy-start.14 = (f32[256]{0:T(256)S(1)}, f32[256]{0:T(256)}, u32[]{:S(2)}) copy-start(f32[256]{0:T(256)} %param.32) | copy-start | bytes 3076
  0.8 5.1 %copy-start.15 = (f32[256]{0:T(256)S(1)}, f32[256]{0:T(256)}, u32[]{:S(2)}) copy-start(f32[256]{0:T(256)} %param.34) | copy-start | bytes 3076
  0.8 5.1 %copy-start.16 = (f32[256]{0:T(256)S(1)}, f32[256]{0:T(256)}, u32[]{:S(2)}) copy-start(f32[256]{0:T(256)} %param.36) | copy-start | bytes 3076
  0.8 5.1 %copy-start.17 = (f32[256]{0:T(256)S(1)}, f32[256]{0:T(256)}, u32[]{:S(2)}) copy-start(f32[256]{0:T(256)} %param.26) | copy-start | bytes 3076
  2.6 4.7 %collective-permute-start = (bf16[2,64,256]{2,1,0:T(8,128)(2,1)}, bf16[2,64,256]{2,1,0:T(8,128)(2,1)S(1)}, u32[]{:S(2)}, u32[]{:S(2)}) collective-permute-start(bf16[2,64,256]{2,1,0:T(8,128)(2,1)} %get-tuple-element.95), channel_id=1, source_target_pairs={{0,1},{1,0},{2,3},{3,2},{4,5},{5,4},{6,7},{7,6},{8,9},{9,8},{10,11... | collective-permute-start | bytes 196616 | tf_op jit(solution)/shard_map/ppermute | solution.py:489
  3.1 5.5 %collective-permute-start.1 = (bf16[2,64,256]{2,1,0:T(8,128)(2,1)}, bf16[2,64,256]{2,1,0:T(8,128)(2,1)S(1)}, u32[]{:S(2)}, u32[]{:S(2)}) collective-permute-start(bf16[2,64,256]{2,1,0:T(8,128)(2,1)} %get-tuple-element.96), channel_id=1, source_target_pairs={{0,2},{1,3},{2,0},{3,1},{4,6},{5,7},{6,4},{7,5},{8,10},{9,11},{10,... | collective-permute-start | bytes 196616 | tf_op jit(solution)/shard_map/ppermute | solution.py:489
  5.7 4.3 %collective-permute-start.2 = (bf16[2,64,256]{2,1,0:T(8,128)(2,1)}, bf16[2,64,256]{2,1,0:T(8,128)(2,1)S(1)}, u32[]{:S(2)}, u32[]{:S(2)}) collective-permute-start(bf16[2,64,256]{2,1,0:T(8,128)(2,1)} %get-tuple-element.97), channel_id=1, source_target_pairs={{0,3},{1,2},{2,1},{3,0},{4,7},{5,6},{6,5},{7,4},{8,11},{9,10},{10,... | collective-permute-start | bytes 196616 | tf_op jit(solution)/shard_map/ppermute | solution.py:489
  6.0 4.1 %copy-start.6 = (bf16[2,64,256]{2,1,0:T(8,128)(2,1)S(1)}, bf16[2,64,256]{2,1,0:T(8,128)(2,1)}, u32[]{:S(2)}) copy-start(bf16[2,64,256]{2,1,0:T(8,128)(2,1)} %get-tuple-element.94.refs_0_) | copy-start | bytes 196612
  14.9 3.0 %collective-permute-start.3 = (bf16[3328,128]{1,0:T(8,128)(2,1)S(1)}, bf16[3328,128]{1,0:T(8,128)(2,1)S(1)}, u32[]{:S(2)}, u32[]{:S(2)}) collective-permute-start(bf16[3328,128]{1,0:T(8,128)(2,1)S(1)} %get-tuple-element.109), channel_id=1, source_target_pairs={{0,1},{1,0},{2,3},{3,2},{4,5},{5,4},{6,7},{7,6},{8,9},{9,8},{10,11... | collective-permute-start | bytes 2555912 | tf_op jit(solution)/shard_map/ppermute | solution.py:489
  17.4 2.7 %collective-permute-start.7 = (bf16[2400,128]{1,0:T(8,128)(2,1)S(1)}, bf16[2400,128]{1,0:T(8,128)(2,1)S(1)}, u32[]{:S(2)}, u32[]{:S(2)}) collective-permute-start(bf16[2400,128]{1,0:T(8,128)(2,1)S(1)} %get-tuple-element.117), channel_id=1, source_target_pairs={{0,1},{1,0},{2,3},{3,2},{4,5},{5,4},{6,7},{7,6},{8,9},{9,8},{10,11... | collective-permute-start | bytes 1843208 | tf_op jit(solution)/shard_map/ppermute | solution.py:489
  18.0 7.7 %collective-permute-start.11 = (bf16[1024,128]{1,0:T(8,128)(2,1)S(1)}, bf16[1024,128]{1,0:T(8,128)(2,1)S(1)}, u32[]{:S(2)}, u32[]{:S(2)}) collective-permute-start(bf16[1024,128]{1,0:T(8,128)(2,1)S(1)} %get-tuple-element.123), channel_id=1, source_target_pairs={{0,2},{1,5},{2,0},{3,7},{4,6},{5,1},{6,4},{7,3},{8,10},{9,13},{10,... | collective-permute-start | bytes 786440 | tf_op jit(solution)/shard_map/ppermute | solution.py:489
  20.2 7.4 %collective-permute-start.12 = (bf16[1152,128]{1,0:T(8,128)(2,1)S(1)}, bf16[1152,128]{1,0:T(8,128)(2,1)S(1)}, u32[]{:S(2)}, u32[]{:S(2)}) collective-permute-start(bf16[1152,128]{1,0:T(8,128)(2,1)S(1)} %get-tuple-element.124), channel_id=1, source_target_pairs={{0,2},{1,5},{2,0},{3,7},{4,6},{5,1},{6,4},{7,3},{8,10},{9,13},{10,... | collective-permute-start | bytes 884744 | tf_op jit(solution)/shard_map/ppermute | solution.py:489
  21.2 8.1 %collective-permute-start.10 = (bf16[432,128]{1,0:T(8,128)(2,1)S(1)}, bf16[432,128]{1,0:T(8,128)(2,1)S(1)}, u32[]{:S(2)}, u32[]{:S(2)}) collective-permute-start(bf16[432,128]{1,0:T(8,128)(2,1)S(1)} %get-tuple-element.122), channel_id=1, source_target_pairs={{0,24},{1,25},{2,26},{3,27},{4,28},{5,29},{6,30},{7,31},{8,16},{9,... | collective-permute-start | bytes 331784 | tf_op jit(solution)/shard_map/ppermute | solution.py:489
  24.9 6.9 %collective-permute-start.8 = (bf16[432,128]{1,0:T(8,128)(2,1)S(1)}, bf16[432,128]{1,0:T(8,128)(2,1)S(1)}, u32[]{:S(2)}, u32[]{:S(2)}) collective-permute-start(bf16[432,128]{1,0:T(8,128)(2,1)S(1)} %get-tuple-element.120), channel_id=1, source_target_pairs={{0,8},{1,9},{2,10},{3,11},{4,12},{5,13},{6,14},{7,15},{8,0},{9,1},... | collective-permute-start | bytes 331784 | tf_op jit(solution)/shard_map/ppermute | solution.py:489
  24.9 9.7 %collective-permute-start.9 = (bf16[432,128]{1,0:T(8,128)(2,1)S(1)}, bf16[432,128]{1,0:T(8,128)(2,1)S(1)}, u32[]{:S(2)}, u32[]{:S(2)}) collective-permute-start(bf16[432,128]{1,0:T(8,128)(2,1)S(1)} %get-tuple-element.121), channel_id=1, source_target_pairs={{0,16},{1,17},{2,18},{3,19},{4,20},{5,21},{6,22},{7,23},{8,24},{9,... | collective-permute-start | bytes 331784 | tf_op jit(solution)/shard_map/ppermute | solution.py:489
  27.7 6.9 %collective-permute-start.13 = (bf16[1088,128]{1,0:T(8,128)(2,1)S(1)}, bf16[1088,128]{1,0:T(8,128)(2,1)S(1)}, u32[]{:S(2)}, u32[]{:S(2)}) collective-permute-start(bf16[1088,128]{1,0:T(8,128)(2,1)S(1)} %get-tuple-element.126), channel_id=1, source_target_pairs={{0,4},{1,3},{2,6},{3,1},{4,0},{5,7},{6,2},{7,5},{8,12},{9,11},{10,... | collective-permute-start | bytes 835592 | tf_op jit(solution)/shard_map/ppermute | solution.py:489
  34.7 5.8 %collective-permute-start.15 = (bf16[272,128]{1,0:T(8,128)(2,1)S(1)}, bf16[272,128]{1,0:T(8,128)(2,1)S(1)}, u32[]{:S(2)}, u32[]{:S(2)}) collective-permute-start(bf16[272,128]{1,0:T(8,128)(2,1)S(1)} %get-tuple-element.128), channel_id=1, source_target_pairs={{0,8},{1,9},{2,10},{3,11},{4,12},{5,13},{6,14},{7,15},{8,0},{9,1},... | collective-permute-start | bytes 208904 | tf_op jit(solution)/shard_map/ppermute | solution.py:489
  36.1 6.7 %collective-permute-start.16 = (bf16[272,128]{1,0:T(8,128)(2,1)S(1)}, bf16[272,128]{1,0:T(8,128)(2,1)S(1)}, u32[]{:S(2)}, u32[]{:S(2)}) collective-permute-start(bf16[272,128]{1,0:T(8,128)(2,1)S(1)} %get-tuple-element.129), channel_id=1, source_target_pairs={{0,16},{1,17},{2,18},{3,19},{4,20},{5,21},{6,22},{7,23},{8,24},{9,... | collective-permute-start | bytes 208904 | tf_op jit(solution)/shard_map/ppermute | solution.py:489
  38.7 6.1 %collective-permute-start.17 = (bf16[272,128]{1,0:T(8,128)(2,1)S(1)}, bf16[272,128]{1,0:T(8,128)(2,1)S(1)}, u32[]{:S(2)}, u32[]{:S(2)}) collective-permute-start(bf16[272,128]{1,0:T(8,128)(2,1)S(1)} %get-tuple-element.130), channel_id=1, source_target_pairs={{0,24},{1,25},{2,26},{3,27},{4,28},{5,29},{6,30},{7,31},{8,16},{9,... | collective-permute-start | bytes 208904 | tf_op jit(solution)/shard_map/ppermute | solution.py:489
  39.2 7.4 %collective-permute-start.14 = (bf16[432,128]{1,0:T(8,128)(2,1)S(1)}, bf16[432,128]{1,0:T(8,128)(2,1)S(1)}, u32[]{:S(2)}, u32[]{:S(2)}) collective-permute-start(bf16[432,128]{1,0:T(8,128)(2,1)S(1)} %shard_map.334.refs_8_.refs_0_.refs_2_.refs_4_), channel_id=1, source_target_pairs={{0,2},{1,5},{2,0},{3,7},{4,6},{5,1},{6,4},{7,3},{8,10},{9,13},{10,... | collective-permute-start | bytes 331784 | tf_op jit(solution)/shard_map/ppermute | solution.py:489
  40.5 4.3 %collective-permute-start.4 = (bf16[2,64,256]{2,1,0:T(8,128)(2,1)S(1)}, bf16[2,64,256]{2,1,0:T(8,128)(2,1)S(1)}, u32[]{:S(2)}, u32[]{:S(2)}) collective-permute-start(bf16[2,64,256]{2,1,0:T(8,128)(2,1)S(1)} %get-tuple-element.112), channel_id=1, source_target_pairs={{0,1},{1,0},{2,3},{3,2},{4,5},{5,4},{6,7},{7,6},{8,9},{9,8},{10,11... | collective-permute-start | bytes 196616 | tf_op jit(solution)/shard_map/ppermute | solution.py:489
  40.6 8.7 %collective-permute-start.5 = (bf16[2,64,256]{2,1,0:T(8,128)(2,1)S(1)}, bf16[2,64,256]{2,1,0:T(8,128)(2,1)S(1)}, u32[]{:S(2)}, u32[]{:S(2)}) collective-permute-start(bf16[2,64,256]{2,1,0:T(8,128)(2,1)S(1)} %get-tuple-element.113), channel_id=1, source_target_pairs={{0,2},{1,3},{2,0},{3,1},{4,6},{5,7},{6,4},{7,5},{8,10},{9,11},{10,... | collective-permute-start | bytes 196616 | tf_op jit(solution)/shard_map/ppermute | solution.py:489
  42.8 8.1 %collective-permute-start.6 = (bf16[2,64,256]{2,1,0:T(8,128)(2,1)S(1)}, bf16[2,64,256]{2,1,0:T(8,128)(2,1)S(1)}, u32[]{:S(2)}, u32[]{:S(2)}) collective-permute-start(bf16[2,64,256]{2,1,0:T(8,128)(2,1)S(1)} %get-tuple-element.114), channel_id=1, source_target_pairs={{0,3},{1,2},{2,1},{3,0},{4,7},{5,6},{6,5},{7,4},{8,11},{9,10},{10,... | collective-permute-start | bytes 196616 | tf_op jit(solution)/shard_map/ppermute | solution.py:489
  44.8 6.8 %collective-permute-start.19 = (bf16[272,128]{1,0:T(8,128)(2,1)S(1)}, bf16[272,128]{1,0:T(8,128)(2,1)S(1)}, u32[]{:S(2)}, u32[]{:S(2)}) collective-permute-start(bf16[272,128]{1,0:T(8,128)(2,1)S(1)} %shard_map.335.refs_6_.refs_0_), channel_id=1, source_target_pairs={{0,8},{1,9},{2,10},{3,11},{4,12},{5,13},{6,14},{7,15},{8,0},{9,1},... | collective-permute-start | bytes 208904 | tf_op jit(solution)/shard_map/ppermute | solution.py:489
  44.9 8.7 %collective-permute-start.20 = (bf16[272,128]{1,0:T(8,128)(2,1)S(1)}, bf16[272,128]{1,0:T(8,128)(2,1)S(1)}, u32[]{:S(2)}, u32[]{:S(2)}) collective-permute-start(bf16[272,128]{1,0:T(8,128)(2,1)S(1)} %shard_map.335.refs_6_.refs_0_), channel_id=1, source_target_pairs={{0,16},{1,17},{2,18},{3,19},{4,20},{5,21},{6,22},{7,23},{8,24},{9,... | collective-permute-start | bytes 208904 | tf_op jit(solution)/shard_map/ppermute | solution.py:489
  46.6 7.0 %collective-permute-start.21 = (bf16[272,128]{1,0:T(8,128)(2,1)S(1)}, bf16[272,128]{1,0:T(8,128)(2,1)S(1)}, u32[]{:S(2)}, u32[]{:S(2)}) collective-permute-start(bf16[272,128]{1,0:T(8,128)(2,1)S(1)} %shard_map.335.refs_6_.refs_0_), channel_id=1, source_target_pairs={{0,24},{1,25},{2,26},{3,27},{4,28},{5,29},{6,30},{7,31},{8,16},{9,... | collective-permute-start | bytes 208904 | tf_op jit(solution)/shard_map/ppermute | solution.py:489
  49.3 6.0 %collective-permute-start.18 = (bf16[432,128]{1,0:T(8,128)(2,1)S(1)}, bf16[432,128]{1,0:T(8,128)(2,1)S(1)}, u32[]{:S(2)}, u32[]{:S(2)}) collective-permute-start(bf16[432,128]{1,0:T(8,128)(2,1)S(1)} %shard_map.336.refs_4_.refs_0_.refs_2_), channel_id=1, source_target_pairs={{0,4},{1,3},{2,6},{3,1},{4,0},{5,7},{6,2},{7,5},{8,12},{9,11},{10,... | collective-permute-start | bytes 331784 | tf_op jit(solution)/shard_map/ppermute | solution.py:489
  53.6 6.6 %collective-permute-start.22 = (bf16[1088,128]{1,0:T(8,128)(2,1)S(1)}, bf16[1088,128]{1,0:T(8,128)(2,1)S(1)}, u32[]{:S(2)}, u32[]{:S(2)}) collective-permute-start(bf16[1088,128]{1,0:T(8,128)(2,1)S(1)} %shard_map.338.refs_6_.refs_0_), channel_id=1, source_target_pairs={{0,4},{1,3},{2,6},{3,1},{4,0},{5,7},{6,2},{7,5},{8,12},{9,11},{10,... | collective-permute-start | bytes 835592 | tf_op jit(solution)/shard_map/ppermute | solution.py:489
  55.3 8.8 %collective-permute-start.23 = (bf16[336,128]{1,0:T(8,128)(2,1)S(1)}, bf16[336,128]{1,0:T(8,128)(2,1)S(1)}, u32[]{:S(2)}, u32[]{:S(2)}) collective-permute-start(bf16[336,128]{1,0:T(8,128)(2,1)S(1)} %get-tuple-element.135.refs_2_.refs_0_), channel_id=1, source_target_pairs={{0,8},{1,9},{2,10},{3,11},{4,12},{5,13},{6,14},{7,15},{8,0},{9,1},... | collective-permute-start | bytes 258056 | tf_op jit(solution)/shard_map/ppermute | solution.py:489
  56.8 7.3 %collective-permute-start.24 = (bf16[336,128]{1,0:T(8,128)(2,1)S(1)}, bf16[336,128]{1,0:T(8,128)(2,1)S(1)}, u32[]{:S(2)}, u32[]{:S(2)}) collective-permute-start(bf16[336,128]{1,0:T(8,128)(2,1)S(1)} %get-tuple-element.135.refs_2_.refs_0_), channel_id=1, source_target_pairs={{0,16},{1,17},{2,18},{3,19},{4,20},{5,21},{6,22},{7,23},{8,24},{9,... | collective-permute-start | bytes 258056 | tf_op jit(solution)/shard_map/ppermute | solution.py:489
  58.2 6.4 %collective-permute-start.25 = (bf16[336,128]{1,0:T(8,128)(2,1)S(1)}, bf16[336,128]{1,0:T(8,128)(2,1)S(1)}, u32[]{:S(2)}, u32[]{:S(2)}) collective-permute-start(bf16[336,128]{1,0:T(8,128)(2,1)S(1)} %get-tuple-element.135.refs_2_.refs_0_), channel_id=1, source_target_pairs={{0,24},{1,25},{2,26},{3,27},{4,28},{5,29},{6,30},{7,31},{8,16},{9,... | collective-permute-start | bytes 258056 | tf_op jit(solution)/shard_map/ppermute | solution.py:489
  60.3 9.6 %collective-permute-start.27 = (bf16[2176,128]{1,0:T(8,128)(2,1)S(1)}, bf16[2176,128]{1,0:T(8,128)(2,1)S(1)}, u32[]{:S(2)}, u32[]{:S(2)}) collective-permute-start(bf16[2176,128]{1,0:T(8,128)(2,1)S(1)} %shard_map.340.token_in.refs_0_), channel_id=1, source_target_pairs={{0,2},{1,5},{2,0},{3,7},{4,6},{5,1},{6,4},{7,3},{8,10},{9,13},{10,... | collective-permute-start | bytes 1671176 | tf_op jit(solution)/shard_map/ppermute | solution.py:489
  64.7 1.7 %collective-permute-start.26 = (bf16[1344,128]{1,0:T(8,128)(2,1)S(1)}, bf16[1344,128]{1,0:T(8,128)(2,1)S(1)}, u32[]{:S(2)}, u32[]{:S(2)}) collective-permute-start(bf16[1344,128]{1,0:T(8,128)(2,1)S(1)} %shard_map.342.mine_ref.token_ref), channel_id=1, source_target_pairs={{0,1},{1,0},{2,3},{3,2},{4,5},{5,4},{6,7},{7,6},{8,9},{9,8},{10,11... | collective-permute-start | bytes 1032200 | tf_op jit(solution)/shard_map/ppermute | solution.py:489
  70.0 2.1 %collective-permute-start.28 = (bf16[2304,128]{1,0:T(8,128)(2,1)S(1)}, bf16[2304,128]{1,0:T(8,128)(2,1)S(1)}, u32[]{:S(2)}, u32[]{:S(2)}) collective-permute-start(bf16[2304,128]{1,0:T(8,128)(2,1)S(1)} %get-tuple-element.141.first_ref), channel_id=1, source_target_pairs={{0,1},{1,0},{2,3},{3,2},{4,5},{5,4},{6,7},{7,6},{8,9},{9,8},{10,11... | collective-permute-start | bytes 1769480 | tf_op jit(solution)/shard_map/ppermute | solution.py:489
  70.1 3.1 %collective-permute-start.29 = (bf16[2048,128]{1,0:T(8,128)(2,1)S(1)}, bf16[2048,128]{1,0:T(8,128)(2,1)S(1)}, u32[]{:S(2)}, u32[]{:S(2)}) collective-permute-start(bf16[2048,128]{1,0:T(8,128)(2,1)S(1)} %get-tuple-element.142.more_ref), channel_id=1, source_target_pairs={{0,1},{1,0},{2,3},{3,2},{4,5},{5,4},{6,7},{7,6},{8,9},{9,8},{10,11... | collective-permute-start | bytes 1572872 | tf_op jit(solution)/shard_map/ppermute | solution.py:489

commit v2 on v1

--- a/solution.py
+++ b/solution.py
@@ -62,10 +62,14 @@
     return [out[3 * i : 3 * i + 1] + out[3 * i + 1 : 3 * i + 2] + out[3 * i + 2 : 3 * i + 3] for i in range(len(rows))]
 
 
+def over(index, n):
+    return index >> (n.bit_length() - 1) if n & (n - 1) == 0 else index // n
+
+
 def spread_matrix(c):
     per = c // GROUPS
-    a = lax.broadcasted_iota(jnp.int32, (c, c), 0) // per
-    b = lax.broadcasted_iota(jnp.int32, (c, c), 1) // per
+    a = over(lax.broadcasted_iota(jnp.int32, (c, c), 0), per)
+    b = over(lax.broadcasted_iota(jnp.int32, (c, c), 1), per)
     return jnp.where(a == b, 1.0, 0.0).astype(BF16)
 
 
@@ -75,8 +79,8 @@
 
 def norm_stats(v, spread, count):
     m, s = exact_rows([col_sum(v), col_sum(v * v)], spread)
-    m = m / count
-    s = s / count
+    m = m * (1.0 / count)
+    s = s * (1.0 / count)
     return m, lax.rsqrt(s - m * m + EPS)
 
 
@@ -84,21 +88,26 @@
     bias_sum = col_sum(d)
     gain_sum = col_sum(d * hat)
     m1, m2 = exact_rows([bias_sum * gain, gain_sum * gain], spread)
-    return inv * (d * gain - m1 / count - hat * (m2 / count)), gain_sum, bias_sum
+    return d * (gain * inv) - hat * (m2 * inv * (1.0 / count)) - m1 * inv * (1.0 / count), gain_sum, bias_sum
+
+
+def sigmoid(v):
+    return 0.5 * jnp.tanh(0.5 * v) + 0.5
 
 
 def silu(v):
-    return v / (1.0 + jnp.exp(-v))
+    return v * sigmoid(v)
 
 
 def silu_slope(v):
-    s = 1.0 / (1.0 + jnp.exp(-v))
+    s = sigmoid(v)
     return s * (1.0 + v * (1.0 - s))
 
 
 def put_shifted(ref, v, w):
     px, c = v.shape
-    col = lax.broadcasted_iota(jnp.int32, (px, c), 0) % w
+    row = lax.broadcasted_iota(jnp.int32, (px, c), 0)
+    col = row & (w - 1) if w & (w - 1) == 0 else row % w
     edge = jnp.zeros((w, 3 * c), BF16)
     ref[0:w, :] = edge
     ref[w + px : 2 * w + px, :] = edge
@@ -110,6 +119,20 @@
 def conv(ref, weight_ref, px, w):
     k = ref.shape[1]
     return sum(mm(ref[a * w : a * w + px, :], weight_ref[a * k : (a + 1) * k, :]) for a in range(3))
+
+
+def conv_back(ref, weight_ref, px, w):
+    c = weight_ref.shape[1]
+    total = None
+    for a in range(3):
+        for b in range(3):
+            tap = 3 * a + b
+            part = mt(
+                ref[(2 - a) * w : (2 - a) * w + px, (2 - b) * c : (3 - b) * c],
+                weight_ref[tap * c : (tap + 1) * c, :],
+            )
+            total = part if total is None else total + part
+    return total
 
 
 def device():
@@ -139,20 +162,11 @@
 
 
 def sums_rows(total):
-    return 2 * (VEC_ROWS + total)
+    return VEC_ROWS + total
 
 
 def own_rows(total):
     return padded(32, 2 * total)
-
-
-def put_both(keep_ref, send_ref, at, v):
-    n, c = v.shape
-    half = c // 2
-    for i in range(2):
-        part = v[:, i * half : (i + 1) * half].astype(BF16)
-        keep_ref[at + i * n : at + (i + 1) * n, :] = part
-        send_ref[at + i * n : at + (i + 1) * n, :] = part
 
 
 def tap_grad(act_t, ref, tap, px, w):
@@ -167,11 +181,12 @@
 
 def pack_kernel(first_hbm, second_hbm, *refs):
     outs, sems = refs[:-1], refs[-1]
+    count = len(outs) // 2
     copies = []
-    for o, out in enumerate(outs):
-        to = lax.axis_index("seq") ^ o
-        for i, source in enumerate((first_hbm, second_hbm)):
-            copies.append(pltpu.make_async_copy(source.at[to], out.at[i], sems.at[2 * o + i]))
+    for i, source in enumerate((first_hbm, second_hbm)):
+        for o in range(count):
+            at = i * count + o
+            copies.append(pltpu.make_async_copy(source.at[lax.axis_index("seq") ^ o], outs[at], sems.at[at]))
     for copy in copies:
         copy.start()
     for copy in copies:
@@ -187,10 +202,9 @@
         second_ref[at] = part[1]
 
 
-def setup_kernel(steps_ref, table_ref, embed_ref, conv1_ref, conv2_ref, qkv_ref, out_ref, *refs):
-    vec_refs = refs[:10]
-    vec_ref, turned1_ref, turned2_ref, qkv_turned_ref, out_turned_ref = refs[10:]
-    c = out_ref.shape[0]
+def setup_kernel(steps_ref, table_ref, embed_ref, conv1_ref, conv2_ref, *refs):
+    vec_refs, (vec_ref, spread_ref) = refs[:-2], refs[-2:]
+    spread_ref[...] = spread_matrix(spread_ref.shape[0])
     steps = table_ref.shape[0]
     step = steps_ref[lax.axis_index("seq")]
     pick = jnp.where(lax.broadcasted_iota(jnp.int32, (16, steps), 1) == step, 1.0, 0.0).astype(BF16)
@@ -198,78 +212,88 @@
     (projected,) = exact_rows([lifted], embed_ref[...])
     rows = [r[...] for r in vec_refs]
     rows[PROJECTED] = rows[PROJECTED] + projected
-    vec_ref[...] = rows_of(rows, 16, c)
-    for source, turned in ((conv1_ref, turned1_ref), (conv2_ref, turned2_ref)):
-        for tap in range(9):
-            turned[(8 - tap) * c : (9 - tap) * c, :] = source[tap * c : (tap + 1) * c, :].T
-    for i in range(3):
-        qkv_turned_ref[i * c : (i + 1) * c, :] = qkv_ref[:, i * c : (i + 1) * c].T
-    out_turned_ref[...] = out_ref[...].T
-
-
-def main_kernel(w, vec_ref, conv1_ref, conv2_ref, qkv_ref, out_ref, qkv_turned_ref, out_turned_ref, *refs):
-    parts, refs = refs[:-12], refs[-12:]
-    (
-        keep_ref, send_ref, small_ref, output_ref, image_ref, act1_ref, hat2_ref, dh2_ref, q2_ref, stat_ref,
-        cot_ref, p_ref,
-    ) = refs
+    vec_ref[...] = rows_of(rows, 16, vec_ref.shape[1])
+
+
+def gather(parts, ref):
+    for o, part in enumerate(parts):
+        ref[at_rows(lax.axis_index("seq") ^ o, part.shape[0]), :] = part[...]
+
+
+def forward_kernel(w, vec_ref, spread_ref, conv1_ref, conv2_ref, qkv_weight_ref, out_weight_ref, *refs):
+    parts, refs = refs[:-11], refs[-11:]
+    output_ref, image_ref, act1_ref, hat2_ref, act2_ref, hat3_ref, qkv_ref, probs_ref, mixed_ref, stat_ref, p_ref = refs
     px, c = act1_ref.shape
     count = float(px * (c // GROUPS))
-    scale = c ** (-0.5)
-    spread = spread_matrix(c)
+    spread = spread_ref[...]
     vec = lambda i: vec_ref[i : i + 1, :]
-    for o, part in enumerate(parts):
-        rows = at_rows(lax.axis_index("seq") ^ o, part.shape[1])
-        image_ref[rows, :] = part[0]
-        cot_ref[rows, :] = part[1]
-
+    gather(parts, image_ref)
     source = image_ref[...].astype(F32)
     m1, inv1 = norm_stats(source, spread, count)
-    act1 = silu((source - m1) * inv1 * vec(N1_GAIN) + vec(N1_BIAS))
+    act1 = silu((source - m1) * (inv1 * vec(N1_GAIN)) + vec(N1_BIAS))
     act1_ref[...] = act1.astype(BF16)
     put_shifted(p_ref, act1, w)
     hidden1 = conv(p_ref, conv1_ref, px, w) + vec(PROJECTED)
     m2, inv2 = norm_stats(hidden1, spread, count)
     hat2 = (hidden1 - m2) * inv2
     hat2_ref[...] = hat2
-    stat_ref[...] = rows_of([m1, inv1, inv2], 8, c)
     act2 = silu(hat2 * vec(N2_GAIN) + vec(N2_BIAS))
+    act2_ref[...] = act2.astype(BF16)
     put_shifted(p_ref, act2, w)
     hidden2 = image_ref[...].astype(F32) + conv(p_ref, conv2_ref, px, w) + vec(C2_BIAS)
-    act2_t = p_ref[w : w + px, c : 2 * c].T
-
     m3, inv3 = norm_stats(hidden2, spread, count)
+    stat_ref[...] = rows_of([m1, inv1, inv2, inv3], 8, c)
     hat3 = (hidden2 - m3) * inv3
+    hat3_ref[...] = hat3
     normed3 = (hat3 * vec(N3_GAIN) + vec(N3_BIAS)).astype(BF16)
-    qkv = mm(normed3, qkv_ref[...])
+    qkv = mm(normed3, qkv_weight_ref[...])
     q = (qkv[:, :c] + vec(Q_BIAS)).astype(BF16)
     k = qkv[:, c : 2 * c].astype(BF16)
     v = qkv[:, 2 * c :].astype(BF16)
-    scores = mt(q, k) * scale
+    qkv_ref[:, :c] = q
+    qkv_ref[:, c : 2 * c] = k
+    qkv_ref[:, 2 * c :] = v
+    scores = mt(q, k) * c ** (-0.5)
     e = jnp.exp(scores - jnp.max(scores, axis=1, keepdims=True))
-    probs = e / jnp.sum(e, axis=1, keepdims=True)
-    low = probs.astype(BF16)
-    mixed = mm(low, v).astype(BF16)
-    output_ref[...] = (hidden2 + mm(mixed, out_ref[...]) + vec(O_BIAS)).astype(BF16)
-
+    probs = e * (1.0 / jnp.sum(e, axis=1, keepdims=True))
+    probs_ref[...] = probs
+    mixed = mm(probs.astype(BF16), v).astype(BF16)
+    mixed_ref[...] = mixed
+    output_ref[...] = (hidden2 + mm(mixed, out_weight_ref[...]) + vec(O_BIAS)).astype(BF16)
+
+
+def main_kernel(w, vec_ref, spread_ref, qkv_weight_ref, out_weight_ref, act2_ref, hat3_ref, qkv_ref, probs_ref, mixed_ref, stat_ref, *refs):
+    parts, (keep_ref, send_ref, small_ref, dh2_ref, q2_ref, cot_ref) = refs[:-6], refs[-6:]
+    px, c = act2_ref.shape
+    count = float(px * (c // GROUPS))
+    scale = c ** (-0.5)
+    spread = spread_ref[...]
+    vec = lambda i: vec_ref[i : i + 1, :]
+    gather(parts, cot_ref)
     cot = cot_ref[...]
-    put_halves(keep_ref, send_ref, 12 * c, tm(mixed, cot))
     cot_wide = cot.astype(F32)
-    d_mixed = mm(cot, out_turned_ref[...]).astype(BF16)
+    probs = probs_ref[...]
+    q, k, v = qkv_ref[:, :c], qkv_ref[:, c : 2 * c], qkv_ref[:, 2 * c :]
+    put_halves(keep_ref, send_ref, 12 * c, tm(mixed_ref[...], cot))
+    d_mixed = mt(cot, out_weight_ref[...]).astype(BF16)
     d_probs = mt(d_mixed, v)
     inner = jnp.sum(probs * d_probs, axis=1, keepdims=True)
     d_scores = (probs * (d_probs - inner)).astype(BF16)
     d_q = (mm(d_scores, k) * scale).astype(BF16)
     d_k = (tm(d_scores, q) * scale).astype(BF16)
-    d_v = tm(low, d_mixed).astype(BF16)
-    normed3_t = normed3.T
+    d_v = tm(probs.astype(BF16), d_mixed).astype(BF16)
+    hat3 = hat3_ref[...]
+    normed3_t = (hat3 * vec(N3_GAIN) + vec(N3_BIAS)).astype(BF16).T
+    d_normed3 = None
     for i, d in enumerate((d_q, d_k, d_v)):
         put_halves(keep_ref, send_ref, (9 + i) * c, mm(normed3_t, d))
-    d_normed3 = mm(jnp.concatenate([d_q, d_k, d_v], axis=1), qkv_turned_ref[...])
-    d_src3, g_n3g, g_n3b = norm_back(d_normed3, hat3, inv3, vec(N3_GAIN), spread, count)
+        part = mt(d, qkv_weight_ref[:, i * c : (i + 1) * c])
+        d_normed3 = part if d_normed3 is None else d_normed3 + part
+    d_src3, g_n3g, g_n3b = norm_back(d_normed3, hat3, stat_ref[3:4, :], vec(N3_GAIN), spread, count)
     d_hidden2 = cot_wide + d_src3
     dh2_ref[...] = d_hidden2
     put_shifted(q2_ref, d_hidden2, w)
+    act2_t = act2_ref[...].T
     for tap in range(9):
         put_halves(keep_ref, send_ref, tap * c, tap_grad(act2_t, q2_ref, tap, px, w))
     sums = [g_n3g, g_n3b, col_sum(d_q.astype(F32)), col_sum(cot_wide), col_sum(d_hidden2)]
@@ -277,14 +301,14 @@
 
 
 def back_kernel(
-    w, total, steps_ref, vec_ref, turned2_ref, act1_ref, hat2_ref, q2_ref, stat_ref, small_ref, keep_ref, send_ref, q1_ref,
+    w, total, steps_ref, vec_ref, spread_ref, conv2_ref, act1_ref, hat2_ref, q2_ref, stat_ref, small_ref, keep_ref, send_ref, q1_ref,
 ):
     px, c = act1_ref.shape
     count = float(px * (c // GROUPS))
-    spread = spread_matrix(c)
+    spread = spread_ref[...]
     vec = lambda i: vec_ref[i : i + 1, :]
     hat2 = hat2_ref[...]
-    d = conv(q2_ref, turned2_ref, px, w) * silu_slope(hat2 * vec(N2_GAIN) + vec(N2_BIAS))
+    d = conv_back(q2_ref, conv2_ref, px, w) * silu_slope(hat2 * vec(N2_GAIN) + vec(N2_BIAS))
     d_hidden1, g_n2g, g_n2b = norm_back(d, hat2, stat_ref[2:3, :], vec(N2_GAIN), spread, count)
     put_shifted(q1_ref, d_hidden1, w)
     act1_t = act1_ref[...].T
@@ -297,20 +321,20 @@
     rows = [small_ref[i : i + 1, :] for i in range(5)] + [g_n2g, g_n2b] + digits
     own = lax.broadcasted_iota(jnp.int32, (total, c), 0) == device()
     sums = [rows_of(rows, VEC_ROWS, c), jnp.where(own, col_sum(d_hidden1), 0.0)]
-    put_both(keep_ref, send_ref, keep_ref.shape[0] - sums_rows(total), jnp.concatenate(sums, axis=0))
+    put_halves(keep_ref, send_ref, keep_ref.shape[0] - sums_rows(total), jnp.concatenate(sums, axis=0))
 
 
 def source_kernel(
-    w, vec_ref, turned1_ref, image_ref, dh2_ref, q1_ref, stat_ref, output_ref, token_ref, own_ref, *refs
+    w, vec_ref, spread_ref, conv1_ref, image_ref, dh2_ref, q1_ref, stat_ref, output_ref, token_ref, own_ref, *refs
 ):
     parts, grad_ref = refs[:-1], refs[-1]
     px, c = image_ref.shape
     count = float(px * (c // GROUPS))
-    spread = spread_matrix(c)
+    spread = spread_ref[...]
     vec = lambda i: vec_ref[i : i + 1, :]
     inv1 = stat_ref[1:2, :]
     hat1 = (image_ref[...].astype(F32) - stat_ref[0:1, :]) * inv1
-    d = conv(q1_ref, turned1_ref, px, w) * silu_slope(hat1 * vec(N1_GAIN) + vec(N1_BIAS))
+    d = conv_back(q1_ref, conv1_ref, px, w) * silu_slope(hat1 * vec(N1_GAIN) + vec(N1_BIAS))
     d_src1, g_n1g, g_n1b = norm_back(d, hat1, inv1, vec(N1_GAIN), spread, count)
     grad_ref[...] = (dh2_ref[...] + d_src1).astype(BF16)
     for o, part in enumerate(parts):
@@ -383,10 +407,10 @@
         for i, (target, row, col) in enumerate(plan):
             self.half(source, i * c, buffer, i * c, target, row, col + core * (c // 2))
 
-    def first(self, source, core, buffer, at, conv1_hbm):
+    def first(self, source, start, core, buffer, at, conv1_hbm):
         c = conv1_hbm.shape[1]
         for tap in range(9):
-            self.half(source, tap * c, buffer, at + tap * c, conv1_hbm, tap * c, core * (c // 2))
+            self.half(source, start + tap * c, buffer, at + tap * c, conv1_hbm, tap * c, core * (c // 2))
 
     def wait(self):
         for copy in self.copies:
@@ -397,16 +421,17 @@
     return tm(jnp.concatenate(a, axis=0).astype(BF16), jnp.concatenate(b, axis=0).astype(BF16))
 
 
-def table_kernel(total, sums_ref, table_ref, embed_ref, token_in, grad_table_hbm, grad_embed_hbm, *refs):
+def table_kernel(total, sums_ref, got_ref, table_ref, embed_ref, token_in, grad_table_hbm, grad_embed_hbm, *refs):
     vec_refs, token_ref = refs[:8], refs[8]
     grad_table_ref, grad_embed_ref, sems = refs[9:]
     token_ref[...] = jnp.zeros_like(token_ref)
     steps = table_ref.shape[0]
     writer = Writer(sems)
-    n = VEC_ROWS + total
+    left = device() & 1 == 0
 
     def take(row, rows):
-        return sums_ref[row : row + rows, :].astype(F32), sums_ref[n + row : n + row + rows, :].astype(F32)
+        a, b = [ref[row : row + rows, :].astype(F32) for ref in (sums_ref, got_ref)]
+        return jnp.where(left, a, b), jnp.where(left, b, a)
 
     d_proj = jnp.concatenate(take(VEC_ROWS, total), axis=1)
     rows = jnp.concatenate(take(0, VEC_ROWS), axis=1)
@@ -451,25 +476,19 @@
     writer.wait()
 
 
-def middle_kernel(more_ref, first_ref, conv2_in, conv1_hbm, conv2_hbm, qkv_hbm, out_hbm, buffer, sems):
+def write_late(split, late_ref, core, buffer, sems, conv1_hbm, conv2_hbm, qkv_hbm, out_hbm):
     writer = Writer(sems)
-    core = device() & 1
-    writer.more(more_ref, core, buffer, conv2_hbm, qkv_hbm, out_hbm)
-    writer.first(first_ref, core, buffer, (13 - EARLY_TAPS) * out_hbm.shape[0], conv1_hbm)
+    writer.more(late_ref, core, buffer, conv2_hbm, qkv_hbm, out_hbm)
+    writer.first(late_ref, split, core, buffer, (13 - EARLY_TAPS) * out_hbm.shape[0], conv1_hbm)
     writer.wait()
 
 
-def more_kernel(more_ref, conv2_in, qkv_in, out_in, token_ref, conv2_hbm, qkv_hbm, out_hbm, buffer, sems):
-    writer = Writer(sems)
-    writer.more(more_ref, 1 - (device() & 1), buffer, conv2_hbm, qkv_hbm, out_hbm)
-    writer.wait()
-
-
-def first_kernel(first_ref, conv1_in, conv1_hbm, token_ref, buffer, sems):
-    token_ref[...] = jnp.zeros_like(token_ref)
-    writer = Writer(sems)
-    writer.first(first_ref, 1 - (device() & 1), buffer, 0, conv1_hbm)
-    writer.wait()
+def middle_kernel(split, late_ref, conv2_in, conv1_hbm, conv2_hbm, qkv_hbm, out_hbm, buffer, sems):
+    write_late(split, late_ref, device() & 1, buffer, sems, conv1_hbm, conv2_hbm, qkv_hbm, out_hbm)
+
+
+def last_kernel(split, late_ref, conv1_in, conv2_in, qkv_in, out_in, conv1_hbm, conv2_hbm, qkv_hbm, out_hbm, buffer, sems):
+    write_late(split, late_ref, 1 - (device() & 1), buffer, sems, conv1_hbm, conv2_hbm, qkv_hbm, out_hbm)
 
 
 def call(kernel, outs, specs, out_specs=None, scratch=(), limit=40, cost=1, aliases={}):
@@ -566,38 +585,41 @@
     def trade(parts):
         return [parts[0]] + [permute(p, lambda i, o=o + 1: i ^ o, total) for o, p in enumerate(parts[1:])]
 
-    pieces = trade(
-        call(pack_kernel, [pair] * seq, [HBM] * 2, None, [pltpu.SemaphoreType.DMA((2 * seq,))], 54, EARLY_COST)(
-            images.reshape(block), cotangent.reshape(block)
-        )
+    pieces = call(pack_kernel, [shape(block[1:], BF16)] * (2 * seq), [HBM] * 2, None, [pltpu.SemaphoreType.DMA((2 * seq,))], 54, EARLY_COST)(
+        images.reshape(block), cotangent.reshape(block)
     )
+    images_here, cots_here = trade(pieces[:seq]), trade(pieces[seq:])
     vectors = [norm1_gain, norm1_bias, norm2_gain, norm2_bias, conv2_bias, norm3_gain, norm3_bias, query_bias, out_bias, embed_bias]
-    vec, turned1, turned2, qkv_turned, out_turned = call(
-        setup_kernel,
-        [shape((16, c), F32)] + [shape((n, c), BF16) for n in (9 * c, 9 * c, 3 * c, c)],
-        [SMEM] + [VMEM] * 16,
-        cost=EARLY_COST,
-    )(timesteps, step_table, embed_weight, conv1, conv2, qkv_weight, out_weight, *[v.reshape(1, c) for v in vectors])
+    vec, spread = call(setup_kernel, [shape((16, c), F32), shape((c, c), BF16)], [SMEM] + [VMEM] * 2 + [ANY] * 2 + [VMEM] * 10, cost=EARLY_COST)(
+        timesteps, step_table, embed_weight, conv1, conv2, *[v.reshape(1, c) for v in vectors]
+    )
     half = lambda n: shape((n, c // 2), BF16)
-    keep_e, send_e, small, output, image, act1, hat2, d_hidden2, q2, stats = call(
+    output, image, act1, hat2, *kept, stats = call(
+        functools.partial(forward_kernel, w),
+        [field(BF16), field(BF16), field(BF16), field(F32), field(BF16), field(F32), shape((px, 3 * c), BF16), field(F32), field(BF16)]
+        + [shape((8, c), F32)],
+        [VMEM] * (6 + seq),
+        None,
+        [pltpu.VMEM(shifted, BF16)],
+    )(vec, spread, conv1, conv2, qkv_weight, out_weight, *images_here)
+    keep_e, send_e, small, d_hidden2, q2 = call(
         functools.partial(main_kernel, w),
-        [half(rows_a + rows_m)] * 2
-        + [shape((8, c), F32), field(BF16), field(BF16), field(BF16), field(F32), field(F32), shape(shifted, BF16), shape((8, c), F32)],
-        [VMEM] * (7 + seq),
+        [half(rows_a + rows_m)] * 2 + [shape((8, c), F32), field(F32), shape(shifted, BF16)],
+        [VMEM] * (10 + seq),
         None,
-        [pltpu.VMEM((px, c), BF16), pltpu.VMEM(shifted, BF16)],
-    )(vec, conv1, conv2, qkv_weight, out_weight, qkv_turned, out_turned, *pieces)
+        [pltpu.VMEM((px, c), BF16)],
+    )(vec, spread, qkv_weight, out_weight, *kept, stats, *cots_here)
     swap = lambda array: permute(array, lambda i: i ^ 1, total)
     got_e = swap(send_e)
     keep_1, send_1, q1 = call(
-        functools.partial(back_kernel, w, total), [half(rows_1 + rows_v)] * 2 + [shape(shifted, BF16)], [SMEM] + [VMEM] * 7
-    )(timesteps, vec, turned2, act1, hat2, q2, stats, small)
+        functools.partial(back_kernel, w, total), [half(rows_1 + rows_v)] * 2 + [shape(shifted, BF16)], [SMEM] + [VMEM] * 8
+    )(timesteps, vec, spread, conv2, act1, hat2, q2, stats, small)
     got_1 = swap(send_1)
     m = Chain(total, [([keep_e, got_e], rows_a, rows_m, False)])
     token = m.add(near[0], q1)
     own, *results = call(
-        functools.partial(source_kernel, w), [half(rows_o)] + [pair] * seq, [VMEM] * 7 + [ANY], None, [pltpu.VMEM((px, c), BF16)]
-    )(vec, turned1, image, d_hidden2, q1, stats, output, token)
+        functools.partial(source_kernel, w), [half(rows_o)] + [pair] * seq, [VMEM] * 8 + [ANY], None, [pltpu.VMEM((px, c), BF16)]
+    )(vec, spread, conv1, image, d_hidden2, q1, stats, output, token)
     results = trade(results)
     f = Chain(total, [([keep_1, got_1], 0, rows_1, False)])
     a = Chain(total, [([keep_e, got_e], 0, rows_a, False), ([own], 0, rows_o, False), ([keep_1, got_1], rows_1, rows_v, True)])
@@ -634,10 +656,10 @@
     grad_table, grad_embed, *vecs, token = call(
         functools.partial(table_kernel, total),
         outs + [shape((1, c), F32)] * 8 + [tiny],
-        [VMEM] * 3 + [ANY],
+        [VMEM] * 4 + [ANY],
         [HBM] * 2 + [VMEM] * 9,
         [pltpu.VMEM(o.shape, F32) for o in outs] + [pltpu.SemaphoreType.DMA((1 + -(-step_table.shape[0] // 256),))],
-    )(sums, step_table, embed_weight, token)
+    )(sums, swap(sums), step_table, embed_weight, token)
     for i in range(len(far))[::-1]:
         token = a.join(far[i], token, LONG_COST, sizes_a(far_cuts[i]))
         a.spread(far[i - 1] if i else core)
@@ -649,15 +671,16 @@
         [HBM] + [VMEM] * 3,
         [pltpu.VMEM((EARLY_TAPS * c, c), F32), pltpu.SemaphoreType.DMA((EARLY_TAPS,))],
     )(*a.parts, token)
-    more, first = b.join(near[0], token, 1, [[rows_m], [rows_1]], True)
-    got_more, got_first = swap(more), swap(first)
+    late = b.join(near[0], token, 1, sizes_b(1))
+    got_late = swap(late)
     scratch = lambda blocks: [pltpu.VMEM((blocks * c, c // 2), F32), pltpu.SemaphoreType.DMA((blocks,))]
     count = 13 - EARLY_TAPS
-    grad_conv1, *others = call(middle_kernel, grads, [VMEM] * 2 + [HBM], [HBM] * 4, scratch(count + 9), aliases={2: 1})(more, first, grad_conv2)
-    grad_conv1, token = call(first_kernel, grads[:1] + [tiny], [VMEM, HBM], [HBM, VMEM], scratch(9), aliases={1: 0})(got_first, grad_conv1)
-    grad_conv2, grad_qkv, grad_out = call(
-        more_kernel, grads[1:], [VMEM] + [HBM] * 3 + [ANY], [HBM] * 3, scratch(count), aliases={1: 0, 2: 1, 3: 2}
-    )(got_more, *others, token)
+    grads_half = call(
+        functools.partial(middle_kernel, rows_m), grads, [VMEM] + [HBM], [HBM] * 4, scratch(count + 9), aliases={1: 1}
+    )(late, grad_conv2)
+    grad_conv1, grad_conv2, grad_qkv, grad_out = call(
+        functools.partial(last_kernel, rows_m), grads, [VMEM] + [HBM] * 4, [HBM] * 4, scratch(count + 9), aliases={1: 0, 2: 1, 3: 2, 4: 3}
+    )(got_late, *grads_half)
     one = lambda r: vecs[r].reshape(c)
     return (
         output.reshape(images.shape), grad_images.reshape(images.shape), grad_table, grad_norm1_gain.reshape(c), grad_norm1_bias.reshape(c),

time: 74.4 us -> 73.8 us (level)
  starting transfers between devices: 32.3 us -> 33.9 us
  waiting for transfers between devices: 19.8 us -> 18.6 us
  Pallas kernels: 20.9 us -> 19.9 us
    pallas_call x1, Pallas kernels: 4.76 us -> 1.82 us  [shards(): call(functools.partial(main_kernel, w), [half(rows_a + rows_m)] * 2 + [sh...]
    pallas_call x5, Pallas kernels: 6.78 us -> 8.75 us  [the longest x1 2.97 us: shards(): call(functools.partial(forward_kernel, w), [field(BF16), field(BF16), fie...]
    ppermute x30 -> x33, starting transfers between devices: 32.3 us -> 33.9 us  [permute(): return lax.ppermute(array, AXES, [(i, partner(i)) for i in range(total)])]
    ppermute x30 -> x33, waiting for transfers between devices: 19.8 us -> 18.6 us  [permute(): return lax.ppermute(array, AXES, [(i, partner(i)) for i in range(total)])]
  transfers between devices with their start and end apart: 30 -> 33, of which waited for: 12 -> 13; matrix products, arithmetic and copies ran while one was open for 0% -> 0% of each run, Pallas kernels for 18% -> 20%
where the time goes in v2:
time: 73.8 us; the launch traced here: 73.7 us
  starting transfers between devices  33.9 us (46%)
  Pallas kernels  19.9 us (27%)
  waiting for transfers between devices  18.6 us (25%)
  between operations  1.16 us (2%)
    ppermute x33, starting transfers between devices, permute(): return lax.ppermute(array, AXES, [(i, partner(i)) for i in range(total)])  33.9 us
    ppermute x33, waiting for transfers between devices, permute(): return lax.ppermute(array, AXES, [(i, partner(i)) for i in range(total)])  18.6 us
    pallas_call x1, Pallas kernels, shards(): call(functools.partial(forward_kernel, w), [field(BF16), field(BF16), fie...  2.97 us
    pallas_call x1, Pallas kernels, shards(): call(functools.partial(table_kernel, total), outs + [shape((1, c), F32)]...  2.8 us
    pallas_call x1, Pallas kernels, shards(): call(functools.partial(back_kernel, w, total), [half(rows_1 + rows_v)] *...  2.38 us
    pallas_call x1, Pallas kernels, shards(): call(functools.partial(main_kernel, w), [half(rows_a + rows_m)] * 2 + [sh...  1.82 us
    pallas_call x1, Pallas kernels, shards(): call(pack_kernel, [shape(block[1:], BF16)] * (2 * seq), [HBM] * 2, None,...  1.79 us
    pallas_call x1, Pallas kernels, shards(): call(functools.partial(early_kernel, rows_o), grads[:1] + [shape((1, c),...  1.69 us
  transfers between devices with their start and end apart: 33, of which 13 were waited for; matrix products, arithmetic and copies ran while one was open for 0% of the time, Pallas kernels for 20%

profile of v2, /device:TPU:0, one launch (start us, length us, event | category | flops | bytes accessed | tf_op | source)
XLA Modules:
  0.0 73.7 jit_solution(17697103212522049448)
XLA Ops:
  0.8 1.8 %shard_map.323 = (bf16[64,256]{1,0:T(8,128)(2,1)}, bf16[64,256]{1,0:T(8,128)(2,1)}, bf16[64,256]{1,0:T(8,128)(2,1)}, bf16[64,256]{1,0:T(8,128)(2,1)}, bf16[64,25...) custom-call(bf16[4,64,256]{2,1,0:T(8,128)(2,1)} %bitcast.46, ...), custom_call_target="tpu_custom_call" | custom-call | flops 20000000000 | bytes 1 | tf_op jit(solution)/shard_map/pallas_call | solution.py:588
  2.6 0.5 collective-permute-start
  3.1 2.6 %collective-permute-start.1 = (bf16[64,256]{1,0:T(8,128)(2,1)}, bf16[64,256]{1,0:T(8,128)(2,1)S(1)}, u32[]{:S(2)}, u32[]{:S(2)}) collective-permute-start(bf16[64,256]{1,0:T(8,128)(2,1)} %get-tuple-element.97), channel_id=1, source_target_pairs={{0,2},{1,3},{2,0},{3,1},{4,6},{5,7},{6,4},{7,5},{8,10},{9,11},{10,... | collective-permute-start | bytes 98312 | tf_op jit(solution)/shard_map/ppermute | solution.py:508
  5.7 0.1 collective-permute-start.2
  5.8 0.1 collective-permute-start.3
  5.9 1.9 %collective-permute-start.4 = (bf16[64,256]{1,0:T(8,128)(2,1)}, bf16[64,256]{1,0:T(8,128)(2,1)S(1)}, u32[]{:S(2)}, u32[]{:S(2)}) collective-permute-start(bf16[64,256]{1,0:T(8,128)(2,1)} %get-tuple-element.108), channel_id=1, source_target_pairs={{0,2},{1,3},{2,0},{3,1},{4,6},{5,7},{6,4},{7,5},{8,10},{9,11},{10,... | collective-permute-start | bytes 98312 | tf_op jit(solution)/shard_map/ppermute | solution.py:508
  7.9 0.0 collective-permute-done.refs_1_
  8.0 0.0 copy-start.2
  8.0 0.0 copy-start.4
  8.0 0.0 copy-start.7
  8.1 1.0 %shard_map.322 = (f32[16,256]{1,0:T(8,128)S(1)}, bf16[256,256]{1,0:T(8,128)(2,1)S(1)}) custom-call(s32[4]{0:T(128)S(1)} %copy-done.8, bf16[1000,512]{1,0:T(8,128)(2,1)S(1)} %copy-done.3, bf16[512,256]{1,0:T(8,128)(2,1)S(1)} %copy-done.5, bf16[2304,256]{1,0:T(8,128)(2,1)S(1)} %bitcast.28, bf16[2304,256]{1,0:T(8,128)(2,1)S(1)} %bitcast.31, ...), custom_call_target="tpu_custom_call" | custom-call | flops 20000000000 | bytes 1 | tf_op jit(solution)/shard_map/pallas_call | solution.py:593
  9.0 0.2 collective-permute-done.2.refs_3_
  9.3 3.0 %shard_map.324 = (bf16[256,256]{1,0:T(8,128)(2,1)S(1)}, bf16[256,256]{1,0:T(8,128)(2,1)S(1)}, bf16[256,256]{1,0:T(8,128)(2,1)S(1)}, f32[256,256]{1,0:T(8,128)S(1...) custom-call(f32[16,256]{1,0:T(8,128)S(1)} %get-tuple-element.93.vec_, ...), custom_call_target="tpu_custom_call" | custom-call | flops 1 | bytes 1 | tf_op jit(solution)/shard_map/pallas_call | solution.py:597
  12.3 0.0 collective-permute-done.3.refs_1_
  12.3 1.8 %shard_map.325 = (bf16[3328,128]{1,0:T(8,128)(2,1)S(1)}, bf16[3328,128]{1,0:T(8,128)(2,1)S(1)}, f32[8,256]{1,0:T(8,128)S(1)}, f32[256,256]{1,0:T(8,128)S(1)}, bf16[288,768]{1,0:T(8,128)(2,1)S(1)}) custom-call(f32[16,256]{1,0:T(8,128)S(1)} %get-tuple-element.93.vec_ref, bf16[256,256]{1,0:T(8,128)(2,1)S(1)} %get-tuple-element.94.spread_ref, ...), custom_call_target="tpu_custom_call" | custom-call | flops 1 | bytes 1 | tf_op jit(solution)/shard_map/pallas_call | solution.py:605
  14.1 0.5 collective-permute-start.6
  14.6 2.4 %shard_map.326 = (bf16[2352,128]{1,0:T(8,128)(2,1)S(1)}, bf16[2352,128]{1,0:T(8,128)(2,1)S(1)}, bf16[288,768]{1,0:T(8,128)(2,1)S(1)}) custom-call(s32[4]{0:T(128)S(1)} %copy-done.8, f32[16,256]{1,0:T(8,128)S(1)} %get-tuple-element.93.vec_ref, bf16[256,256]{1,0:T(8,128)(2,1)S(1)} %get-tuple-element.94.spread_ref, bf16[2304,256]{1,0:T(8,128)(2,1)S(1)} %bitcast.33, ...), custom_call_target="tpu_custom_call" | custom-call | flops 1 | bytes 1 | tf_op jit(solution)/shard_map/pallas_call | solution.py:614
  17.0 0.2 collective-permute-start.10
  17.2 0.1 shard_map.327
  17.3 1.5 %collective-permute-start.14 = (bf16[1024,128]{1,0:T(8,128)(2,1)S(1)}, bf16[1024,128]{1,0:T(8,128)(2,1)S(1)}, u32[]{:S(2)}, u32[]{:S(2)}) collective-permute-start(bf16[1024,128]{1,0:T(8,128)(2,1)S(1)} %get-tuple-element.132), channel_id=1, source_target_pairs={{0,2},{1,5},{2,0},{3,7},{4,6},{5,1},{6,4},{7,3},{8,10},{9,13},{10,... | collective-permute-start | bytes 786440 | tf_op jit(solution)/shard_map/ppermute | solution.py:508
  18.8 0.8 %shard_map.328 = (bf16[64,128]{1,0:T(8,128)(2,1)S(1)}, bf16[2,64,256]{2,1,0:T(8,128)(2,1)S(1)}, bf16[2,64,256]{2,1,0:T(8,128)(2,1)S(1)}, bf16[2,64,256]{2,1,0:T(8,128)(2,1)S(1)}, bf16[2,64,256]{2,1,0:T(8,128)(2,1)S(1)}) custom-call(f32[16,256]{1,0:T(8,128)S(1)} %get-tuple-element.93.vec_ref, bf16[256,256]{1,0:T(8,128)(2,1)S(1)} %get-tuple-element.94.spread_ref, ...), custom_call_target="tpu_custom_call" | custom-call | flops 1 | bytes 1 | tf_op jit(solution)/shard_map/pallas_call | solution.py:620
  19.6 0.2 shard_map.329
  19.7 1.1 %collective-permute-start.15 = (bf16[1152,128]{1,0:T(8,128)(2,1)S(1)}, bf16[1152,128]{1,0:T(8,128)(2,1)S(1)}, u32[]{:S(2)}, u32[]{:S(2)}) collective-permute-start(bf16[1152,128]{1,0:T(8,128)(2,1)S(1)} %get-tuple-element.133), channel_id=1, source_target_pairs={{0,2},{1,5},{2,0},{3,7},{4,6},{5,1},{6,4},{7,3},{8,10},{9,13},{10,... | collective-permute-start | bytes 884744 | tf_op jit(solution)/shard_map/ppermute | solution.py:508
  20.8 0.1 shard_map.330
  20.9 1.6 %collective-permute-start.11 = (bf16[384,128]{1,0:T(8,128)(2,1)S(1)}, bf16[384,128]{1,0:T(8,128)(2,1)S(1)}, u32[]{:S(2)}, u32[]{:S(2)}) collective-permute-start(bf16[384,128]{1,0:T(8,128)(2,1)S(1)} %get-tuple-element.129), channel_id=1, source_target_pairs={{0,8},{1,9},{2,10},{3,11},{4,12},{5,13},{6,14},{7,15},{8,0},{9,1},... | collective-permute-start | bytes 294920 | tf_op jit(solution)/shard_map/ppermute | solution.py:508
  22.5 2.6 %collective-permute-start.12 = (bf16[384,128]{1,0:T(8,128)(2,1)S(1)}, bf16[384,128]{1,0:T(8,128)(2,1)S(1)}, u32[]{:S(2)}, u32[]{:S(2)}) collective-permute-start(bf16[384,128]{1,0:T(8,128)(2,1)S(1)} %get-tuple-element.130), channel_id=1, source_target_pairs={{0,16},{1,17},{2,18},{3,19},{4,20},{5,21},{6,22},{7,23},{8,24},{9,... | collective-permute-start | bytes 294920 | tf_op jit(solution)/shard_map/ppermute | solution.py:508
  25.1 0.2 collective-permute-start.13
  25.3 0.1 shard_map.331.refs_0_.refs_3_
  25.4 1.5 %collective-permute-done.15.refs_2_ = bf16[1152,128]{1,0:T(8,128)(2,1)S(1)} collective-permute-done((bf16[1152,128]{1,0:T(8,128)(2,1)S(1)}, bf16[1152,128]{1,0:T(8,128)(2,1)S(1)}, u32[]{:S(2)}, u32[]{:S(2)}) %collective-permute-start.15) | collective-permute-done | bytes 294944 | tf_op jit(solution)/shard_map/ppermute | solution.py:508
  26.9 0.1 shard_map.332
  27.0 1.6 %collective-permute-start.16 = (bf16[1088,128]{1,0:T(8,128)(2,1)S(1)}, bf16[1088,128]{1,0:T(8,128)(2,1)S(1)}, u32[]{:S(2)}, u32[]{:S(2)}) collective-permute-start(bf16[1088,128]{1,0:T(8,128)(2,1)S(1)} %get-tuple-element.135), channel_id=1, source_target_pairs={{0,4},{1,3},{2,6},{3,1},{4,0},{5,7},{6,2},{7,5},{8,12},{9,11},{10,... | collective-permute-start | bytes 835592 | tf_op jit(solution)/shard_map/ppermute | solution.py:508
  28.6 4.5 %collective-permute-done.12.refs_2_.refs_6_.refs_10_ = bf16[384,128]{1,0:T(8,128)(2,1)S(1)} collective-permute-done((bf16[384,128]{1,0:T(8,128)(2,1)S(1)}, bf16[384,128]{1,0:T(8,128)(2,1)S(1)}, u32[]{:S(2)}, u32[]{:S(2)}) %collective-permute-start.12) | collective-permute-done | bytes 98336 | tf_op jit(solution)/shard_map/ppermute | solution.py:508
  33.0 0.1 shard_map.333.refs_4_.refs_0_.refs_1_.refs_2_
  33.1 0.5 collective-permute-done.16.refs_1_.refs_3_
  33.6 0.1 shard_map.334
  33.7 1.6 %collective-permute-start.18 = (bf16[272,128]{1,0:T(8,128)(2,1)S(1)}, bf16[272,128]{1,0:T(8,128)(2,1)S(1)}, u32[]{:S(2)}, u32[]{:S(2)}) collective-permute-start(bf16[272,128]{1,0:T(8,128)(2,1)S(1)} %get-tuple-element.137), channel_id=1, source_target_pairs={{0,8},{1,9},{2,10},{3,11},{4,12},{5,13},{6,14},{7,15},{8,0},{9,1},... | collective-permute-start | bytes 208904 | tf_op jit(solution)/shard_map/ppermute | solution.py:508
  35.3 2.6 %collective-permute-start.19 = (bf16[272,128]{1,0:T(8,128)(2,1)S(1)}, bf16[272,128]{1,0:T(8,128)(2,1)S(1)}, u32[]{:S(2)}, u32[]{:S(2)}) collective-permute-start(bf16[272,128]{1,0:T(8,128)(2,1)S(1)} %get-tuple-element.138), channel_id=1, source_target_pairs={{0,16},{1,17},{2,18},{3,19},{4,20},{5,21},{6,22},{7,23},{8,24},{9,... | collective-permute-start | bytes 208904 | tf_op jit(solution)/shard_map/ppermute | solution.py:508
  37.9 0.2 collective-permute-start.20
  38.2 1.5 %collective-permute-start.17 = (bf16[384,128]{1,0:T(8,128)(2,1)S(1)}, bf16[384,128]{1,0:T(8,128)(2,1)S(1)}, u32[]{:S(2)}, u32[]{:S(2)}) collective-permute-start(bf16[384,128]{1,0:T(8,128)(2,1)S(1)} %shard_map.335.refs_8_.refs_0_.refs_2_.refs_4_), channel_id=1, source_target_pairs={{0,2},{1,5},{2,0},{3,7},{4,6},{5,1},{6,4},{7,3},{8,10},{9,13},{10,... | collective-permute-start | bytes 294920 | tf_op jit(solution)/shard_map/ppermute | solution.py:508
  39.7 0.6 collective-permute-start.8
  40.3 1.8 %collective-permute-done.19.refs_2_.refs_6_ = bf16[272,128]{1,0:T(8,128)(2,1)S(1)} collective-permute-done((bf16[272,128]{1,0:T(8,128)(2,1)S(1)}, bf16[272,128]{1,0:T(8,128)(2,1)S(1)}, u32[]{:S(2)}, u32[]{:S(2)}) %collective-permute-start.19) | collective-permute-done | bytes 69664 | tf_op jit(solution)/shard_map/ppermute | solution.py:508
  42.0 2.0 %collective-permute-done.20.refs_3_.refs_7_ = bf16[272,128]{1,0:T(8,128)(2,1)S(1)} collective-permute-done((bf16[272,128]{1,0:T(8,128)(2,1)S(1)}, bf16[272,128]{1,0:T(8,128)(2,1)S(1)}, u32[]{:S(2)}, u32[]{:S(2)}) %collective-permute-start.20) | collective-permute-done | bytes 69664 | tf_op jit(solution)/shard_map/ppermute | solution.py:508
  44.1 1.2 %collective-permute-start.24 = (bf16[272,128]{1,0:T(8,128)(2,1)S(1)}, bf16[272,128]{1,0:T(8,128)(2,1)S(1)}, u32[]{:S(2)}, u32[]{:S(2)}) collective-permute-start(bf16[272,128]{1,0:T(8,128)(2,1)S(1)} %shard_map.336.refs_6_.refs_0_), channel_id=1, source_target_pairs={{0,24},{1,25},{2,26},{3,27},{4,28},{5,29},{6,30},{7,31},{8,16},{9,... | collective-permute-start | bytes 208904 | tf_op jit(solution)/shard_map/ppermute | solution.py:508
  45.3 3.2 %collective-permute-start.22 = (bf16[272,128]{1,0:T(8,128)(2,1)S(1)}, bf16[272,128]{1,0:T(8,128)(2,1)S(1)}, u32[]{:S(2)}, u32[]{:S(2)}) collective-permute-start(bf16[272,128]{1,0:T(8,128)(2,1)S(1)} %shard_map.336.refs_6_.refs_0_), channel_id=1, source_target_pairs={{0,8},{1,9},{2,10},{3,11},{4,12},{5,13},{6,14},{7,15},{8,0},{9,1},... | collective-permute-start | bytes 208904 | tf_op jit(solution)/shard_map/ppermute | solution.py:508
  48.6 1.5 %collective-permute-start.21 = (bf16[384,128]{1,0:T(8,128)(2,1)S(1)}, bf16[384,128]{1,0:T(8,128)(2,1)S(1)}, u32[]{:S(2)}, u32[]{:S(2)}) collective-permute-start(bf16[384,128]{1,0:T(8,128)(2,1)S(1)} %shard_map.337.refs_4_.refs_0_.refs_2_), channel_id=1, source_target_pairs={{0,4},{1,3},{2,6},{3,1},{4,0},{5,7},{6,2},{7,5},{8,12},{9,11},{10,... | collective-permute-start | bytes 294920 | tf_op jit(solution)/shard_map/ppermute | solution.py:508
  50.1 0.7 shard_map.338
  50.9 1.7 %collective-permute-done.23.refs_2_ = bf16[272,128]{1,0:T(8,128)(2,1)S(1)} collective-permute-done((bf16[272,128]{1,0:T(8,128)(2,1)S(1)}, bf16[272,128]{1,0:T(8,128)(2,1)S(1)}, u32[]{:S(2)}, u32[]{:S(2)}) %collective-permute-start.23) | collective-permute-done | bytes 69664 | tf_op jit(solution)/shard_map/ppermute | solution.py:508
  52.6 0.4 collective-permute-done.22.refs_1_
  53.0 1.6 %collective-permute-start.26 = (bf16[1088,128]{1,0:T(8,128)(2,1)S(1)}, bf16[1088,128]{1,0:T(8,128)(2,1)S(1)}, u32[]{:S(2)}, u32[]{:S(2)}) collective-permute-start(bf16[1088,128]{1,0:T(8,128)(2,1)S(1)} %shard_map.339.refs_6_.refs_0_), channel_id=1, source_target_pairs={{0,4},{1,3},{2,6},{3,1},{4,0},{5,7},{6,2},{7,5},{8,12},{9,11},{10,... | collective-permute-start | bytes 835592 | tf_op jit(solution)/shard_map/ppermute | solution.py:508
  54.6 2.2 %collective-permute-start.29 = (bf16[336,128]{1,0:T(8,128)(2,1)S(1)}, bf16[336,128]{1,0:T(8,128)(2,1)S(1)}, u32[]{:S(2)}, u32[]{:S(2)}) collective-permute-start(bf16[336,128]{1,0:T(8,128)(2,1)S(1)} %get-tuple-element.144.refs_2_.refs_0_), channel_id=1, source_target_pairs={{0,24},{1,25},{2,26},{3,27},{4,28},{5,29},{6,30},{7,31},{8,16},{9,... | collective-permute-start | bytes 258056 | tf_op jit(solution)/shard_map/ppermute | solution.py:508
  56.8 2.2 %collective-permute-start.27 = (bf16[336,128]{1,0:T(8,128)(2,1)S(1)}, bf16[336,128]{1,0:T(8,128)(2,1)S(1)}, u32[]{:S(2)}, u32[]{:S(2)}) collective-permute-start(bf16[336,128]{1,0:T(8,128)(2,1)S(1)} %get-tuple-element.144.refs_2_.refs_0_), channel_id=1, source_target_pairs={{0,8},{1,9},{2,10},{3,11},{4,12},{5,13},{6,14},{7,15},{8,0},{9,1},... | collective-permute-start | bytes 258056 | tf_op jit(solution)/shard_map/ppermute | solution.py:508
  59.1 0.6 collective-permute-done.26.refs_1_
  59.7 0.7 %collective-permute-start.31 = (bf16[2176,128]{1,0:T(8,128)(2,1)S(1)}, bf16[2176,128]{1,0:T(8,128)(2,1)S(1)}, u32[]{:S(2)}, u32[]{:S(2)}) collective-permute-start(bf16[2176,128]{1,0:T(8,128)(2,1)S(1)} %shard_map.341.token_in.refs_0_), channel_id=1, source_target_pairs={{0,2},{1,5},{2,0},{3,7},{4,6},{5,1},{6,4},{7,3},{8,10},{9,13},{10,... | collective-permute-start | bytes 1671176 | tf_op jit(solution)/shard_map/ppermute | solution.py:508
  60.4 2.8 %shard_map.342 = (f32[1000,512]{1,0:T(8,128)}, f32[512,256]{1,0:T(8,128)}, f32[1,256]{1,0:T(1,128)}, f32[1,256]{1,0:T(1,128)}, f32[1,256]{1,0:T(1,128)}, /*index...) custom-call(bf16[48,128]{1,0:T(8,128)(2,1)S(1)} %get-tuple-element.1, ...), custom_call_target="tpu_custom_call" | custom-call | flops 1 | bytes 1 | tf_op jit(solution)/shard_map/pallas_call | solution.py:656
  63.2 1.0 %collective-permute-done.28.refs_2_ = bf16[336,128]{1,0:T(8,128)(2,1)S(1)} collective-permute-done((bf16[336,128]{1,0:T(8,128)(2,1)S(1)}, bf16[336,128]{1,0:T(8,128)(2,1)S(1)}, u32[]{:S(2)}, u32[]{:S(2)}) %collective-permute-start.28) | collective-permute-done | bytes 86048 | tf_op jit(solution)/shard_map/ppermute | solution.py:508
  64.2 0.1 collective-permute-start.30
  64.3 1.6 %collective-permute-done.30.got_ref = bf16[1344,128]{1,0:T(8,128)(2,1)S(1)} collective-permute-done((bf16[1344,128]{1,0:T(8,128)(2,1)S(1)}, bf16[1344,128]{1,0:T(8,128)(2,1)S(1)}, u32[]{:S(2)}, u32[]{:S(2)}) %collective-permute-start.30) | collective-permute-done | bytes 344096 | tf_op jit(solution)/shard_map/ppermute | solution.py:508
  66.0 1.7 %shard_map.344 = (f32[2304,256]{1,0:T(8,128)}, f32[1,256]{1,0:T(1,128)}, f32[1,256]{1,0:T(1,128)}, f32[8,128]{1,0:T(8,128)S(1)}) custom-call(bf16[1344,128]{1,0:T(8,128)(2,1)S(1)} %shard_map.343.mine_ref.token_ref, bf16[1344,128]{1,0:T(8,128)(2,1)S(1)} %collective-permute-done.30.got_ref, bf16[1344,128]{1,0:T(8,128)(2,1)S(1)} %shard_map.343.mine_ref.token_ref), custom_call_target="tpu_custom_call" | custom-call | flops 1 | bytes 1 | tf_op jit(solution)/shard_map/pallas_call | solution.py:667
  67.7 1.6 %collective-permute-done.31.refs_1_ = bf16[2176,128]{1,0:T(8,128)(2,1)S(1)} collective-permute-done((bf16[2176,128]{1,0:T(8,128)(2,1)S(1)}, bf16[2176,128]{1,0:T(8,128)(2,1)S(1)}, u32[]{:S(2)}, u32[]{:S(2)}) %collective-permute-start.31) | collective-permute-done | bytes 557088 | tf_op jit(solution)/shard_map/ppermute | solution.py:508
  69.3 0.1 shard_map.345.late_ref
  69.4 0.1 collective-permute-start.32
  69.4 1.5 %shard_map.346 = (f32[2304,256]{1,0:T(8,128)}, f32[2304,256]{1,0:T(8,128)}, f32[256,768]{1,0:T(8,128)}, f32[256,256]{1,0:T(8,128)}) custom-call(bf16[4352,128]{1,0:T(8,128)(2,1)S(1)} %shard_map.345.late_ref, f32[2304,256]{1,0:T(8,128)} %get-tuple-element.150.conv2_in), custom_call_target="tpu_custom_call", output_to_operand_aliasing={{1}: (1, {})} | custom-call | flops 1 | bytes 1 | tf_op jit(solution)/shard_map/pallas_call | solution.py:678
  71.0 1.2 %collective-permute-done.32.late_ref = bf16[4352,128]{1,0:T(8,128)(2,1)S(1)} collective-permute-done((bf16[4352,128]{1,0:T(8,128)(2,1)S(1)}, bf16[4352,128]{1,0:T(8,128)(2,1)S(1)}, u32[]{:S(2)}, u32[]{:S(2)}) %collective-permute-start.32) | collective-permute-done | bytes 1114144 | tf_op jit(solution)/shard_map/ppermute | solution.py:508
  72.2 1.5 %shard_map.347 = (f32[2304,256]{1,0:T(8,128)}, f32[2304,256]{1,0:T(8,128)}, f32[256,768]{1,0:T(8,128)}, f32[256,256]{1,0:T(8,128)}) custom-call(bf16[4352,128]{1,0:T(8,128)(2,1)S(1)} %collective-permute-done.32.late_ref, f32[2304,256]{1,0:T(8,128)} %get-tuple-element.151.conv1_in, ...), custom_call_target="tpu_custom_call", output_to_operand_aliasing={{0}: (1, {}), {1}: (2, {}), {2}: (3, {}), {3}: (4, {})} | custom-call | flops 1 | bytes 1 | tf_op jit(solution)/shard_map/pallas_call | solution.py:681
  (66 shorter events, 0.4 us)
Async XLA Ops:
  0.7 7.2 %copy-start = (bf16[3,3,256,256]{3,2,1,0:T(8,128)(2,1)S(1)}, bf16[3,3,256,256]{3,2,1,0:T(8,128)(2,1)}, u32[]{:S(2)}) copy-start(bf16[3,3,256,256]{3,2,1,0:T(8,128)(2,1)} %param.24) | copy-start | bytes 3538948
  0.7 7.2 %copy-start.1 = (bf16[3,3,256,256]{3,2,1,0:T(8,128)(2,1)S(1)}, bf16[3,3,256,256]{3,2,1,0:T(8,128)(2,1)}, u32[]{:S(2)}) copy-start(bf16[3,3,256,256]{3,2,1,0:T(8,128)(2,1)} %param.29) | copy-start | bytes 3538948
  0.7 7.2 %copy-start.3 = (bf16[1000,512]{1,0:T(8,128)(2,1)S(1)}, bf16[1000,512]{1,0:T(8,128)(2,1)}, u32[]{:S(2)}) copy-start(bf16[1000,512]{1,0:T(8,128)(2,1)} %table_ref.3) | copy-start | bytes 3072004
  0.7 7.2 %copy-start.5 = (bf16[512,256]{1,0:T(8,128)(2,1)S(1)}, bf16[512,256]{1,0:T(8,128)(2,1)}, u32[]{:S(2)}) copy-start(bf16[512,256]{1,0:T(8,128)(2,1)} %embed_ref.3) | copy-start | bytes 786436
  0.7 7.2 %copy-start.8 = (s32[4]{0:T(128)S(1)}, s32[4]{0:T(128)}, u32[]{:S(2)}) copy-start(s32[4]{0:T(128)} %steps_ref.3) | copy-start | bytes 52
  0.7 7.2 %copy-start.9 = (f32[256]{0:T(256)S(1)}, f32[256]{0:T(256)}, u32[]{:S(2)}) copy-start(f32[256]{0:T(256)} %param.22) | copy-start | bytes 3076
  0.7 7.2 %copy-start.10 = (f32[256]{0:T(256)S(1)}, f32[256]{0:T(256)}, u32[]{:S(2)}) copy-start(f32[256]{0:T(256)} %param.23) | copy-start | bytes 3076
  0.7 7.2 %copy-start.11 = (f32[256]{0:T(256)S(1)}, f32[256]{0:T(256)}, u32[]{:S(2)}) copy-start(f32[256]{0:T(256)} %param.27) | copy-start | bytes 3076
  0.7 7.2 %copy-start.12 = (f32[256]{0:T(256)S(1)}, f32[256]{0:T(256)}, u32[]{:S(2)}) copy-start(f32[256]{0:T(256)} %param.28) | copy-start | bytes 3076
  0.8 7.2 %copy-start.13 = (f32[256]{0:T(256)S(1)}, f32[256]{0:T(256)}, u32[]{:S(2)}) copy-start(f32[256]{0:T(256)} %param.30) | copy-start | bytes 3076
  0.8 7.2 %copy-start.14 = (f32[256]{0:T(256)S(1)}, f32[256]{0:T(256)}, u32[]{:S(2)}) copy-start(f32[256]{0:T(256)} %param.31) | copy-start | bytes 3076
  0.8 7.2 %copy-start.15 = (f32[256]{0:T(256)S(1)}, f32[256]{0:T(256)}, u32[]{:S(2)}) copy-start(f32[256]{0:T(256)} %param.32) | copy-start | bytes 3076
  0.8 7.2 %copy-start.16 = (f32[256]{0:T(256)S(1)}, f32[256]{0:T(256)}, u32[]{:S(2)}) copy-start(f32[256]{0:T(256)} %param.34) | copy-start | bytes 3076
  0.8 7.2 %copy-start.17 = (f32[256]{0:T(256)S(1)}, f32[256]{0:T(256)}, u32[]{:S(2)}) copy-start(f32[256]{0:T(256)} %param.36) | copy-start | bytes 3076
  0.8 7.2 %copy-start.18 = (f32[256]{0:T(256)S(1)}, f32[256]{0:T(256)}, u32[]{:S(2)}) copy-start(f32[256]{0:T(256)} %param.26) | copy-start | bytes 3076
  2.6 5.3 %collective-permute-start = (bf16[64,256]{1,0:T(8,128)(2,1)}, bf16[64,256]{1,0:T(8,128)(2,1)S(1)}, u32[]{:S(2)}, u32[]{:S(2)}) collective-permute-start(bf16[64,256]{1,0:T(8,128)(2,1)} %get-tuple-element.96), channel_id=1, source_target_pairs={{0,1},{1,0},{2,3},{3,2},{4,5},{5,4},{6,7},{7,6},{8,9},{9,8},{10,11... | collective-permute-start | bytes 98312 | tf_op jit(solution)/shard_map/ppermute | solution.py:508
  3.1 5.9 %collective-permute-start.1 = (bf16[64,256]{1,0:T(8,128)(2,1)}, bf16[64,256]{1,0:T(8,128)(2,1)S(1)}, u32[]{:S(2)}, u32[]{:S(2)}) collective-permute-start(bf16[64,256]{1,0:T(8,128)(2,1)} %get-tuple-element.97), channel_id=1, source_target_pairs={{0,2},{1,3},{2,0},{3,1},{4,6},{5,7},{6,4},{7,5},{8,10},{9,11},{10,... | collective-permute-start | bytes 98312 | tf_op jit(solution)/shard_map/ppermute | solution.py:508
  5.7 3.6 %collective-permute-start.2 = (bf16[64,256]{1,0:T(8,128)(2,1)}, bf16[64,256]{1,0:T(8,128)(2,1)S(1)}, u32[]{:S(2)}, u32[]{:S(2)}) collective-permute-start(bf16[64,256]{1,0:T(8,128)(2,1)} %get-tuple-element.98), channel_id=1, source_target_pairs={{0,3},{1,2},{2,1},{3,0},{4,7},{5,6},{6,5},{7,4},{8,11},{9,10},{10,... | collective-permute-start | bytes 98312 | tf_op jit(solution)/shard_map/ppermute | solution.py:508
  5.8 6.5 %collective-permute-start.3 = (bf16[64,256]{1,0:T(8,128)(2,1)}, bf16[64,256]{1,0:T(8,128)(2,1)S(1)}, u32[]{:S(2)}, u32[]{:S(2)}) collective-permute-start(bf16[64,256]{1,0:T(8,128)(2,1)} %get-tuple-element.107), channel_id=1, source_target_pairs={{0,1},{1,0},{2,3},{3,2},{4,5},{5,4},{6,7},{7,6},{8,9},{9,8},{10,11... | collective-permute-start | bytes 98312 | tf_op jit(solution)/shard_map/ppermute | solution.py:508
  5.9 6.3 %collective-permute-start.4 = (bf16[64,256]{1,0:T(8,128)(2,1)}, bf16[64,256]{1,0:T(8,128)(2,1)S(1)}, u32[]{:S(2)}, u32[]{:S(2)}) collective-permute-start(bf16[64,256]{1,0:T(8,128)(2,1)} %get-tuple-element.108), channel_id=1, source_target_pairs={{0,2},{1,3},{2,0},{3,1},{4,6},{5,7},{6,4},{7,5},{8,10},{9,11},{10,... | collective-permute-start | bytes 98312 | tf_op jit(solution)/shard_map/ppermute | solution.py:508
  7.9 4.4 %collective-permute-start.5 = (bf16[64,256]{1,0:T(8,128)(2,1)}, bf16[64,256]{1,0:T(8,128)(2,1)S(1)}, u32[]{:S(2)}, u32[]{:S(2)}) collective-permute-start(bf16[64,256]{1,0:T(8,128)(2,1)} %get-tuple-element.109), channel_id=1, source_target_pairs={{0,3},{1,2},{2,1},{3,0},{4,7},{5,6},{6,5},{7,4},{8,11},{9,10},{10,... | collective-permute-start | bytes 98312 | tf_op jit(solution)/shard_map/ppermute | solution.py:508
  8.0 1.3 %copy-start.2 = (bf16[256,768]{1,0:T(8,128)(2,1)S(1)}, bf16[256,768]{1,0:T(8,128)(2,1)}, u32[]{:S(2)}) copy-start(bf16[256,768]{1,0:T(8,128)(2,1)} %qkv_weight_ref.3) | copy-start | bytes 1179652
  8.0 1.2 %copy-start.4 = (bf16[256,256]{1,0:T(8,128)(2,1)S(1)}, bf16[256,256]{1,0:T(8,128)(2,1)}, u32[]{:S(2)}) copy-start(bf16[256,256]{1,0:T(8,128)(2,1)} %out_weight_ref.3) | copy-start | bytes 393220
  8.0 1.2 %copy-start.7 = (bf16[64,256]{1,0:T(8,128)(2,1)S(1)}, bf16[64,256]{1,0:T(8,128)(2,1)}, u32[]{:S(2)}) copy-start(bf16[64,256]{1,0:T(8,128)(2,1)} %get-tuple-element.95.refs_0_) | copy-start | bytes 98308
  9.0 3.3 %copy-start.6 = (bf16[64,256]{1,0:T(8,128)(2,1)S(1)}, bf16[64,256]{1,0:T(8,128)(2,1)}, u32[]{:S(2)}) copy-start(bf16[64,256]{1,0:T(8,128)(2,1)} %get-tuple-element.106.refs_0_) | copy-start | bytes 98308
  14.1 3.0 %collective-permute-start.6 = (bf16[3328,128]{1,0:T(8,128)(2,1)S(1)}, bf16[3328,128]{1,0:T(8,128)(2,1)S(1)}, u32[]{:S(2)}, u32[]{:S(2)}) collective-permute-start(bf16[3328,128]{1,0:T(8,128)(2,1)S(1)} %get-tuple-element.118), channel_id=1, source_target_pairs={{0,1},{1,0},{2,3},{3,2},{4,5},{5,4},{6,7},{7,6},{8,9},{9,8},{10,11... | collective-permute-start | bytes 2555912 | tf_op jit(solution)/shard_map/ppermute | solution.py:508
  17.0 2.6 %collective-permute-start.10 = (bf16[2352,128]{1,0:T(8,128)(2,1)S(1)}, bf16[2352,128]{1,0:T(8,128)(2,1)S(1)}, u32[]{:S(2)}, u32[]{:S(2)}) collective-permute-start(bf16[2352,128]{1,0:T(8,128)(2,1)S(1)} %get-tuple-element.126), channel_id=1, source_target_pairs={{0,1},{1,0},{2,3},{3,2},{4,5},{5,4},{6,7},{7,6},{8,9},{9,8},{10,11... | collective-permute-start | bytes 1806344 | tf_op jit(solution)/shard_map/ppermute | solution.py:508
  17.3 8.1 %collective-permute-start.14 = (bf16[1024,128]{1,0:T(8,128)(2,1)S(1)}, bf16[1024,128]{1,0:T(8,128)(2,1)S(1)}, u32[]{:S(2)}, u32[]{:S(2)}) collective-permute-start(bf16[1024,128]{1,0:T(8,128)(2,1)S(1)} %get-tuple-element.132), channel_id=1, source_target_pairs={{0,2},{1,5},{2,0},{3,7},{4,6},{5,1},{6,4},{7,3},{8,10},{9,13},{10,... | collective-permute-start | bytes 786440 | tf_op jit(solution)/shard_map/ppermute | solution.py:508
  19.7 7.1 %collective-permute-start.15 = (bf16[1152,128]{1,0:T(8,128)(2,1)S(1)}, bf16[1152,128]{1,0:T(8,128)(2,1)S(1)}, u32[]{:S(2)}, u32[]{:S(2)}) collective-permute-start(bf16[1152,128]{1,0:T(8,128)(2,1)S(1)} %get-tuple-element.133), channel_id=1, source_target_pairs={{0,2},{1,5},{2,0},{3,7},{4,6},{5,1},{6,4},{7,3},{8,10},{9,13},{10,... | collective-permute-start | bytes 884744 | tf_op jit(solution)/shard_map/ppermute | solution.py:508
  20.9 7.7 %collective-permute-start.11 = (bf16[384,128]{1,0:T(8,128)(2,1)S(1)}, bf16[384,128]{1,0:T(8,128)(2,1)S(1)}, u32[]{:S(2)}, u32[]{:S(2)}) collective-permute-start(bf16[384,128]{1,0:T(8,128)(2,1)S(1)} %get-tuple-element.129), channel_id=1, source_target_pairs={{0,8},{1,9},{2,10},{3,11},{4,12},{5,13},{6,14},{7,15},{8,0},{9,1},... | collective-permute-start | bytes 294920 | tf_op jit(solution)/shard_map/ppermute | solution.py:508
  22.5 10.5 %collective-permute-start.12 = (bf16[384,128]{1,0:T(8,128)(2,1)S(1)}, bf16[384,128]{1,0:T(8,128)(2,1)S(1)}, u32[]{:S(2)}, u32[]{:S(2)}) collective-permute-start(bf16[384,128]{1,0:T(8,128)(2,1)S(1)} %get-tuple-element.130), channel_id=1, source_target_pairs={{0,16},{1,17},{2,18},{3,19},{4,20},{5,21},{6,22},{7,23},{8,24},{9,... | collective-permute-start | bytes 294920 | tf_op jit(solution)/shard_map/ppermute | solution.py:508
  25.1 7.9 %collective-permute-start.13 = (bf16[384,128]{1,0:T(8,128)(2,1)S(1)}, bf16[384,128]{1,0:T(8,128)(2,1)S(1)}, u32[]{:S(2)}, u32[]{:S(2)}) collective-permute-start(bf16[384,128]{1,0:T(8,128)(2,1)S(1)} %get-tuple-element.131), channel_id=1, source_target_pairs={{0,24},{1,25},{2,26},{3,27},{4,28},{5,29},{6,30},{7,31},{8,16},{9,... | collective-permute-start | bytes 294920 | tf_op jit(solution)/shard_map/ppermute | solution.py:508
  27.0 6.6 %collective-permute-start.16 = (bf16[1088,128]{1,0:T(8,128)(2,1)S(1)}, bf16[1088,128]{1,0:T(8,128)(2,1)S(1)}, u32[]{:S(2)}, u32[]{:S(2)}) collective-permute-start(bf16[1088,128]{1,0:T(8,128)(2,1)S(1)} %get-tuple-element.135), channel_id=1, source_target_pairs={{0,4},{1,3},{2,6},{3,1},{4,0},{5,7},{6,2},{7,5},{8,12},{9,11},{10,... | collective-permute-start | bytes 835592 | tf_op jit(solution)/shard_map/ppermute | solution.py:508
  33.7 6.0 %collective-permute-start.18 = (bf16[272,128]{1,0:T(8,128)(2,1)S(1)}, bf16[272,128]{1,0:T(8,128)(2,1)S(1)}, u32[]{:S(2)}, u32[]{:S(2)}) collective-permute-start(bf16[272,128]{1,0:T(8,128)(2,1)S(1)} %get-tuple-element.137), channel_id=1, source_target_pairs={{0,8},{1,9},{2,10},{3,11},{4,12},{5,13},{6,14},{7,15},{8,0},{9,1},... | collective-permute-start | bytes 208904 | tf_op jit(solution)/shard_map/ppermute | solution.py:508
  35.3 6.7 %collective-permute-start.19 = (bf16[272,128]{1,0:T(8,128)(2,1)S(1)}, bf16[272,128]{1,0:T(8,128)(2,1)S(1)}, u32[]{:S(2)}, u32[]{:S(2)}) collective-permute-start(bf16[272,128]{1,0:T(8,128)(2,1)S(1)} %get-tuple-element.138), channel_id=1, source_target_pairs={{0,16},{1,17},{2,18},{3,19},{4,20},{5,21},{6,22},{7,23},{8,24},{9,... | collective-permute-start | bytes 208904 | tf_op jit(solution)/shard_map/ppermute | solution.py:508
  37.9 6.1 %collective-permute-start.20 = (bf16[272,128]{1,0:T(8,128)(2,1)S(1)}, bf16[272,128]{1,0:T(8,128)(2,1)S(1)}, u32[]{:S(2)}, u32[]{:S(2)}) collective-permute-start(bf16[272,128]{1,0:T(8,128)(2,1)S(1)} %get-tuple-element.139), channel_id=1, source_target_pairs={{0,24},{1,25},{2,26},{3,27},{4,28},{5,29},{6,30},{7,31},{8,16},{9,... | collective-permute-start | bytes 208904 | tf_op jit(solution)/shard_map/ppermute | solution.py:508
  38.2 7.1 %collective-permute-start.17 = (bf16[384,128]{1,0:T(8,128)(2,1)S(1)}, bf16[384,128]{1,0:T(8,128)(2,1)S(1)}, u32[]{:S(2)}, u32[]{:S(2)}) collective-permute-start(bf16[384,128]{1,0:T(8,128)(2,1)S(1)} %shard_map.335.refs_8_.refs_0_.refs_2_.refs_4_), channel_id=1, source_target_pairs={{0,2},{1,5},{2,0},{3,7},{4,6},{5,1},{6,4},{7,3},{8,10},{9,13},{10,... | collective-permute-start | bytes 294920 | tf_op jit(solution)/shard_map/ppermute | solution.py:508
  39.7 5.6 %collective-permute-start.7 = (bf16[2,64,256]{2,1,0:T(8,128)(2,1)S(1)}, bf16[2,64,256]{2,1,0:T(8,128)(2,1)S(1)}, u32[]{:S(2)}, u32[]{:S(2)}) collective-permute-start(bf16[2,64,256]{2,1,0:T(8,128)(2,1)S(1)} %get-tuple-element.121), channel_id=1, source_target_pairs={{0,1},{1,0},{2,3},{3,2},{4,5},{5,4},{6,7},{7,6},{8,9},{9,8},{10,11... | collective-permute-start | bytes 196616 | tf_op jit(solution)/shard_map/ppermute | solution.py:508
  39.7 8.9 %collective-permute-start.8 = (bf16[2,64,256]{2,1,0:T(8,128)(2,1)S(1)}, bf16[2,64,256]{2,1,0:T(8,128)(2,1)S(1)}, u32[]{:S(2)}, u32[]{:S(2)}) collective-permute-start(bf16[2,64,256]{2,1,0:T(8,128)(2,1)S(1)} %get-tuple-element.122), channel_id=1, source_target_pairs={{0,2},{1,3},{2,0},{3,1},{4,6},{5,7},{6,4},{7,5},{8,10},{9,11},{10,... | collective-permute-start | bytes 196616 | tf_op jit(solution)/shard_map/ppermute | solution.py:508
  42.0 8.1 %collective-permute-start.9 = (bf16[2,64,256]{2,1,0:T(8,128)(2,1)S(1)}, bf16[2,64,256]{2,1,0:T(8,128)(2,1)S(1)}, u32[]{:S(2)}, u32[]{:S(2)}) collective-permute-start(bf16[2,64,256]{2,1,0:T(8,128)(2,1)S(1)} %get-tuple-element.123), channel_id=1, source_target_pairs={{0,3},{1,2},{2,1},{3,0},{4,7},{5,6},{6,5},{7,4},{8,11},{9,10},{10,... | collective-permute-start | bytes 196616 | tf_op jit(solution)/shard_map/ppermute | solution.py:508
  44.1 6.8 %collective-permute-start.24 = (bf16[272,128]{1,0:T(8,128)(2,1)S(1)}, bf16[272,128]{1,0:T(8,128)(2,1)S(1)}, u32[]{:S(2)}, u32[]{:S(2)}) collective-permute-start(bf16[272,128]{1,0:T(8,128)(2,1)S(1)} %shard_map.336.refs_6_.refs_0_), channel_id=1, source_target_pairs={{0,24},{1,25},{2,26},{3,27},{4,28},{5,29},{6,30},{7,31},{8,16},{9,... | collective-permute-start | bytes 208904 | tf_op jit(solution)/shard_map/ppermute | solution.py:508
  45.3 7.3 %collective-permute-start.23 = (bf16[272,128]{1,0:T(8,128)(2,1)S(1)}, bf16[272,128]{1,0:T(8,128)(2,1)S(1)}, u32[]{:S(2)}, u32[]{:S(2)}) collective-permute-start(bf16[272,128]{1,0:T(8,128)(2,1)S(1)} %shard_map.336.refs_6_.refs_0_), channel_id=1, source_target_pairs={{0,16},{1,17},{2,18},{3,19},{4,20},{5,21},{6,22},{7,23},{8,24},{9,... | collective-permute-start | bytes 208904 | tf_op jit(solution)/shard_map/ppermute | solution.py:508
  45.3 7.7 %collective-permute-start.22 = (bf16[272,128]{1,0:T(8,128)(2,1)S(1)}, bf16[272,128]{1,0:T(8,128)(2,1)S(1)}, u32[]{:S(2)}, u32[]{:S(2)}) collective-permute-start(bf16[272,128]{1,0:T(8,128)(2,1)S(1)} %shard_map.336.refs_6_.refs_0_), channel_id=1, source_target_pairs={{0,8},{1,9},{2,10},{3,11},{4,12},{5,13},{6,14},{7,15},{8,0},{9,1},... | collective-permute-start | bytes 208904 | tf_op jit(solution)/shard_map/ppermute | solution.py:508
  48.6 6.0 %collective-permute-start.21 = (bf16[384,128]{1,0:T(8,128)(2,1)S(1)}, bf16[384,128]{1,0:T(8,128)(2,1)S(1)}, u32[]{:S(2)}, u32[]{:S(2)}) collective-permute-start(bf16[384,128]{1,0:T(8,128)(2,1)S(1)} %shard_map.337.refs_4_.refs_0_.refs_2_), channel_id=1, source_target_pairs={{0,4},{1,3},{2,6},{3,1},{4,0},{5,7},{6,2},{7,5},{8,12},{9,11},{10,... | collective-permute-start | bytes 294920 | tf_op jit(solution)/shard_map/ppermute | solution.py:508
  53.0 6.6 %collective-permute-start.26 = (bf16[1088,128]{1,0:T(8,128)(2,1)S(1)}, bf16[1088,128]{1,0:T(8,128)(2,1)S(1)}, u32[]{:S(2)}, u32[]{:S(2)}) collective-permute-start(bf16[1088,128]{1,0:T(8,128)(2,1)S(1)} %shard_map.339.refs_6_.refs_0_), channel_id=1, source_target_pairs={{0,4},{1,3},{2,6},{3,1},{4,0},{5,7},{6,2},{7,5},{8,12},{9,11},{10,... | collective-permute-start | bytes 835592 | tf_op jit(solution)/shard_map/ppermute | solution.py:508
  54.6 8.6 %collective-permute-start.29 = (bf16[336,128]{1,0:T(8,128)(2,1)S(1)}, bf16[336,128]{1,0:T(8,128)(2,1)S(1)}, u32[]{:S(2)}, u32[]{:S(2)}) collective-permute-start(bf16[336,128]{1,0:T(8,128)(2,1)S(1)} %get-tuple-element.144.refs_2_.refs_0_), channel_id=1, source_target_pairs={{0,24},{1,25},{2,26},{3,27},{4,28},{5,29},{6,30},{7,31},{8,16},{9,... | collective-permute-start | bytes 258056 | tf_op jit(solution)/shard_map/ppermute | solution.py:508
  56.8 7.4 %collective-permute-start.28 = (bf16[336,128]{1,0:T(8,128)(2,1)S(1)}, bf16[336,128]{1,0:T(8,128)(2,1)S(1)}, u32[]{:S(2)}, u32[]{:S(2)}) collective-permute-start(bf16[336,128]{1,0:T(8,128)(2,1)S(1)} %get-tuple-element.144.refs_2_.refs_0_), channel_id=1, source_target_pairs={{0,16},{1,17},{2,18},{3,19},{4,20},{5,21},{6,22},{7,23},{8,24},{9,... | collective-permute-start | bytes 258056 | tf_op jit(solution)/shard_map/ppermute | solution.py:508
  56.8 7.4 %collective-permute-start.27 = (bf16[336,128]{1,0:T(8,128)(2,1)S(1)}, bf16[336,128]{1,0:T(8,128)(2,1)S(1)}, u32[]{:S(2)}, u32[]{:S(2)}) collective-permute-start(bf16[336,128]{1,0:T(8,128)(2,1)S(1)} %get-tuple-element.144.refs_2_.refs_0_), channel_id=1, source_target_pairs={{0,8},{1,9},{2,10},{3,11},{4,12},{5,13},{6,14},{7,15},{8,0},{9,1},... | collective-permute-start | bytes 258056 | tf_op jit(solution)/shard_map/ppermute | solution.py:508
  59.1 1.4 %collective-permute-start.25 = (bf16[48,128]{1,0:T(8,128)(2,1)S(1)}, bf16[48,128]{1,0:T(8,128)(2,1)S(1)}, u32[]{:S(2)}, u32[]{:S(2)}) collective-permute-start(bf16[48,128]{1,0:T(8,128)(2,1)S(1)} %get-tuple-element.143.sums_ref), channel_id=1, source_target_pairs={{0,1},{1,0},{2,3},{3,2},{4,5},{5,4},{6,7},{7,6},{8,9},{9,8},{10,11... | collective-permute-start | bytes 36872 | tf_op jit(solution)/shard_map/ppermute | solution.py:508
  59.7 9.6 %collective-permute-start.31 = (bf16[2176,128]{1,0:T(8,128)(2,1)S(1)}, bf16[2176,128]{1,0:T(8,128)(2,1)S(1)}, u32[]{:S(2)}, u32[]{:S(2)}) collective-permute-start(bf16[2176,128]{1,0:T(8,128)(2,1)S(1)} %shard_map.341.token_in.refs_0_), channel_id=1, source_target_pairs={{0,2},{1,5},{2,0},{3,7},{4,6},{5,1},{6,4},{7,3},{8,10},{9,13},{10,... | collective-permute-start | bytes 1671176 | tf_op jit(solution)/shard_map/ppermute | solution.py:508
  64.2 1.7 %collective-permute-start.30 = (bf16[1344,128]{1,0:T(8,128)(2,1)S(1)}, bf16[1344,128]{1,0:T(8,128)(2,1)S(1)}, u32[]{:S(2)}, u32[]{:S(2)}) collective-permute-start(bf16[1344,128]{1,0:T(8,128)(2,1)S(1)} %shard_map.343.mine_ref.token_ref), channel_id=1, source_target_pairs={{0,1},{1,0},{2,3},{3,2},{4,5},{5,4},{6,7},{7,6},{8,9},{9,8},{10,11... | collective-permute-start | bytes 1032200 | tf_op jit(solution)/shard_map/ppermute | solution.py:508
  69.4 2.8 %collective-permute-start.32 = (bf16[4352,128]{1,0:T(8,128)(2,1)S(1)}, bf16[4352,128]{1,0:T(8,128)(2,1)S(1)}, u32[]{:S(2)}, u32[]{:S(2)}) collective-permute-start(bf16[4352,128]{1,0:T(8,128)(2,1)S(1)} %shard_map.345.late_ref), channel_id=1, source_target_pairs={{0,1},{1,0},{2,3},{3,2},{4,5},{5,4},{6,7},{7,6},{8,9},{9,8},{10,11... | collective-permute-start | bytes 3342344 | tf_op jit(solution)/shard_map/ppermute | solution.py:508

commit v3 on v2

--- a/solution.py
+++ b/solution.py
@@ -26,7 +26,7 @@
 N3G, N3B, QB, OB, C2B, N2G, N2B, EB = range(8)
 HIGH, LOW = 7, 8
 VEC_ROWS = 16
-EARLY_TAPS = 5
+EARLY_TAPS = 6
 DIGIT = 32
 
 

time: 73.8 us -> 73.6 us (level)
  transfers between devices with their start and end apart: 33 -> 33, of which waited for: 13 -> 10; matrix products, arithmetic and copies ran while one was open for 0% -> 0% of each run, Pallas kernels for 20% -> 20%
where the time goes in v3:
time: 73.6 us; the launch traced here: 73.4 us
  starting transfers between devices  33.2 us (45%)
  Pallas kernels  19.9 us (27%)
  waiting for transfers between devices  19 us (26%)
  between operations  1.17 us (2%)
    ppermute x33, starting transfers between devices, permute(): return lax.ppermute(array, AXES, [(i, partner(i)) for i in range(total)])  33.2 us
    ppermute x33, waiting for transfers between devices, permute(): return lax.ppermute(array, AXES, [(i, partner(i)) for i in range(total)])  19 us
    pallas_call x1, Pallas kernels, shards(): call(functools.partial(forward_kernel, w), [field(BF16), field(BF16), fie...  2.97 us
    pallas_call x1, Pallas kernels, shards(): call(functools.partial(table_kernel, total), outs + [shape((1, c), F32)]...  2.8 us
    pallas_call x1, Pallas kernels, shards(): call(functools.partial(back_kernel, w, total), [half(rows_1 + rows_v)] *...  2.38 us
    pallas_call x1, Pallas kernels, shards(): call(functools.partial(main_kernel, w), [half(rows_a + rows_m)] * 2 + [sh...  1.82 us
    pallas_call x1, Pallas kernels, shards(): call(pack_kernel, [shape(block[1:], BF16)] * (2 * seq), [HBM] * 2, None,...  1.79 us
    pallas_call x1, Pallas kernels, shards(): call(functools.partial(early_kernel, rows_o), grads[:1] + [shape((1, c),...  1.79 us
  transfers between devices with their start and end apart: 33, of which 10 were waited for; matrix products, arithmetic and copies ran while one was open for 0% of the time, Pallas kernels for 20%

profile of v3, /device:TPU:0, one launch (start us, length us, event | category | flops | bytes accessed | tf_op | source)
XLA Modules:
  0.0 73.4 jit_solution(11382166250397291041)
XLA Ops:
  0.8 1.8 %shard_map.323 = (bf16[64,256]{1,0:T(8,128)(2,1)}, bf16[64,256]{1,0:T(8,128)(2,1)}, bf16[64,256]{1,0:T(8,128)(2,1)}, bf16[64,256]{1,0:T(8,128)(2,1)}, bf16[64,25...) custom-call(bf16[4,64,256]{2,1,0:T(8,128)(2,1)} %bitcast.46, ...), custom_call_target="tpu_custom_call" | custom-call | flops 20000000000 | bytes 1 | tf_op jit(solution)/shard_map/pallas_call | solution.py:588
  2.6 0.5 collective-permute-start
  3.1 2.6 %collective-permute-start.1 = (bf16[64,256]{1,0:T(8,128)(2,1)}, bf16[64,256]{1,0:T(8,128)(2,1)S(1)}, u32[]{:S(2)}, u32[]{:S(2)}) collective-permute-start(bf16[64,256]{1,0:T(8,128)(2,1)} %get-tuple-element.97), channel_id=1, source_target_pairs={{0,2},{1,3},{2,0},{3,1},{4,6},{5,7},{6,4},{7,5},{8,10},{9,11},{10,... | collective-permute-start | bytes 98312 | tf_op jit(solution)/shard_map/ppermute | solution.py:508
  5.7 0.1 collective-permute-start.2
  5.8 0.1 collective-permute-start.3
  5.9 1.9 %collective-permute-start.4 = (bf16[64,256]{1,0:T(8,128)(2,1)}, bf16[64,256]{1,0:T(8,128)(2,1)S(1)}, u32[]{:S(2)}, u32[]{:S(2)}) collective-permute-start(bf16[64,256]{1,0:T(8,128)(2,1)} %get-tuple-element.108), channel_id=1, source_target_pairs={{0,2},{1,3},{2,0},{3,1},{4,6},{5,7},{6,4},{7,5},{8,10},{9,11},{10,... | collective-permute-start | bytes 98312 | tf_op jit(solution)/shard_map/ppermute | solution.py:508
  8.0 0.0 copy-start.2
  8.0 0.0 copy-start.4
  8.0 0.0 copy-start.7
  8.1 1.0 %shard_map.322 = (f32[16,256]{1,0:T(8,128)S(1)}, bf16[256,256]{1,0:T(8,128)(2,1)S(1)}) custom-call(s32[4]{0:T(128)S(1)} %copy-done.8, bf16[1000,512]{1,0:T(8,128)(2,1)S(1)} %copy-done.3, bf16[512,256]{1,0:T(8,128)(2,1)S(1)} %copy-done.5, bf16[2304,256]{1,0:T(8,128)(2,1)S(1)} %bitcast.28, bf16[2304,256]{1,0:T(8,128)(2,1)S(1)} %bitcast.31, ...), custom_call_target="tpu_custom_call" | custom-call | flops 20000000000 | bytes 1 | tf_op jit(solution)/shard_map/pallas_call | solution.py:593
  9.0 0.2 collective-permute-done.2.refs_3_
  9.3 3.0 %shard_map.324 = (bf16[256,256]{1,0:T(8,128)(2,1)S(1)}, bf16[256,256]{1,0:T(8,128)(2,1)S(1)}, bf16[256,256]{1,0:T(8,128)(2,1)S(1)}, f32[256,256]{1,0:T(8,128)S(1...) custom-call(f32[16,256]{1,0:T(8,128)S(1)} %get-tuple-element.93.vec_, ...), custom_call_target="tpu_custom_call" | custom-call | flops 1 | bytes 1 | tf_op jit(solution)/shard_map/pallas_call | solution.py:597
  12.3 0.0 collective-permute-done.3.refs_1_
  12.3 0.0 collective-permute-done.4.refs_2_
  12.3 1.8 %shard_map.325 = (bf16[3328,128]{1,0:T(8,128)(2,1)S(1)}, bf16[3328,128]{1,0:T(8,128)(2,1)S(1)}, f32[8,256]{1,0:T(8,128)S(1)}, f32[256,256]{1,0:T(8,128)S(1)}, bf16[288,768]{1,0:T(8,128)(2,1)S(1)}) custom-call(f32[16,256]{1,0:T(8,128)S(1)} %get-tuple-element.93.vec_ref, bf16[256,256]{1,0:T(8,128)(2,1)S(1)} %get-tuple-element.94.spread_ref, ...), custom_call_target="tpu_custom_call" | custom-call | flops 1 | bytes 1 | tf_op jit(solution)/shard_map/pallas_call | solution.py:605
  14.1 0.5 collective-permute-start.6
  14.6 2.4 %shard_map.326 = (bf16[2352,128]{1,0:T(8,128)(2,1)S(1)}, bf16[2352,128]{1,0:T(8,128)(2,1)S(1)}, bf16[288,768]{1,0:T(8,128)(2,1)S(1)}) custom-call(s32[4]{0:T(128)S(1)} %copy-done.8, f32[16,256]{1,0:T(8,128)S(1)} %get-tuple-element.93.vec_ref, bf16[256,256]{1,0:T(8,128)(2,1)S(1)} %get-tuple-element.94.spread_ref, bf16[2304,256]{1,0:T(8,128)(2,1)S(1)} %bitcast.33, ...), custom_call_target="tpu_custom_call" | custom-call | flops 1 | bytes 1 | tf_op jit(solution)/shard_map/pallas_call | solution.py:614
  17.0 0.2 collective-permute-start.10
  17.2 0.1 shard_map.327
  17.3 1.5 %collective-permute-start.14 = (bf16[896,128]{1,0:T(8,128)(2,1)S(1)}, bf16[896,128]{1,0:T(8,128)(2,1)S(1)}, u32[]{:S(2)}, u32[]{:S(2)}) collective-permute-start(bf16[896,128]{1,0:T(8,128)(2,1)S(1)} %get-tuple-element.132), channel_id=1, source_target_pairs={{0,2},{1,5},{2,0},{3,7},{4,6},{5,1},{6,4},{7,3},{8,10},{9,13},{10,... | collective-permute-start | bytes 688136 | tf_op jit(solution)/shard_map/ppermute | solution.py:508
  18.8 0.8 %shard_map.328 = (bf16[64,128]{1,0:T(8,128)(2,1)S(1)}, bf16[2,64,256]{2,1,0:T(8,128)(2,1)S(1)}, bf16[2,64,256]{2,1,0:T(8,128)(2,1)S(1)}, bf16[2,64,256]{2,1,0:T(8,128)(2,1)S(1)}, bf16[2,64,256]{2,1,0:T(8,128)(2,1)S(1)}) custom-call(f32[16,256]{1,0:T(8,128)S(1)} %get-tuple-element.93.vec_ref, bf16[256,256]{1,0:T(8,128)(2,1)S(1)} %get-tuple-element.94.spread_ref, ...), custom_call_target="tpu_custom_call" | custom-call | flops 1 | bytes 1 | tf_op jit(solution)/shard_map/pallas_call | solution.py:620
  19.6 0.2 shard_map.329
  19.7 1.1 %collective-permute-start.15 = (bf16[1152,128]{1,0:T(8,128)(2,1)S(1)}, bf16[1152,128]{1,0:T(8,128)(2,1)S(1)}, u32[]{:S(2)}, u32[]{:S(2)}) collective-permute-start(bf16[1152,128]{1,0:T(8,128)(2,1)S(1)} %get-tuple-element.133), channel_id=1, source_target_pairs={{0,2},{1,5},{2,0},{3,7},{4,6},{5,1},{6,4},{7,3},{8,10},{9,13},{10,... | collective-permute-start | bytes 884744 | tf_op jit(solution)/shard_map/ppermute | solution.py:508
  20.8 0.1 shard_map.330
  20.9 1.6 %collective-permute-start.11 = (bf16[448,128]{1,0:T(8,128)(2,1)S(1)}, bf16[448,128]{1,0:T(8,128)(2,1)S(1)}, u32[]{:S(2)}, u32[]{:S(2)}) collective-permute-start(bf16[448,128]{1,0:T(8,128)(2,1)S(1)} %get-tuple-element.129), channel_id=1, source_target_pairs={{0,8},{1,9},{2,10},{3,11},{4,12},{5,13},{6,14},{7,15},{8,0},{9,1},... | collective-permute-start | bytes 344072 | tf_op jit(solution)/shard_map/ppermute | solution.py:508
  22.5 2.6 %collective-permute-start.12 = (bf16[448,128]{1,0:T(8,128)(2,1)S(1)}, bf16[448,128]{1,0:T(8,128)(2,1)S(1)}, u32[]{:S(2)}, u32[]{:S(2)}) collective-permute-start(bf16[448,128]{1,0:T(8,128)(2,1)S(1)} %get-tuple-element.130), channel_id=1, source_target_pairs={{0,16},{1,17},{2,18},{3,19},{4,20},{5,21},{6,22},{7,23},{8,24},{9,... | collective-permute-start | bytes 344072 | tf_op jit(solution)/shard_map/ppermute | solution.py:508
  25.1 0.2 collective-permute-start.13
  25.4 0.1 shard_map.331.refs_0_.refs_3_
  25.4 1.1 %collective-permute-done.15.refs_2_ = bf16[1152,128]{1,0:T(8,128)(2,1)S(1)} collective-permute-done((bf16[1152,128]{1,0:T(8,128)(2,1)S(1)}, bf16[1152,128]{1,0:T(8,128)(2,1)S(1)}, u32[]{:S(2)}, u32[]{:S(2)}) %collective-permute-start.15) | collective-permute-done | bytes 294944 | tf_op jit(solution)/shard_map/ppermute | solution.py:508
  26.5 0.1 shard_map.332
  26.6 1.6 %collective-permute-start.16 = (bf16[1024,128]{1,0:T(8,128)(2,1)S(1)}, bf16[1024,128]{1,0:T(8,128)(2,1)S(1)}, u32[]{:S(2)}, u32[]{:S(2)}) collective-permute-start(bf16[1024,128]{1,0:T(8,128)(2,1)S(1)} %get-tuple-element.135), channel_id=1, source_target_pairs={{0,4},{1,3},{2,6},{3,1},{4,0},{5,7},{6,2},{7,5},{8,12},{9,11},{10,... | collective-permute-start | bytes 786440 | tf_op jit(solution)/shard_map/ppermute | solution.py:508
  28.2 6.1 %collective-permute-done.12.refs_2_.refs_6_.refs_10_ = bf16[448,128]{1,0:T(8,128)(2,1)S(1)} collective-permute-done((bf16[448,128]{1,0:T(8,128)(2,1)S(1)}, bf16[448,128]{1,0:T(8,128)(2,1)S(1)}, u32[]{:S(2)}, u32[]{:S(2)}) %collective-permute-start.12) | collective-permute-done | bytes 114720 | tf_op jit(solution)/shard_map/ppermute | solution.py:508
  34.3 0.1 shard_map.333.refs_4_.refs_0_.refs_1_.refs_2_
  34.4 0.1 shard_map.334
  34.5 1.9 %collective-permute-start.18 = (bf16[256,128]{1,0:T(8,128)(2,1)S(1)}, bf16[256,128]{1,0:T(8,128)(2,1)S(1)}, u32[]{:S(2)}, u32[]{:S(2)}) collective-permute-start(bf16[256,128]{1,0:T(8,128)(2,1)S(1)} %get-tuple-element.137), channel_id=1, source_target_pairs={{0,8},{1,9},{2,10},{3,11},{4,12},{5,13},{6,14},{7,15},{8,0},{9,1},... | collective-permute-start | bytes 196616 | tf_op jit(solution)/shard_map/ppermute | solution.py:508
  36.3 1.2 %collective-permute-start.19 = (bf16[256,128]{1,0:T(8,128)(2,1)S(1)}, bf16[256,128]{1,0:T(8,128)(2,1)S(1)}, u32[]{:S(2)}, u32[]{:S(2)}) collective-permute-start(bf16[256,128]{1,0:T(8,128)(2,1)S(1)} %get-tuple-element.138), channel_id=1, source_target_pairs={{0,16},{1,17},{2,18},{3,19},{4,20},{5,21},{6,22},{7,23},{8,24},{9,... | collective-permute-start | bytes 196616 | tf_op jit(solution)/shard_map/ppermute | solution.py:508
  37.6 1.4 %collective-permute-start.20 = (bf16[256,128]{1,0:T(8,128)(2,1)S(1)}, bf16[256,128]{1,0:T(8,128)(2,1)S(1)}, u32[]{:S(2)}, u32[]{:S(2)}) collective-permute-start(bf16[256,128]{1,0:T(8,128)(2,1)S(1)} %get-tuple-element.139), channel_id=1, source_target_pairs={{0,24},{1,25},{2,26},{3,27},{4,28},{5,29},{6,30},{7,31},{8,16},{9,... | collective-permute-start | bytes 196616 | tf_op jit(solution)/shard_map/ppermute | solution.py:508
  38.9 1.4 %collective-permute-start.17 = (bf16[448,128]{1,0:T(8,128)(2,1)S(1)}, bf16[448,128]{1,0:T(8,128)(2,1)S(1)}, u32[]{:S(2)}, u32[]{:S(2)}) collective-permute-start(bf16[448,128]{1,0:T(8,128)(2,1)S(1)} %shard_map.335.refs_8_.refs_0_.refs_2_.refs_4_), channel_id=1, source_target_pairs={{0,2},{1,5},{2,0},{3,7},{4,6},{5,1},{6,4},{7,3},{8,10},{9,13},{10,... | collective-permute-start | bytes 344072 | tf_op jit(solution)/shard_map/ppermute | solution.py:508
  40.3 0.7 collective-permute-start.8
  41.0 1.5 %collective-permute-done.19.refs_2_.refs_6_ = bf16[256,128]{1,0:T(8,128)(2,1)S(1)} collective-permute-done((bf16[256,128]{1,0:T(8,128)(2,1)S(1)}, bf16[256,128]{1,0:T(8,128)(2,1)S(1)}, u32[]{:S(2)}, u32[]{:S(2)}) %collective-permute-start.19) | collective-permute-done | bytes 65568 | tf_op jit(solution)/shard_map/ppermute | solution.py:508
  42.5 1.2 %collective-permute-done.20.refs_3_.refs_7_ = bf16[256,128]{1,0:T(8,128)(2,1)S(1)} collective-permute-done((bf16[256,128]{1,0:T(8,128)(2,1)S(1)}, bf16[256,128]{1,0:T(8,128)(2,1)S(1)}, u32[]{:S(2)}, u32[]{:S(2)}) %collective-permute-start.20) | collective-permute-done | bytes 65568 | tf_op jit(solution)/shard_map/ppermute | solution.py:508
  43.8 1.8 %collective-permute-start.24 = (bf16[256,128]{1,0:T(8,128)(2,1)S(1)}, bf16[256,128]{1,0:T(8,128)(2,1)S(1)}, u32[]{:S(2)}, u32[]{:S(2)}) collective-permute-start(bf16[256,128]{1,0:T(8,128)(2,1)S(1)} %shard_map.336.refs_6_.refs_0_), channel_id=1, source_target_pairs={{0,24},{1,25},{2,26},{3,27},{4,28},{5,29},{6,30},{7,31},{8,16},{9,... | collective-permute-start | bytes 196616 | tf_op jit(solution)/shard_map/ppermute | solution.py:508
  45.5 0.5 collective-permute-start.23
  46.1 2.2 %collective-permute-start.22 = (bf16[256,128]{1,0:T(8,128)(2,1)S(1)}, bf16[256,128]{1,0:T(8,128)(2,1)S(1)}, u32[]{:S(2)}, u32[]{:S(2)}) collective-permute-start(bf16[256,128]{1,0:T(8,128)(2,1)S(1)} %shard_map.336.refs_6_.refs_0_), channel_id=1, source_target_pairs={{0,8},{1,9},{2,10},{3,11},{4,12},{5,13},{6,14},{7,15},{8,0},{9,1},... | collective-permute-start | bytes 196616 | tf_op jit(solution)/shard_map/ppermute | solution.py:508
  48.3 1.4 %collective-permute-start.21 = (bf16[448,128]{1,0:T(8,128)(2,1)S(1)}, bf16[448,128]{1,0:T(8,128)(2,1)S(1)}, u32[]{:S(2)}, u32[]{:S(2)}) collective-permute-start(bf16[448,128]{1,0:T(8,128)(2,1)S(1)} %shard_map.337.refs_4_.refs_0_.refs_2_), channel_id=1, source_target_pairs={{0,4},{1,3},{2,6},{3,1},{4,0},{5,7},{6,2},{7,5},{8,12},{9,11},{10,... | collective-permute-start | bytes 344072 | tf_op jit(solution)/shard_map/ppermute | solution.py:508
  49.6 0.7 shard_map.338
  50.4 3.0 %collective-permute-done.23.refs_2_ = bf16[256,128]{1,0:T(8,128)(2,1)S(1)} collective-permute-done((bf16[256,128]{1,0:T(8,128)(2,1)S(1)}, bf16[256,128]{1,0:T(8,128)(2,1)S(1)}, u32[]{:S(2)}, u32[]{:S(2)}) %collective-permute-start.23) | collective-permute-done | bytes 65568 | tf_op jit(solution)/shard_map/ppermute | solution.py:508
  53.4 0.8 %collective-permute-start.26 = (bf16[1024,128]{1,0:T(8,128)(2,1)S(1)}, bf16[1024,128]{1,0:T(8,128)(2,1)S(1)}, u32[]{:S(2)}, u32[]{:S(2)}) collective-permute-start(bf16[1024,128]{1,0:T(8,128)(2,1)S(1)} %shard_map.339.refs_6_.refs_0_), channel_id=1, source_target_pairs={{0,4},{1,3},{2,6},{3,1},{4,0},{5,7},{6,2},{7,5},{8,12},{9,11},{10,... | collective-permute-start | bytes 786440 | tf_op jit(solution)/shard_map/ppermute | solution.py:508
  54.2 2.4 %collective-permute-start.29 = (bf16[400,128]{1,0:T(8,128)(2,1)S(1)}, bf16[400,128]{1,0:T(8,128)(2,1)S(1)}, u32[]{:S(2)}, u32[]{:S(2)}) collective-permute-start(bf16[400,128]{1,0:T(8,128)(2,1)S(1)} %get-tuple-element.144.refs_2_.refs_0_), channel_id=1, source_target_pairs={{0,24},{1,25},{2,26},{3,27},{4,28},{5,29},{6,30},{7,31},{8,16},{9,... | collective-permute-start | bytes 307208 | tf_op jit(solution)/shard_map/ppermute | solution.py:508
  56.6 2.1 %collective-permute-start.27 = (bf16[400,128]{1,0:T(8,128)(2,1)S(1)}, bf16[400,128]{1,0:T(8,128)(2,1)S(1)}, u32[]{:S(2)}, u32[]{:S(2)}) collective-permute-start(bf16[400,128]{1,0:T(8,128)(2,1)S(1)} %get-tuple-element.144.refs_2_.refs_0_), channel_id=1, source_target_pairs={{0,8},{1,9},{2,10},{3,11},{4,12},{5,13},{6,14},{7,15},{8,0},{9,1},... | collective-permute-start | bytes 307208 | tf_op jit(solution)/shard_map/ppermute | solution.py:508
  58.7 1.1 %collective-permute-done.26.refs_1_ = bf16[1024,128]{1,0:T(8,128)(2,1)S(1)} collective-permute-done((bf16[1024,128]{1,0:T(8,128)(2,1)S(1)}, bf16[1024,128]{1,0:T(8,128)(2,1)S(1)}, u32[]{:S(2)}, u32[]{:S(2)}) %collective-permute-start.26) | collective-permute-done | bytes 262176 | tf_op jit(solution)/shard_map/ppermute | solution.py:508
  59.8 0.1 shard_map.341.token_in.refs_0_
  59.9 0.8 %collective-permute-start.31 = (bf16[2048,128]{1,0:T(8,128)(2,1)S(1)}, bf16[2048,128]{1,0:T(8,128)(2,1)S(1)}, u32[]{:S(2)}, u32[]{:S(2)}) collective-permute-start(bf16[2048,128]{1,0:T(8,128)(2,1)S(1)} %shard_map.341.token_in.refs_0_), channel_id=1, source_target_pairs={{0,2},{1,5},{2,0},{3,7},{4,6},{5,1},{6,4},{7,3},{8,10},{9,13},{10,... | collective-permute-start | bytes 1572872 | tf_op jit(solution)/shard_map/ppermute | solution.py:508
  60.7 2.8 %shard_map.342 = (f32[1000,512]{1,0:T(8,128)}, f32[512,256]{1,0:T(8,128)}, f32[1,256]{1,0:T(1,128)}, f32[1,256]{1,0:T(1,128)}, f32[1,256]{1,0:T(1,128)}, /*index...) custom-call(bf16[48,128]{1,0:T(8,128)(2,1)S(1)} %get-tuple-element.1, ...), custom_call_target="tpu_custom_call" | custom-call | flops 1 | bytes 1 | tf_op jit(solution)/shard_map/pallas_call | solution.py:656
  63.5 1.9 %collective-permute-done.28.refs_2_ = bf16[400,128]{1,0:T(8,128)(2,1)S(1)} collective-permute-done((bf16[400,128]{1,0:T(8,128)(2,1)S(1)}, bf16[400,128]{1,0:T(8,128)(2,1)S(1)}, u32[]{:S(2)}, u32[]{:S(2)}) %collective-permute-start.28) | collective-permute-done | bytes 102432 | tf_op jit(solution)/shard_map/ppermute | solution.py:508
  65.5 0.1 collective-permute-start.30
  65.6 1.7 %collective-permute-done.30.got_ref = bf16[1600,128]{1,0:T(8,128)(2,1)S(1)} collective-permute-done((bf16[1600,128]{1,0:T(8,128)(2,1)S(1)}, bf16[1600,128]{1,0:T(8,128)(2,1)S(1)}, u32[]{:S(2)}, u32[]{:S(2)}) %collective-permute-start.30) | collective-permute-done | bytes 409632 | tf_op jit(solution)/shard_map/ppermute | solution.py:508
  67.3 1.8 %shard_map.344 = (f32[2304,256]{1,0:T(8,128)}, f32[1,256]{1,0:T(1,128)}, f32[1,256]{1,0:T(1,128)}, f32[8,128]{1,0:T(8,128)S(1)}) custom-call(bf16[1600,128]{1,0:T(8,128)(2,1)S(1)} %shard_map.343.mine_ref.token_ref, bf16[1600,128]{1,0:T(8,128)(2,1)S(1)} %collective-permute-done.30.got_ref, bf16[1600,128]{1,0:T(8,128)(2,1)S(1)} %shard_map.343.mine_ref.token_ref), custom_call_target="tpu_custom_call" | custom-call | flops 1 | bytes 1 | tf_op jit(solution)/shard_map/pallas_call | solution.py:667
  69.1 0.0 collective-permute-done.31.refs_1_
  69.1 0.1 shard_map.345.late_ref
  69.2 0.2 collective-permute-start.32
  69.4 1.4 %shard_map.346 = (f32[2304,256]{1,0:T(8,128)}, f32[2304,256]{1,0:T(8,128)}, f32[256,768]{1,0:T(8,128)}, f32[256,256]{1,0:T(8,128)}) custom-call(bf16[4096,128]{1,0:T(8,128)(2,1)S(1)} %shard_map.345.late_ref, f32[2304,256]{1,0:T(8,128)} %get-tuple-element.150.conv2_in), custom_call_target="tpu_custom_call", output_to_operand_aliasing={{1}: (1, {})} | custom-call | flops 1 | bytes 1 | tf_op jit(solution)/shard_map/pallas_call | solution.py:678
  70.9 1.1 %collective-permute-done.32.late_ref = bf16[4096,128]{1,0:T(8,128)(2,1)S(1)} collective-permute-done((bf16[4096,128]{1,0:T(8,128)(2,1)S(1)}, bf16[4096,128]{1,0:T(8,128)(2,1)S(1)}, u32[]{:S(2)}, u32[]{:S(2)}) %collective-permute-start.32) | collective-permute-done | bytes 1048608 | tf_op jit(solution)/shard_map/ppermute | solution.py:508
  71.9 1.4 %shard_map.347 = (f32[2304,256]{1,0:T(8,128)}, f32[2304,256]{1,0:T(8,128)}, f32[256,768]{1,0:T(8,128)}, f32[256,256]{1,0:T(8,128)}) custom-call(bf16[4096,128]{1,0:T(8,128)(2,1)S(1)} %collective-permute-done.32.late_ref, f32[2304,256]{1,0:T(8,128)} %get-tuple-element.151.conv1_in, ...), custom_call_target="tpu_custom_call", output_to_operand_aliasing={{0}: (1, {}), {1}: (2, {}), {2}: (3, {}), {3}: (4, {})} | custom-call | flops 1 | bytes 1 | tf_op jit(solution)/shard_map/pallas_call | solution.py:681
  (66 shorter events, 0.3 us)
Async XLA Ops:
  0.7 7.2 %copy-start = (bf16[3,3,256,256]{3,2,1,0:T(8,128)(2,1)S(1)}, bf16[3,3,256,256]{3,2,1,0:T(8,128)(2,1)}, u32[]{:S(2)}) copy-start(bf16[3,3,256,256]{3,2,1,0:T(8,128)(2,1)} %param.24) | copy-start | bytes 3538948
  0.7 7.2 %copy-start.1 = (bf16[3,3,256,256]{3,2,1,0:T(8,128)(2,1)S(1)}, bf16[3,3,256,256]{3,2,1,0:T(8,128)(2,1)}, u32[]{:S(2)}) copy-start(bf16[3,3,256,256]{3,2,1,0:T(8,128)(2,1)} %param.29) | copy-start | bytes 3538948
  0.7 7.2 %copy-start.3 = (bf16[1000,512]{1,0:T(8,128)(2,1)S(1)}, bf16[1000,512]{1,0:T(8,128)(2,1)}, u32[]{:S(2)}) copy-start(bf16[1000,512]{1,0:T(8,128)(2,1)} %table_ref.3) | copy-start | bytes 3072004
  0.7 7.2 %copy-start.5 = (bf16[512,256]{1,0:T(8,128)(2,1)S(1)}, bf16[512,256]{1,0:T(8,128)(2,1)}, u32[]{:S(2)}) copy-start(bf16[512,256]{1,0:T(8,128)(2,1)} %embed_ref.3) | copy-start | bytes 786436
  0.7 7.2 %copy-start.8 = (s32[4]{0:T(128)S(1)}, s32[4]{0:T(128)}, u32[]{:S(2)}) copy-start(s32[4]{0:T(128)} %steps_ref.3) | copy-start | bytes 52
  0.7 7.2 %copy-start.9 = (f32[256]{0:T(256)S(1)}, f32[256]{0:T(256)}, u32[]{:S(2)}) copy-start(f32[256]{0:T(256)} %param.22) | copy-start | bytes 3076
  0.7 7.2 %copy-start.10 = (f32[256]{0:T(256)S(1)}, f32[256]{0:T(256)}, u32[]{:S(2)}) copy-start(f32[256]{0:T(256)} %param.23) | copy-start | bytes 3076
  0.7 7.2 %copy-start.11 = (f32[256]{0:T(256)S(1)}, f32[256]{0:T(256)}, u32[]{:S(2)}) copy-start(f32[256]{0:T(256)} %param.27) | copy-start | bytes 3076
  0.7 7.2 %copy-start.12 = (f32[256]{0:T(256)S(1)}, f32[256]{0:T(256)}, u32[]{:S(2)}) copy-start(f32[256]{0:T(256)} %param.28) | copy-start | bytes 3076
  0.8 7.2 %copy-start.13 = (f32[256]{0:T(256)S(1)}, f32[256]{0:T(256)}, u32[]{:S(2)}) copy-start(f32[256]{0:T(256)} %param.30) | copy-start | bytes 3076
  0.8 7.2 %copy-start.14 = (f32[256]{0:T(256)S(1)}, f32[256]{0:T(256)}, u32[]{:S(2)}) copy-start(f32[256]{0:T(256)} %param.31) | copy-start | bytes 3076
  0.8 7.2 %copy-start.15 = (f32[256]{0:T(256)S(1)}, f32[256]{0:T(256)}, u32[]{:S(2)}) copy-start(f32[256]{0:T(256)} %param.32) | copy-start | bytes 3076
  0.8 7.2 %copy-start.16 = (f32[256]{0:T(256)S(1)}, f32[256]{0:T(256)}, u32[]{:S(2)}) copy-start(f32[256]{0:T(256)} %param.34) | copy-start | bytes 3076
  0.8 7.2 %copy-start.17 = (f32[256]{0:T(256)S(1)}, f32[256]{0:T(256)}, u32[]{:S(2)}) copy-start(f32[256]{0:T(256)} %param.36) | copy-start | bytes 3076
  0.8 7.2 %copy-start.18 = (f32[256]{0:T(256)S(1)}, f32[256]{0:T(256)}, u32[]{:S(2)}) copy-start(f32[256]{0:T(256)} %param.26) | copy-start | bytes 3076
  2.6 5.3 %collective-permute-start = (bf16[64,256]{1,0:T(8,128)(2,1)}, bf16[64,256]{1,0:T(8,128)(2,1)S(1)}, u32[]{:S(2)}, u32[]{:S(2)}) collective-permute-start(bf16[64,256]{1,0:T(8,128)(2,1)} %get-tuple-element.96), channel_id=1, source_target_pairs={{0,1},{1,0},{2,3},{3,2},{4,5},{5,4},{6,7},{7,6},{8,9},{9,8},{10,11... | collective-permute-start | bytes 98312 | tf_op jit(solution)/shard_map/ppermute | solution.py:508
  3.1 5.9 %collective-permute-start.1 = (bf16[64,256]{1,0:T(8,128)(2,1)}, bf16[64,256]{1,0:T(8,128)(2,1)S(1)}, u32[]{:S(2)}, u32[]{:S(2)}) collective-permute-start(bf16[64,256]{1,0:T(8,128)(2,1)} %get-tuple-element.97), channel_id=1, source_target_pairs={{0,2},{1,3},{2,0},{3,1},{4,6},{5,7},{6,4},{7,5},{8,10},{9,11},{10,... | collective-permute-start | bytes 98312 | tf_op jit(solution)/shard_map/ppermute | solution.py:508
  5.7 3.6 %collective-permute-start.2 = (bf16[64,256]{1,0:T(8,128)(2,1)}, bf16[64,256]{1,0:T(8,128)(2,1)S(1)}, u32[]{:S(2)}, u32[]{:S(2)}) collective-permute-start(bf16[64,256]{1,0:T(8,128)(2,1)} %get-tuple-element.98), channel_id=1, source_target_pairs={{0,3},{1,2},{2,1},{3,0},{4,7},{5,6},{6,5},{7,4},{8,11},{9,10},{10,... | collective-permute-start | bytes 98312 | tf_op jit(solution)/shard_map/ppermute | solution.py:508
  5.8 6.5 %collective-permute-start.3 = (bf16[64,256]{1,0:T(8,128)(2,1)}, bf16[64,256]{1,0:T(8,128)(2,1)S(1)}, u32[]{:S(2)}, u32[]{:S(2)}) collective-permute-start(bf16[64,256]{1,0:T(8,128)(2,1)} %get-tuple-element.107), channel_id=1, source_target_pairs={{0,1},{1,0},{2,3},{3,2},{4,5},{5,4},{6,7},{7,6},{8,9},{9,8},{10,11... | collective-permute-start | bytes 98312 | tf_op jit(solution)/shard_map/ppermute | solution.py:508
  5.9 6.3 %collective-permute-start.4 = (bf16[64,256]{1,0:T(8,128)(2,1)}, bf16[64,256]{1,0:T(8,128)(2,1)S(1)}, u32[]{:S(2)}, u32[]{:S(2)}) collective-permute-start(bf16[64,256]{1,0:T(8,128)(2,1)} %get-tuple-element.108), channel_id=1, source_target_pairs={{0,2},{1,3},{2,0},{3,1},{4,6},{5,7},{6,4},{7,5},{8,10},{9,11},{10,... | collective-permute-start | bytes 98312 | tf_op jit(solution)/shard_map/ppermute | solution.py:508
  7.9 4.4 %collective-permute-start.5 = (bf16[64,256]{1,0:T(8,128)(2,1)}, bf16[64,256]{1,0:T(8,128)(2,1)S(1)}, u32[]{:S(2)}, u32[]{:S(2)}) collective-permute-start(bf16[64,256]{1,0:T(8,128)(2,1)} %get-tuple-element.109), channel_id=1, source_target_pairs={{0,3},{1,2},{2,1},{3,0},{4,7},{5,6},{6,5},{7,4},{8,11},{9,10},{10,... | collective-permute-start | bytes 98312 | tf_op jit(solution)/shard_map/ppermute | solution.py:508
  8.0 1.3 %copy-start.2 = (bf16[256,768]{1,0:T(8,128)(2,1)S(1)}, bf16[256,768]{1,0:T(8,128)(2,1)}, u32[]{:S(2)}) copy-start(bf16[256,768]{1,0:T(8,128)(2,1)} %qkv_weight_ref.3) | copy-start | bytes 1179652
  8.0 1.2 %copy-start.4 = (bf16[256,256]{1,0:T(8,128)(2,1)S(1)}, bf16[256,256]{1,0:T(8,128)(2,1)}, u32[]{:S(2)}) copy-start(bf16[256,256]{1,0:T(8,128)(2,1)} %out_weight_ref.3) | copy-start | bytes 393220
  8.0 1.2 %copy-start.7 = (bf16[64,256]{1,0:T(8,128)(2,1)S(1)}, bf16[64,256]{1,0:T(8,128)(2,1)}, u32[]{:S(2)}) copy-start(bf16[64,256]{1,0:T(8,128)(2,1)} %get-tuple-element.95.refs_0_) | copy-start | bytes 98308
  9.0 3.3 %copy-start.6 = (bf16[64,256]{1,0:T(8,128)(2,1)S(1)}, bf16[64,256]{1,0:T(8,128)(2,1)}, u32[]{:S(2)}) copy-start(bf16[64,256]{1,0:T(8,128)(2,1)} %get-tuple-element.106.refs_0_) | copy-start | bytes 98308
  14.1 3.0 %collective-permute-start.6 = (bf16[3328,128]{1,0:T(8,128)(2,1)S(1)}, bf16[3328,128]{1,0:T(8,128)(2,1)S(1)}, u32[]{:S(2)}, u32[]{:S(2)}) collective-permute-start(bf16[3328,128]{1,0:T(8,128)(2,1)S(1)} %get-tuple-element.118), channel_id=1, source_target_pairs={{0,1},{1,0},{2,3},{3,2},{4,5},{5,4},{6,7},{7,6},{8,9},{9,8},{10,11... | collective-permute-start | bytes 2555912 | tf_op jit(solution)/shard_map/ppermute | solution.py:508
  17.0 2.6 %collective-permute-start.10 = (bf16[2352,128]{1,0:T(8,128)(2,1)S(1)}, bf16[2352,128]{1,0:T(8,128)(2,1)S(1)}, u32[]{:S(2)}, u32[]{:S(2)}) collective-permute-start(bf16[2352,128]{1,0:T(8,128)(2,1)S(1)} %get-tuple-element.126), channel_id=1, source_target_pairs={{0,1},{1,0},{2,3},{3,2},{4,5},{5,4},{6,7},{7,6},{8,9},{9,8},{10,11... | collective-permute-start | bytes 1806344 | tf_op jit(solution)/shard_map/ppermute | solution.py:508
  17.3 8.1 %collective-permute-start.14 = (bf16[896,128]{1,0:T(8,128)(2,1)S(1)}, bf16[896,128]{1,0:T(8,128)(2,1)S(1)}, u32[]{:S(2)}, u32[]{:S(2)}) collective-permute-start(bf16[896,128]{1,0:T(8,128)(2,1)S(1)} %get-tuple-element.132), channel_id=1, source_target_pairs={{0,2},{1,5},{2,0},{3,7},{4,6},{5,1},{6,4},{7,3},{8,10},{9,13},{10,... | collective-permute-start | bytes 688136 | tf_op jit(solution)/shard_map/ppermute | solution.py:508
  19.7 6.8 %collective-permute-start.15 = (bf16[1152,128]{1,0:T(8,128)(2,1)S(1)}, bf16[1152,128]{1,0:T(8,128)(2,1)S(1)}, u32[]{:S(2)}, u32[]{:S(2)}) collective-permute-start(bf16[1152,128]{1,0:T(8,128)(2,1)S(1)} %get-tuple-element.133), channel_id=1, source_target_pairs={{0,2},{1,5},{2,0},{3,7},{4,6},{5,1},{6,4},{7,3},{8,10},{9,13},{10,... | collective-permute-start | bytes 884744 | tf_op jit(solution)/shard_map/ppermute | solution.py:508
  20.9 7.3 %collective-permute-start.11 = (bf16[448,128]{1,0:T(8,128)(2,1)S(1)}, bf16[448,128]{1,0:T(8,128)(2,1)S(1)}, u32[]{:S(2)}, u32[]{:S(2)}) collective-permute-start(bf16[448,128]{1,0:T(8,128)(2,1)S(1)} %get-tuple-element.129), channel_id=1, source_target_pairs={{0,8},{1,9},{2,10},{3,11},{4,12},{5,13},{6,14},{7,15},{8,0},{9,1},... | collective-permute-start | bytes 344072 | tf_op jit(solution)/shard_map/ppermute | solution.py:508
  22.5 11.8 %collective-permute-start.12 = (bf16[448,128]{1,0:T(8,128)(2,1)S(1)}, bf16[448,128]{1,0:T(8,128)(2,1)S(1)}, u32[]{:S(2)}, u32[]{:S(2)}) collective-permute-start(bf16[448,128]{1,0:T(8,128)(2,1)S(1)} %get-tuple-element.130), channel_id=1, source_target_pairs={{0,16},{1,17},{2,18},{3,19},{4,20},{5,21},{6,22},{7,23},{8,24},{9,... | collective-permute-start | bytes 344072 | tf_op jit(solution)/shard_map/ppermute | solution.py:508
  25.1 9.2 %collective-permute-start.13 = (bf16[448,128]{1,0:T(8,128)(2,1)S(1)}, bf16[448,128]{1,0:T(8,128)(2,1)S(1)}, u32[]{:S(2)}, u32[]{:S(2)}) collective-permute-start(bf16[448,128]{1,0:T(8,128)(2,1)S(1)} %get-tuple-element.131), channel_id=1, source_target_pairs={{0,24},{1,25},{2,26},{3,27},{4,28},{5,29},{6,30},{7,31},{8,16},{9,... | collective-permute-start | bytes 344072 | tf_op jit(solution)/shard_map/ppermute | solution.py:508
  26.6 7.7 %collective-permute-start.16 = (bf16[1024,128]{1,0:T(8,128)(2,1)S(1)}, bf16[1024,128]{1,0:T(8,128)(2,1)S(1)}, u32[]{:S(2)}, u32[]{:S(2)}) collective-permute-start(bf16[1024,128]{1,0:T(8,128)(2,1)S(1)} %get-tuple-element.135), channel_id=1, source_target_pairs={{0,4},{1,3},{2,6},{3,1},{4,0},{5,7},{6,2},{7,5},{8,12},{9,11},{10,... | collective-permute-start | bytes 786440 | tf_op jit(solution)/shard_map/ppermute | solution.py:508
  34.5 5.9 %collective-permute-start.18 = (bf16[256,128]{1,0:T(8,128)(2,1)S(1)}, bf16[256,128]{1,0:T(8,128)(2,1)S(1)}, u32[]{:S(2)}, u32[]{:S(2)}) collective-permute-start(bf16[256,128]{1,0:T(8,128)(2,1)S(1)} %get-tuple-element.137), channel_id=1, source_target_pairs={{0,8},{1,9},{2,10},{3,11},{4,12},{5,13},{6,14},{7,15},{8,0},{9,1},... | collective-permute-start | bytes 196616 | tf_op jit(solution)/shard_map/ppermute | solution.py:508
  36.3 6.2 %collective-permute-start.19 = (bf16[256,128]{1,0:T(8,128)(2,1)S(1)}, bf16[256,128]{1,0:T(8,128)(2,1)S(1)}, u32[]{:S(2)}, u32[]{:S(2)}) collective-permute-start(bf16[256,128]{1,0:T(8,128)(2,1)S(1)} %get-tuple-element.138), channel_id=1, source_target_pairs={{0,16},{1,17},{2,18},{3,19},{4,20},{5,21},{6,22},{7,23},{8,24},{9,... | collective-permute-start | bytes 196616 | tf_op jit(solution)/shard_map/ppermute | solution.py:508
  37.6 6.2 %collective-permute-start.20 = (bf16[256,128]{1,0:T(8,128)(2,1)S(1)}, bf16[256,128]{1,0:T(8,128)(2,1)S(1)}, u32[]{:S(2)}, u32[]{:S(2)}) collective-permute-start(bf16[256,128]{1,0:T(8,128)(2,1)S(1)} %get-tuple-element.139), channel_id=1, source_target_pairs={{0,24},{1,25},{2,26},{3,27},{4,28},{5,29},{6,30},{7,31},{8,16},{9,... | collective-permute-start | bytes 196616 | tf_op jit(solution)/shard_map/ppermute | solution.py:508
  38.9 7.1 %collective-permute-start.17 = (bf16[448,128]{1,0:T(8,128)(2,1)S(1)}, bf16[448,128]{1,0:T(8,128)(2,1)S(1)}, u32[]{:S(2)}, u32[]{:S(2)}) collective-permute-start(bf16[448,128]{1,0:T(8,128)(2,1)S(1)} %shard_map.335.refs_8_.refs_0_.refs_2_.refs_4_), channel_id=1, source_target_pairs={{0,2},{1,5},{2,0},{3,7},{4,6},{5,1},{6,4},{7,3},{8,10},{9,13},{10,... | collective-permute-start | bytes 344072 | tf_op jit(solution)/shard_map/ppermute | solution.py:508
  40.3 5.2 %collective-permute-start.7 = (bf16[2,64,256]{2,1,0:T(8,128)(2,1)S(1)}, bf16[2,64,256]{2,1,0:T(8,128)(2,1)S(1)}, u32[]{:S(2)}, u32[]{:S(2)}) collective-permute-start(bf16[2,64,256]{2,1,0:T(8,128)(2,1)S(1)} %get-tuple-element.121), channel_id=1, source_target_pairs={{0,1},{1,0},{2,3},{3,2},{4,5},{5,4},{6,7},{7,6},{8,9},{9,8},{10,11... | collective-permute-start | bytes 196616 | tf_op jit(solution)/shard_map/ppermute | solution.py:508
  40.3 7.9 %collective-permute-start.8 = (bf16[2,64,256]{2,1,0:T(8,128)(2,1)S(1)}, bf16[2,64,256]{2,1,0:T(8,128)(2,1)S(1)}, u32[]{:S(2)}, u32[]{:S(2)}) collective-permute-start(bf16[2,64,256]{2,1,0:T(8,128)(2,1)S(1)} %get-tuple-element.122), channel_id=1, source_target_pairs={{0,2},{1,3},{2,0},{3,1},{4,6},{5,7},{6,4},{7,5},{8,10},{9,11},{10,... | collective-permute-start | bytes 196616 | tf_op jit(solution)/shard_map/ppermute | solution.py:508
  42.5 7.1 %collective-permute-start.9 = (bf16[2,64,256]{2,1,0:T(8,128)(2,1)S(1)}, bf16[2,64,256]{2,1,0:T(8,128)(2,1)S(1)}, u32[]{:S(2)}, u32[]{:S(2)}) collective-permute-start(bf16[2,64,256]{2,1,0:T(8,128)(2,1)S(1)} %get-tuple-element.123), channel_id=1, source_target_pairs={{0,3},{1,2},{2,1},{3,0},{4,7},{5,6},{6,5},{7,4},{8,11},{9,10},{10,... | collective-permute-start | bytes 196616 | tf_op jit(solution)/shard_map/ppermute | solution.py:508
  43.8 6.6 %collective-permute-start.24 = (bf16[256,128]{1,0:T(8,128)(2,1)S(1)}, bf16[256,128]{1,0:T(8,128)(2,1)S(1)}, u32[]{:S(2)}, u32[]{:S(2)}) collective-permute-start(bf16[256,128]{1,0:T(8,128)(2,1)S(1)} %shard_map.336.refs_6_.refs_0_), channel_id=1, source_target_pairs={{0,24},{1,25},{2,26},{3,27},{4,28},{5,29},{6,30},{7,31},{8,16},{9,... | collective-permute-start | bytes 196616 | tf_op jit(solution)/shard_map/ppermute | solution.py:508
  45.5 7.8 %collective-permute-start.23 = (bf16[256,128]{1,0:T(8,128)(2,1)S(1)}, bf16[256,128]{1,0:T(8,128)(2,1)S(1)}, u32[]{:S(2)}, u32[]{:S(2)}) collective-permute-start(bf16[256,128]{1,0:T(8,128)(2,1)S(1)} %shard_map.336.refs_6_.refs_0_), channel_id=1, source_target_pairs={{0,16},{1,17},{2,18},{3,19},{4,20},{5,21},{6,22},{7,23},{8,24},{9,... | collective-permute-start | bytes 196616 | tf_op jit(solution)/shard_map/ppermute | solution.py:508
  46.1 7.3 %collective-permute-start.22 = (bf16[256,128]{1,0:T(8,128)(2,1)S(1)}, bf16[256,128]{1,0:T(8,128)(2,1)S(1)}, u32[]{:S(2)}, u32[]{:S(2)}) collective-permute-start(bf16[256,128]{1,0:T(8,128)(2,1)S(1)} %shard_map.336.refs_6_.refs_0_), channel_id=1, source_target_pairs={{0,8},{1,9},{2,10},{3,11},{4,12},{5,13},{6,14},{7,15},{8,0},{9,1},... | collective-permute-start | bytes 196616 | tf_op jit(solution)/shard_map/ppermute | solution.py:508
  48.3 5.9 %collective-permute-start.21 = (bf16[448,128]{1,0:T(8,128)(2,1)S(1)}, bf16[448,128]{1,0:T(8,128)(2,1)S(1)}, u32[]{:S(2)}, u32[]{:S(2)}) collective-permute-start(bf16[448,128]{1,0:T(8,128)(2,1)S(1)} %shard_map.337.refs_4_.refs_0_.refs_2_), channel_id=1, source_target_pairs={{0,4},{1,3},{2,6},{3,1},{4,0},{5,7},{6,2},{7,5},{8,12},{9,11},{10,... | collective-permute-start | bytes 344072 | tf_op jit(solution)/shard_map/ppermute | solution.py:508
  53.4 6.4 %collective-permute-start.26 = (bf16[1024,128]{1,0:T(8,128)(2,1)S(1)}, bf16[1024,128]{1,0:T(8,128)(2,1)S(1)}, u32[]{:S(2)}, u32[]{:S(2)}) collective-permute-start(bf16[1024,128]{1,0:T(8,128)(2,1)S(1)} %shard_map.339.refs_6_.refs_0_), channel_id=1, source_target_pairs={{0,4},{1,3},{2,6},{3,1},{4,0},{5,7},{6,2},{7,5},{8,12},{9,11},{10,... | collective-permute-start | bytes 786440 | tf_op jit(solution)/shard_map/ppermute | solution.py:508
  54.2 9.3 %collective-permute-start.29 = (bf16[400,128]{1,0:T(8,128)(2,1)S(1)}, bf16[400,128]{1,0:T(8,128)(2,1)S(1)}, u32[]{:S(2)}, u32[]{:S(2)}) collective-permute-start(bf16[400,128]{1,0:T(8,128)(2,1)S(1)} %get-tuple-element.144.refs_2_.refs_0_), channel_id=1, source_target_pairs={{0,24},{1,25},{2,26},{3,27},{4,28},{5,29},{6,30},{7,31},{8,16},{9,... | collective-permute-start | bytes 307208 | tf_op jit(solution)/shard_map/ppermute | solution.py:508
  56.6 8.9 %collective-permute-start.28 = (bf16[400,128]{1,0:T(8,128)(2,1)S(1)}, bf16[400,128]{1,0:T(8,128)(2,1)S(1)}, u32[]{:S(2)}, u32[]{:S(2)}) collective-permute-start(bf16[400,128]{1,0:T(8,128)(2,1)S(1)} %get-tuple-element.144.refs_2_.refs_0_), channel_id=1, source_target_pairs={{0,16},{1,17},{2,18},{3,19},{4,20},{5,21},{6,22},{7,23},{8,24},{9,... | collective-permute-start | bytes 307208 | tf_op jit(solution)/shard_map/ppermute | solution.py:508
  56.6 8.9 %collective-permute-start.27 = (bf16[400,128]{1,0:T(8,128)(2,1)S(1)}, bf16[400,128]{1,0:T(8,128)(2,1)S(1)}, u32[]{:S(2)}, u32[]{:S(2)}) collective-permute-start(bf16[400,128]{1,0:T(8,128)(2,1)S(1)} %get-tuple-element.144.refs_2_.refs_0_), channel_id=1, source_target_pairs={{0,8},{1,9},{2,10},{3,11},{4,12},{5,13},{6,14},{7,15},{8,0},{9,1},... | collective-permute-start | bytes 307208 | tf_op jit(solution)/shard_map/ppermute | solution.py:508
  58.7 2.0 %collective-permute-start.25 = (bf16[48,128]{1,0:T(8,128)(2,1)S(1)}, bf16[48,128]{1,0:T(8,128)(2,1)S(1)}, u32[]{:S(2)}, u32[]{:S(2)}) collective-permute-start(bf16[48,128]{1,0:T(8,128)(2,1)S(1)} %get-tuple-element.143.sums_ref), channel_id=1, source_target_pairs={{0,1},{1,0},{2,3},{3,2},{4,5},{5,4},{6,7},{7,6},{8,9},{9,8},{10,11... | collective-permute-start | bytes 36872 | tf_op jit(solution)/shard_map/ppermute | solution.py:508
  59.9 9.2 %collective-permute-start.31 = (bf16[2048,128]{1,0:T(8,128)(2,1)S(1)}, bf16[2048,128]{1,0:T(8,128)(2,1)S(1)}, u32[]{:S(2)}, u32[]{:S(2)}) collective-permute-start(bf16[2048,128]{1,0:T(8,128)(2,1)S(1)} %shard_map.341.token_in.refs_0_), channel_id=1, source_target_pairs={{0,2},{1,5},{2,0},{3,7},{4,6},{5,1},{6,4},{7,3},{8,10},{9,13},{10,... | collective-permute-start | bytes 1572872 | tf_op jit(solution)/shard_map/ppermute | solution.py:508
  65.5 1.8 %collective-permute-start.30 = (bf16[1600,128]{1,0:T(8,128)(2,1)S(1)}, bf16[1600,128]{1,0:T(8,128)(2,1)S(1)}, u32[]{:S(2)}, u32[]{:S(2)}) collective-permute-start(bf16[1600,128]{1,0:T(8,128)(2,1)S(1)} %shard_map.343.mine_ref.token_ref), channel_id=1, source_target_pairs={{0,1},{1,0},{2,3},{3,2},{4,5},{5,4},{6,7},{7,6},{8,9},{9,8},{10,11... | collective-permute-start | bytes 1228808 | tf_op jit(solution)/shard_map/ppermute | solution.py:508
  69.2 2.7 %collective-permute-start.32 = (bf16[4096,128]{1,0:T(8,128)(2,1)S(1)}, bf16[4096,128]{1,0:T(8,128)(2,1)S(1)}, u32[]{:S(2)}, u32[]{:S(2)}) collective-permute-start(bf16[4096,128]{1,0:T(8,128)(2,1)S(1)} %shard_map.345.late_ref), channel_id=1, source_target_pairs={{0,1},{1,0},{2,3},{3,2},{4,5},{5,4},{6,7},{7,6},{8,9},{9,8},{10,11... | collective-permute-start | bytes 3145736 | tf_op jit(solution)/shard_map/ppermute | solution.py:508
